TPU v7x, 128 devices: a whole 4x4x4 slice. The times are simulated.
128 devices in a mesh: gx: 16 (over x, z), gy: 8 (over y, core).
Axes of the slice: x: 4, y: 4, z: 4, core: 2. Of those that a mesh axis runs over, the one named last changes fastest.
Arguments:
- values: float32 [16, 524288], P(None, ('gx', 'gy')), may hold values from -6 to 6
- coords: float32 [3, 524288], P(None, ('gx', 'gy')), may hold values from 0 to 1
- order: int32 [524288], P(('gx', 'gy')), may hold values from 0 to 4095, as said below
- leaf_basis: float32 [8192, 4096], P(('gx', 'gy')), may hold values from -0.75 to 0.75
- leaf_transfer: float32 [8192, 4096], P(('gx', 'gy')), may hold values from -0.5 to 0.5
- middle_transfer: float32 [1024, 4096], P(('gx', 'gy')), may hold values from -0.5 to 0.5
- root_transfer: float32 [128, 4096], P(('gx', 'gy')), may hold values from -0.5 to 0.5
- leaf_skeleton: float32 [8192, 192], P(('gx', 'gy')), may hold values from 0 to 1
- middle_skeleton: float32 [1024, 192], P(('gx', 'gy')), may hold values from 0 to 1
- root_skeleton: float32 [128, 192], P(('gx', 'gy')), may hold values from 0 to 1
- top_skeleton: float32 [16, 192], replicated, may hold values from 0 to 1
- leaf_far: int32 [8192, 64], P(('gx', 'gy')), may hold values from 0 to 1023
- middle_far: int32 [1024, 64], P(('gx', 'gy')), may hold values from 0 to 255
- root_far: int32 [128, 64], P(('gx', 'gy')), may hold values from 0 to 127
- leaf_near: int32 [8192, 26], P(('gx', 'gy')), may hold values from 0 to 79
- leaf_sends: int32 [131072], P(('gx', 'gy')), may hold values from 0 to 63
- middle_sends: int32 [32768], P(('gx', 'gy')), may hold values from 0 to 7
Outputs:
- product: float32 [16, 524288], P(None, ('gx', 'gy'))
Inputs may be any that keep to these rules, and one draw needn't show every extreme that they name: `order`: each consecutive block of 4096 entries is a permutation of 0 to 4095.
All inputs are finite; a program needn't handle non-finite values.
Results may differ from a plain program's by a relative error of at most 0.00012.
Values sent between devices are 32-bit elements; how exact they have to be, the bound alone decides.
No kernel may reach another device: no remote copies, remote signals or barrier semaphores. Data moves between devices by JAX's collectives and lax.ppermute only.
A program may use at most 192 MiB of HBM per device.

v0:
```python
import math

import jax
import jax.numpy as jnp
from jax import lax
from jax.sharding import PartitionSpec as P

LEAF = 64
RANK = 64
RHS = 16


decay_rate = math.sqrt(3.0) / 0.3
highest = lax.Precision.HIGHEST


def from_behind(block, axis, distance):
    devices = range(lax.axis_size(axis))
    route = [(i - distance, i) for i in devices if i - distance in devices]
    return lax.ppermute(block, axis, route)


def matern(left, right):
    delta = left[..., :, :, None] - right[..., :, None, :]
    distance = jnp.sqrt(jnp.sum(delta * delta, axis=-3))
    scaled = decay_rate * distance
    return (1.0 + scaled) * jnp.exp(-scaled)


def interact(target_points, table_points, table_values, index):
    count = index.shape[0]
    listed = index.shape[1]
    block = math.gcd(count, 16)
    inner = target_points.shape[-1]

    def block_product(inputs):
        targets, chosen = inputs
        kernel = matern(targets[:, None], table_points[chosen])
        return jnp.einsum("nfks,nfsr->nkr", kernel, table_values[chosen], precision=highest)

    result = lax.map(
        block_product,
        (
            target_points.reshape(count // block, block, 3, inner),
            index.reshape(count // block, block, listed),
        ),
    )
    return result.reshape(count, inner, table_values.shape[-1])


def shards(
    values,
    coords,
    order,
    leaf_basis,
    leaf_transfer,
    middle_transfer,
    root_transfer,
    leaf_skeleton,
    middle_skeleton,
    root_skeleton,
    top_skeleton,
    leaf_far,
    middle_far,
    root_far,
    leaf_near,
    leaf_sends,
    middle_sends,
):
    leaves = leaf_basis.shape[0]
    middles = middle_transfer.shape[0]
    roots = root_transfer.shape[0]
    width = values.shape[1]
    x_tree = jnp.take(values, order, axis=1)
    points_tree = jnp.take(coords, order, axis=1)
    leaf_values = x_tree.reshape(RHS, leaves, LEAF).transpose(1, 2, 0)
    leaf_points = points_tree.reshape(3, leaves, LEAF).transpose(1, 0, 2)
    basis = leaf_basis.reshape(leaves, LEAF, RANK)
    leaf_maps = leaf_transfer.reshape(leaves, RANK, RANK)
    middle_maps = middle_transfer.reshape(middles, RANK, RANK)
    root_maps = root_transfer.reshape(roots, RANK, RANK)
    up_leaf = jnp.einsum("lpr,lpk->lkr", leaf_values, basis, precision=highest)
    outgoing = up_leaf[leaf_sends].reshape(-1, RANK * RHS)
    outgoing_skeleton = leaf_skeleton[leaf_sends]
    received, received_skeleton = (
        lax.all_to_all(outgoing, ("gx", "gy"), split_axis=0, concat_axis=0, tiled=True),
        lax.all_to_all(outgoing_skeleton, ("gx", "gy"), split_axis=0, concat_axis=0, tiled=True),
    )
    up_middle = (
        jnp.einsum("nkm,nkr->nmr", leaf_maps, up_leaf, precision=highest)
        .reshape(middles, 8, RANK, RHS)
        .sum(axis=1)
    )
    middle_out = up_middle[middle_sends].reshape(-1, RANK * RHS)
    middle_out_skeleton = middle_skeleton[middle_sends]
    middle_in, middle_in_skeleton = (
        lax.all_to_all(middle_out, ("gx", "gy"), split_axis=0, concat_axis=0, tiled=True),
        lax.all_to_all(middle_out_skeleton, ("gx", "gy"), split_axis=0, concat_axis=0, tiled=True),
    )
    up_root = (
        jnp.einsum("nkm,nkr->nmr", middle_maps, up_middle, precision=highest)
        .reshape(roots, 8, RANK, RHS)
        .sum(axis=1)
    )
    top_term = jnp.einsum("nkm,nkr->mr", root_maps, up_root, precision=highest)
    top_count = top_skeleton.shape[0]
    all_roots, all_skeleton = (
        lax.all_gather(up_root.reshape(roots, RANK * RHS), ("gx", "gy"), axis=0, tiled=True),
        lax.all_gather(root_skeleton, ("gx", "gy"), axis=0, tiled=True),
    )
    parent_sum = lax.psum(top_term, "gy")
    parents = lax.all_gather(parent_sum[None], "gx", axis=0, tiled=True)
    rim_width = leaves // 8
    flat_values = leaf_values.reshape(leaves, LEAF * RHS)
    flat_points = leaf_points.reshape(leaves, 3 * LEAF)
    before_values, before_points = from_behind(
        (flat_values[leaves - rim_width :], flat_points[leaves - rim_width :]), ("gx", "gy"), 1
    )
    after_values, after_points = from_behind(
        (flat_values[:rim_width], flat_points[:rim_width]), ("gx", "gy"), -1
    )
    table_values = jnp.concatenate([before_values, flat_values, after_values], axis=0).reshape(
        leaves + 2 * rim_width, LEAF, RHS
    )
    table_points = jnp.concatenate([before_points, flat_points, after_points], axis=0).reshape(
        leaves + 2 * rim_width, 3, LEAF
    )
    own_rows = jnp.arange(leaves, dtype=jnp.int32) + rim_width
    near_index = jnp.concatenate([own_rows[:, None], leaf_near], axis=1)
    near_values = interact(leaf_points, table_points, table_values, near_index)
    far_leaf = interact(
        leaf_skeleton.reshape(leaves, 3, RANK),
        received_skeleton.reshape(-1, 3, RANK),
        received.reshape(-1, RANK, RHS),
        leaf_far,
    )
    far_middle = interact(
        middle_skeleton.reshape(middles, 3, RANK),
        middle_in_skeleton.reshape(-1, 3, RANK),
        middle_in.reshape(-1, RANK, RHS),
        middle_far,
    )
    far_root = interact(
        root_skeleton.reshape(roots, 3, RANK),
        all_skeleton.reshape(-1, 3, RANK),
        all_roots.reshape(-1, RANK, RHS),
        root_far,
    )
    group = lax.axis_index("gx")
    top_points = top_skeleton.reshape(top_count, 3, RANK)
    mine = lax.dynamic_index_in_dim(top_points, group, 0, keepdims=True)
    top_kernel = matern(mine, top_points)
    others = (jnp.arange(top_count, dtype=jnp.int32) != group)[:, None, None]
    top_kernel = jnp.where(others, top_kernel, 0.0)
    top_far = jnp.einsum("hks,hsr->kr", top_kernel, parents, precision=highest)
    down_root = far_root + jnp.einsum("nkm,mr->nkr", root_maps, top_far, precision=highest)
    down_middle = far_middle + jnp.einsum(
        "nkm,nmr->nkr", middle_maps, jnp.repeat(down_root, 8, axis=0), precision=highest
    )
    down_leaf = far_leaf + jnp.einsum(
        "nkm,nmr->nkr", leaf_maps, jnp.repeat(down_middle, 8, axis=0), precision=highest
    )
    far_values = jnp.einsum("lpk,lkr->lpr", basis, down_leaf, precision=highest)
    y_tree = (far_values + near_values).transpose(2, 0, 1).reshape(RHS, width)
    return jnp.zeros_like(values).at[:, order].set(y_tree)


def solution(mesh):
    placed = (
        P(None, ("gx", "gy")),
        P(None, ("gx", "gy")),
        P(("gx", "gy")),
        P(("gx", "gy"), None),
        P(("gx", "gy"), None),
        P(("gx", "gy"), None),
        P(("gx", "gy"), None),
        P(("gx", "gy"), None),
        P(("gx", "gy"), None),
        P(("gx", "gy"), None),
        P(),
        P(("gx", "gy"), None),
        P(("gx", "gy"), None),
        P(("gx", "gy"), None),
        P(("gx", "gy"), None),
        P(("gx", "gy")),
        P(("gx", "gy")),
    )
    return jax.shard_map(
        shards, mesh=mesh, in_specs=placed, out_specs=P(None, ("gx", "gy")), check_vma=False
    )
```

profile of v0, /device:TPU:1, one launch (start us, length us, event | category | flops | bytes accessed | tf_op | source)
XLA Modules:
  0.0 1046.6 jit_solution(9794858323939009849)
XLA Ops:
  55.9 18.7 %all-to-all-start.2 = ((f32[128,2,192]{2,1,0:T(2,128)}), f32[128,2,192]{2,1,0:T(2,128)}, u32[]{:S(2)}, u32[]{:S(2)}) async-start(f32[128,2,192]{2,1,0:T(2,128)} %all_to_all.28), calls=%async_computation.2 | async-start | bytes 524288 | tf_op jit(solution)/shard_map/all_to_all | solution.py:98
  87.0 40.8 %all-gather.1 = f32[128,1,1024]{2,1,0:T(1,128)} all-gather(f32[1,1,1024]{2,1,0:T(1,128)S(1)} %reshape.426), channel_id=1, replica_groups=mesh['gx'=16,'gy'=8] {'gx','gy'}, dimensions={0}, use_global_device_ids=true | all-gather | bytes 528384 | tf_op jit(solution)/shard_map/all_gather | solution.py:108
  141.5 42.4 %all-gather = f32[128,1,192]{2,1,0:T(1,128)S(1)} all-gather(f32[1,1,192]{2,1,0:T(1,128)S(1)} %bitcast.159), channel_id=1, replica_groups=mesh['gx'=16,'gy'=8] {'gx','gy'}, dimensions={0}, use_global_device_ids=true | all-gather | bytes 99072 | tf_op jit(solution)/shard_map/all_gather | solution.py:109
  263.8 18.6 %copy.88 = f32[1024,64,16]{2,1,0:T(8,128)} copy(f32[1024,64,16]{1,2,0:T(8,128)} %gather_fusion.6) | data formatting | bytes 8388608 | tf_op jit(solution)/shard_map/gather | solution.py:83
  282.4 28.3 %all_to_all.26 = f32[128,8,1024]{2,1,0:T(8,128)} reshape(f32[1024,64,16]{2,1,0:T(8,128)} %copy.88) | data formatting | bytes 8388608 | tf_op jit(solution)/shard_map/all_to_all | solution.py:86
  325.5 180.4 %while.5 = (s32[]{:T(128)}, f32[4,16,64,16]{2,3,1,0:T(8,128)S(1)}, f32[4,16,3,64]{3,2,1,0:T(4,128)S(1)}, s32[4,16,27]{2,1,0:T(8,128)S(1)}, f32[80,3,64]{2,1,0:T(...) while((s32[]{:T(128)}, f32[4,16,64,16]{2,3,1,0:T(8,128)S(1)}, f32[4,16,3,64]{3,2,1,0:T(4,128)S(1)}, ...), condition=%wide.region_10.11_spmd, body=%wide.region_8.10_spmd.sunk | while | flops 360974624 | bytes 20643744 | solution.py:41
  330.8 17.3 %multiply_reduce_fusion.8 = f32[16,27,64,64]{3,2,1,0:T(8,128)} fusion(f32[16,27,3,64]{3,2,1,0:T(4,128)S(1)} %bitcast.144, f32[16,3,64]{2,1,0:T(4,128)S(1)} %dynamic-slice_bitcast_fusion.6), kind=kLoop, calls=%fused_computation.32.clone.1 | loop fusion | flops 14155776 | bytes 7421952 | tf_op jit(solution)/shard_map/while/body/eval_jaxpr/reduce_sum | solution.py:25
  348.1 22.4 %fusion.122 = f32[4,16,64,16]{2,3,1,0:T(8,128)S(1)} fusion(f32[4,16,64,16]{2,3,1,0:T(8,128)S(1)} %get-tuple-element.243, s32[]{:T(128)S(6)} %copy.114, f32[16,27,64,16]{2,3,1,0:T(8,128)} %bitcast.142, f32[16,27,64,64]{3,2,1,0:T(8,128)} %multiply_reduce_fusion.8), kind=kOutput, calls=%fused_computation.43.clone.1 | convolution fusion | flops 346816512 | bytes 8978436 | tf_op jit(solution)/shard_map/while/body/eval_jaxpr/nfks,nfsr->nkr/dot_general | solution.py:39
  393.2 22.4 %fusion.122 = f32[4,16,64,16]{2,3,1,0:T(8,128)S(1)} fusion(f32[4,16,64,16]{2,3,1,0:T(8,128)S(1)} %get-tuple-element.243, s32[]{:T(128)S(6)} %copy.114, f32[16,27,64,16]{2,3,1,0:T(8,128)} %bitcast.142, f32[16,27,64,64]{3,2,1,0:T(8,128)} %multiply_reduce_fusion.8), kind=kOutput, calls=%fused_computation.43.clone.1 | convolution fusion | flops 346816512 | bytes 8978436 | tf_op jit(solution)/shard_map/while/body/eval_jaxpr/nfks,nfsr->nkr/dot_general | solution.py:39
  438.2 22.4 %fusion.122 = f32[4,16,64,16]{2,3,1,0:T(8,128)S(1)} fusion(f32[4,16,64,16]{2,3,1,0:T(8,128)S(1)} %get-tuple-element.243, s32[]{:T(128)S(6)} %copy.114, f32[16,27,64,16]{2,3,1,0:T(8,128)} %bitcast.142, f32[16,27,64,64]{3,2,1,0:T(8,128)} %multiply_reduce_fusion.8), kind=kOutput, calls=%fused_computation.43.clone.1 | convolution fusion | flops 346816512 | bytes 8978436 | tf_op jit(solution)/shard_map/while/body/eval_jaxpr/nfks,nfsr->nkr/dot_general | solution.py:39
  483.3 22.4 %fusion.122 = f32[4,16,64,16]{2,3,1,0:T(8,128)S(1)} fusion(f32[4,16,64,16]{2,3,1,0:T(8,128)S(1)} %get-tuple-element.243, s32[]{:T(128)S(6)} %copy.114, f32[16,27,64,16]{2,3,1,0:T(8,128)} %bitcast.142, f32[16,27,64,64]{3,2,1,0:T(8,128)} %multiply_reduce_fusion.8), kind=kOutput, calls=%fused_computation.43.clone.1 | convolution fusion | flops 346816512 | bytes 8978436 | tf_op jit(solution)/shard_map/while/body/eval_jaxpr/nfks,nfsr->nkr/dot_general | solution.py:39
  509.4 18.0 %multiply_reduce_fusion.2 = f32[8,64,64,64]{3,2,1,0:T(8,128)} fusion(f32[8,64,3,64]{3,2,1,0:T(4,128)S(1)} %bitcast.146, f32[8,3,64]{2,1,0:T(4,128)S(1)} %sub.99), kind=kLoop, calls=%fused_computation.49 | loop fusion | flops 16777216 | bytes 8787968 | tf_op jit(solution)/shard_map/while/body/eval_jaxpr/reduce_sum | solution.py:25
  545.4 24.7 %fusion.53 = f32[8,64,16]{1,2,0:T(8,128)S(1)} fusion(f32[8,64,64,16]{2,3,1,0:T(8,128)} %bitcast.145, f32[8,64,64,64]{3,2,1,0:T(8,128)} %multiply_reduce_fusion.2), kind=kOutput, calls=%fused_computation.73 | convolution fusion | flops 411041792 | bytes 10518528 | tf_op jit(solution)/shard_map/while/body/eval_jaxpr/nfks,nfsr->nkr/dot_general | solution.py:39
  571.3 19.0 %reshape.267 = f32[1024,64,16]{2,1,0:T(8,128)} reshape(f32[128,8,1024]{2,1,0:T(8,128)} %all-to-all-done.1) | data formatting | bytes 8388608 | tf_op jit(solution)/shard_map/reshape | solution.py:134
  590.3 20.8 %copy.89 = f32[1024,64,16]{1,2,0:T(8,128)} copy(f32[1024,64,16]{2,1,0:T(8,128)} %reshape.267) | data formatting | bytes 8388608 | tf_op jit(solution)/shard_map/while | solution.py:41
  611.1 410.0 %while.4 = (s32[]{:T(128)}, f32[4,16,64,16]{2,3,1,0:T(8,128)S(1)}, f32[4,16,3,64]{3,2,1,0:T(4,128)}, s32[4,16,64]{2,1,0:T(8,128)}, f32[1024,3,64]{2,1,0:T(4,128)}, /*index=5*/f32[1024,64,16]{1,2,0:T(8,128)}, s32[]{:T(128)}) while((s32[]{:T(128)}, f32[4,16,64,16]{2,3,1,0:T(8,128)S(1)}, f32[4,16,3,64]{3,2,1,0:T(4,128)}, s32[4,16,64]{2,1,0:T(8,128)}, ...), condition=%wide.region_2.3_spmd, body=%wide.region_0.0_spmd.sunk | while | flops 855642112 | bytes 69668992 | solution.py:41
  631.0 35.6 %multiply_reduce_fusion.7 = f32[16,64,64,64]{3,2,1,0:T(8,128)} fusion(f32[16,64,3,64]{3,2,1,0:T(4,128)S(1)} %bitcast.143, f32[16,3,64]{2,1,0:T(4,128)S(1)} %dynamic-slice_bitcast_fusion.5), kind=kLoop, calls=%fused_computation.15.clone.1 | loop fusion | flops 33554432 | bytes 17575936 | tf_op jit(solution)/shard_map/while/body/eval_jaxpr/reduce_sum | solution.py:25
  666.6 47.2 %fusion.119 = f32[4,16,64,16]{2,3,1,0:T(8,128)S(1)} fusion(f32[4,16,64,16]{2,3,1,0:T(8,128)S(1)} %get-tuple-element.264, s32[]{:T(128)S(6)} %copy.120, f32[16,64,64,16]{2,3,1,0:T(8,128)S(1)} %bitcast.140, f32[16,64,64,64]{3,2,1,0:T(8,128)} %multiply_reduce_fusion.7), kind=kOutput, calls=%fused_computation.26.clone.1 | convolution fusion | flops 822083584 | bytes 25296900 | tf_op jit(solution)/shard_map/while/body/eval_jaxpr/nfks,nfsr->nkr/dot_general | solution.py:39
  733.4 35.6 %multiply_reduce_fusion.7 = f32[16,64,64,64]{3,2,1,0:T(8,128)} fusion(f32[16,64,3,64]{3,2,1,0:T(4,128)S(1)} %bitcast.143, f32[16,3,64]{2,1,0:T(4,128)S(1)} %dynamic-slice_bitcast_fusion.5), kind=kLoop, calls=%fused_computation.15.clone.1 | loop fusion | flops 33554432 | bytes 17575936 | tf_op jit(solution)/shard_map/while/body/eval_jaxpr/reduce_sum | solution.py:25
  769.0 47.2 %fusion.119 = f32[4,16,64,16]{2,3,1,0:T(8,128)S(1)} fusion(f32[4,16,64,16]{2,3,1,0:T(8,128)S(1)} %get-tuple-element.264, s32[]{:T(128)S(6)} %copy.120, f32[16,64,64,16]{2,3,1,0:T(8,128)S(1)} %bitcast.140, f32[16,64,64,64]{3,2,1,0:T(8,128)} %multiply_reduce_fusion.7), kind=kOutput, calls=%fused_computation.26.clone.1 | convolution fusion | flops 822083584 | bytes 25296900 | tf_op jit(solution)/shard_map/while/body/eval_jaxpr/nfks,nfsr->nkr/dot_general | solution.py:39
  835.8 35.6 %multiply_reduce_fusion.7 = f32[16,64,64,64]{3,2,1,0:T(8,128)} fusion(f32[16,64,3,64]{3,2,1,0:T(4,128)S(1)} %bitcast.143, f32[16,3,64]{2,1,0:T(4,128)S(1)} %dynamic-slice_bitcast_fusion.5), kind=kLoop, calls=%fused_computation.15.clone.1 | loop fusion | flops 33554432 | bytes 17575936 | tf_op jit(solution)/shard_map/while/body/eval_jaxpr/reduce_sum | solution.py:25
  871.4 47.2 %fusion.119 = f32[4,16,64,16]{2,3,1,0:T(8,128)S(1)} fusion(f32[4,16,64,16]{2,3,1,0:T(8,128)S(1)} %get-tuple-element.264, s32[]{:T(128)S(6)} %copy.120, f32[16,64,64,16]{2,3,1,0:T(8,128)S(1)} %bitcast.140, f32[16,64,64,64]{3,2,1,0:T(8,128)} %multiply_reduce_fusion.7), kind=kOutput, calls=%fused_computation.26.clone.1 | convolution fusion | flops 822083584 | bytes 25296900 | tf_op jit(solution)/shard_map/while/body/eval_jaxpr/nfks,nfsr->nkr/dot_general | solution.py:39
  938.2 35.6 %multiply_reduce_fusion.7 = f32[16,64,64,64]{3,2,1,0:T(8,128)} fusion(f32[16,64,3,64]{3,2,1,0:T(4,128)S(1)} %bitcast.143, f32[16,3,64]{2,1,0:T(4,128)S(1)} %dynamic-slice_bitcast_fusion.5), kind=kLoop, calls=%fused_computation.15.clone.1 | loop fusion | flops 33554432 | bytes 17575936 | tf_op jit(solution)/shard_map/while/body/eval_jaxpr/reduce_sum | solution.py:25
  973.8 47.2 %fusion.119 = f32[4,16,64,16]{2,3,1,0:T(8,128)S(1)} fusion(f32[4,16,64,16]{2,3,1,0:T(8,128)S(1)} %get-tuple-element.264, s32[]{:T(128)S(6)} %copy.120, f32[16,64,64,16]{2,3,1,0:T(8,128)S(1)} %bitcast.140, f32[16,64,64,64]{3,2,1,0:T(8,128)} %multiply_reduce_fusion.7), kind=kOutput, calls=%fused_computation.26.clone.1 | convolution fusion | flops 822083584 | bytes 25296900 | tf_op jit(solution)/shard_map/while/body/eval_jaxpr/nfks,nfsr->nkr/dot_general | solution.py:39
  (233 shorter events, 375.4 us)
Async XLA Ops:
  17.7 36.4 %copy-start.2 = (f32[8,192]{1,0:T(8,128)S(1)}, f32[8,192]{1,0:T(8,128)}, u32[]{:S(2)}) copy-start(f32[8,192]{1,0:T(8,128)} %param.29) | copy-start | bytes 18436
  21.4 289.4 %collective-permute-start.1 = (f32[8,192]{1,0:T(8,128)}, f32[8,192]{1,0:T(8,128)}, u32[]{:S(2)}, u32[]{:S(2)}) collective-permute-start(f32[8,192]{1,0:T(8,128)} %slice.27), channel_id=1, source_target_pairs={{1,0},{2,1},{3,2},{4,3},{5,4},{6,5},{7,6},{8,7},{9,8},{10,9},{11,1... | collective-permute-start | bytes 18440 | tf_op jit(solution)/shard_map/ppermute | solution.py:20
  25.4 49.2 %copy-start.29 = (s32[1024]{0:T(1024)S(1)}, s32[1024]{0:T(1024)}, u32[]{:S(2)}) copy-start(s32[1024]{0:T(1024)} %param.36) | copy-start | bytes 12292
  25.5 286.1 %collective-permute-start = (f32[8,192]{1,0:T(8,128)}, f32[8,192]{1,0:T(8,128)}, u32[]{:S(2)}, u32[]{:S(2)}) collective-permute-start(f32[8,192]{1,0:T(8,128)} %slice.25), channel_id=1, source_target_pairs={{0,1},{1,2},{2,3},{3,4},{4,5},{5,6},{6,7},{7,8},{8,9},{9,10},{10,1... | collective-permute-start | bytes 18440 | tf_op jit(solution)/shard_map/ppermute | solution.py:20
  47.6 264.8 %collective-permute-start.3 = (f32[8,1024]{1,0:T(8,128)}, f32[8,1024]{1,0:T(8,128)}, u32[]{:S(2)}, u32[]{:S(2)}) collective-permute-start(f32[8,1024]{1,0:T(8,128)} %slice.31), channel_id=1, source_target_pairs={{1,0},{2,1},{3,2},{4,3},{5,4},{6,5},{7,6},{8,7},{9,8},{10,9},{11,1... | collective-permute-start | bytes 98312 | tf_op jit(solution)/shard_map/ppermute | solution.py:20
  50.4 263.0 %collective-permute-start.2 = (f32[8,1024]{1,0:T(8,128)}, f32[8,1024]{1,0:T(8,128)}, u32[]{:S(2)}, u32[]{:S(2)}) collective-permute-start(f32[8,1024]{1,0:T(8,128)} %slice.29), channel_id=1, source_target_pairs={{0,1},{1,2},{2,3},{3,4},{4,5},{5,6},{6,7},{7,8},{8,9},{9,10},{10,1... | collective-permute-start | bytes 98312 | tf_op jit(solution)/shard_map/ppermute | solution.py:20
  55.9 79.8 %all-to-all-start.2 = ((f32[128,2,192]{2,1,0:T(2,128)}), f32[128,2,192]{2,1,0:T(2,128)}, u32[]{:S(2)}, u32[]{:S(2)}) async-start(f32[128,2,192]{2,1,0:T(2,128)} %all_to_all.28), calls=%async_computation.2 | async-start | bytes 524288 | tf_op jit(solution)/shard_map/all_to_all | solution.py:98
  74.7 56.4 %copy-start.18 = (s32[1024]{0:T(1024)}, s32[1024]{0:T(1024)S(1)}, u32[]{:S(2)}) copy-start(s32[1024]{0:T(1024)S(1)} %fusion.78) | copy-start | bytes 12292
  74.7 53.1 %copy-start.32 = (s32[1,64]{1,0:T(1,128)S(1)}, s32[1,64]{1,0:T(1,128)}, u32[]{:S(2)}) copy-start(s32[1,64]{1,0:T(1,128)} %param.34) | copy-start | bytes 772
  74.7 54.2 %copy-start.24 = (f32[1,4096]{1,0:T(1,128)S(1)}, f32[1,4096]{1,0:T(1,128)}, u32[]{:S(2)}) copy-start(f32[1,4096]{1,0:T(1,128)} %param.27) | copy-start | bytes 49156
  74.7 55.7 %copy-start.22 = (f32[16,192]{1,0:T(8,128)S(1)}, f32[16,192]{1,0:T(8,128)}, u32[]{:S(2)}) copy-start(f32[16,192]{1,0:T(8,128)} %param.31) | copy-start | bytes 36868
  74.7 56.4 %copy-start.1 = (f32[64,192]{1,0:T(8,128)S(1)}, f32[64,192]{1,0:T(8,128)}, u32[]{:S(2)}) copy-start(f32[64,192]{1,0:T(8,128)} %param.28) | copy-start | bytes 147460
  82.9 52.8 %copy-start.4 = (f32[8,64,64]{2,1,0:T(8,128)}, f32[8,64,64]{2,1,0:T(8,128)S(1)}, u32[]{:S(2)}) copy-start(f32[8,64,64]{2,1,0:T(8,128)S(1)} %reshape.274) | copy-start | bytes 393220
  83.0 52.8 %copy-start.30 = (s32[8,64]{1,0:T(8,128)S(1)}, s32[8,64]{1,0:T(8,128)}, u32[]{:S(2)}) copy-start(s32[8,64]{1,0:T(8,128)} %param.33) | copy-start | bytes 6148
  86.5 54.9 %copy-start.27 = (f32[1,192]{1,0:T(1,128)S(1)}, f32[1,192]{1,0:T(1,128)}, u32[]{:S(2)}) copy-start(f32[1,192]{1,0:T(1,128)} %param.30) | copy-start | bytes 2308
  135.8 98.4 %all-to-all-start = ((f32[128,8,192]{2,1,0:T(8,128)}), f32[128,8,192]{2,1,0:T(8,128)}, u32[]{:S(2)}, u32[]{:S(2)}) async-start(f32[128,8,192]{2,1,0:T(8,128)} %bitcast.15), calls=%async_computation | async-start | bytes 2097152 | tf_op jit(solution)/shard_map/all_to_all | solution.py:87
  200.2 51.3 %copy-start.14 = (f32[64,64]{1,0:T(8,128)S(1)}, f32[64,64]{1,0:T(8,128)}, u32[]{:S(2)}) copy-start(f32[64,64]{1,0:T(8,128)} %copy-done.13) | copy-start | bytes 49156
  200.2 52.1 %copy-start.10 = (f32[3,64,64]{2,0,1:T(4,128)S(1)}, f32[3,64,64]{2,0,1:T(4,128)}, u32[]{:S(2)}) copy-start(f32[3,64,64]{2,0,1:T(4,128)} %copy-done.9) | copy-start | bytes 147460
  200.2 53.0 %copy-start.19 = (s32[1024]{0:T(1024)S(1)}, s32[1024]{0:T(1024)}, u32[]{:S(2)}) copy-start(s32[1024]{0:T(1024)} %copy-done.18) | copy-start | bytes 12292
  201.1 51.2 %copy-start.26 = (s32[512]{0:T(512)S(1)}, s32[512]{0:T(512)}, u32[]{:S(2)}) copy-start(s32[512]{0:T(512)} %reshape.351) | copy-start | bytes 6148
  234.2 80.3 %all-to-all-start.3 = ((f32[128,2,1024]{2,1,0:T(2,128)}), f32[128,2,1024]{2,1,0:T(2,128)}, u32[]{:S(2)}, u32[]{:S(2)}) async-start(f32[128,2,1024]{2,1,0:T(2,128)} %all_to_all.30), calls=%async_computation.3 | async-start | bytes 2097152 | tf_op jit(solution)/shard_map/all_to_all | solution.py:97
  314.5 256.8 %all-to-all-start.1 = ((f32[128,8,1024]{2,1,0:T(8,128)}), f32[128,8,1024]{2,1,0:T(8,128)}, u32[]{:S(2)}, u32[]{:S(2)}) async-start(f32[128,8,1024]{2,1,0:T(8,128)} %all_to_all.26), calls=%async_computation.1 | async-start | bytes 8388608 | tf_op jit(solution)/shard_map/all_to_all | solution.py:86
  611.1 410.1 %copy-start.15 = (f32[8,64,16]{1,2,0:T(8,128)S(1)}, f32[8,64,16]{1,2,0:T(8,128)}, u32[]{:S(2)}) copy-start(f32[8,64,16]{1,2,0:T(8,128)} %fusion.56) | copy-start | bytes 98308
  611.1 415.1 %copy-start.7 = (f32[4,16,64,16]{2,3,1,0:T(8,128)S(1)}, f32[4,16,64,16]{2,3,1,0:T(8,128)}, u32[]{:S(2)}) copy-start(f32[4,16,64,16]{2,3,1,0:T(8,128)} %copy-done.6) | copy-start | bytes 786436
  (20 other events, 393.1 us)
where the time goes:
time: 1060 us; the launch traced here: 1050 us
  matrix products  327 us (31%)
  local copies, waits for them, and re-layouts  306 us (29%)
  other arithmetic  240 us (23%)
  blocking collectives  111 us (10%)
  starting transfers between devices  60.6 us (6%)
    dot_general x10, matrix products, block_product(): jnp.einsum('nfks,nfsr->nkr', kernel, table_values[chosen], precision=high...  307 us
    reduce_sum x11, other arithmetic, matern(): distance = jnp.sqrt(jnp.sum(delta * delta, axis=-3))  232 us
    gather x10, local copies, waits for them, and re-layouts, block_product(): table_values[chosen]  67.3 us
    all_gather x1, blocking collectives, shards(): lax.all_gather(root_skeleton, ('gx', 'gy'), axis=0, tiled=True)  42.4 us
    all_gather x1, blocking collectives, shards(): lax.all_gather(up_root.reshape(roots, RANK * RHS), ('gx', 'gy'), axis=0,...  40.8 us
    gather x10, local copies, waits for them, and re-layouts, block_product(): kernel = matern(targets[:, None], table_points[chosen])  32.6 us
    gather x2, local copies, waits for them, and re-layouts, shards(): outgoing = up_leaf[leaf_sends].reshape(-1, RANK * RHS)  29.2 us
    all_to_all x1, local copies, waits for them, and re-layouts, shards(): lax.all_to_all(outgoing, ('gx', 'gy'), split_axis=0, concat_axis=0, tiled...  28.3 us
  transfers between devices with their start and end apart: 8, of which 0 were waited for; matrix products, arithmetic and copies ran while one was open for 33% of the time, Pallas kernels for 0%

commit v1 on v0

v1 whole, which is shorter than its diff:
```python
import math

import jax
import jax.numpy as jnp
from jax import lax
from jax.experimental import pallas as pl
from jax.experimental.pallas import tpu as pltpu
from jax.sharding import PartitionSpec as P

LEAF = 64
RANK = 64
RHS = 16
FEATS = 32
COLS = 4

both = ("gx", "gy")
f32 = jnp.float32
bf16 = jnp.bfloat16
log2e = 1.0 / math.log(2.0)
scale = math.sqrt(3.0) / 0.3 * log2e

VM = pl.BlockSpec(memory_space=pltpu.VMEM)
SM = pl.BlockSpec(memory_space=pltpu.SMEM)


def lanes(shape):
    return lax.broadcasted_iota(jnp.int32, shape, len(shape) - 1)


def swap(x):
    return pltpu.roll(x, 64, axis=x.ndim - 1)


def halves(x):
    high = x.astype(bf16)
    return high, (x - high.astype(f32)).astype(bf16)


def thirds(x):
    first = x.astype(bf16).astype(f32)
    rest = x - first
    second = rest.astype(bf16).astype(f32)
    return first, second, (rest - second).astype(bf16).astype(f32)


NN = (((1,), (0,)), ((), ()))
NT = (((1,), (1,)), ((), ()))


def dot(a, b, dims=NN):
    return lax.dot_general(a, b, dims, preferred_element_type=f32)


def dot3(a, b, dims=NN):
    ah, al = halves(a)
    bh, bl = halves(b)
    rows = a.shape[0]
    first = dot(jnp.concatenate([ah, al], axis=0), bh, dims)
    return first[:rows] + first[rows:] + dot(ah, bl, dims)


def stacked(rows, norm_row, one_row, factor):
    x, y, z = [(jnp.broadcast_to(r, (8, 128)) - 0.5) * scale for r in rows]
    norm = x * x + y * y + z * z
    sub = lax.broadcasted_iota(jnp.int32, (8, 128), 0)
    out = jnp.where(sub < 2, x, jnp.where(sub < 4, y, z)) * factor
    out = jnp.where(sub == norm_row, norm, out)
    return jnp.where(sub == one_row, 1.0, out), sub


def target_features(rows):
    base, sub = stacked(rows, 6, 7, -2.0)
    first, second, third = thirds(base)
    even = sub % 2 == 0
    last = jnp.where(sub == 7, 1.0, jnp.where(even, third, second))
    return jnp.concatenate(
        [first, jnp.where(even, second, first), last, jnp.zeros_like(first)], axis=0
    ).astype(bf16)


def source_features(rows):
    base, sub = stacked(rows, 7, 6, 1.0)
    first, second, third = thirds(base)
    even = sub % 2 == 0
    norm = sub == 7
    return jnp.concatenate(
        [
            jnp.where(even | norm, first, second),
            jnp.where(even, first, jnp.where(norm, second, third)),
            jnp.where(even, first, jnp.where(norm, third, second)),
            jnp.zeros_like(first),
        ],
        axis=0,
    ).astype(bf16)


def source_pair(rows, s_ref, at):
    features = source_features(rows)
    tall = jnp.concatenate([features] * COLS, axis=0)
    eye = (lax.broadcasted_iota(jnp.int32, (128, 128), 0) == lanes((128, 128))).astype(f32).astype(bf16)
    turned = dot(eye, tall, NT).astype(bf16)
    s_ref[at] = turned[:64]
    s_ref[at + 1] = turned[64:]


def put_values(x_ref, at, wide):
    high, low = halves(wide)
    x_ref[at, 0] = high
    x_ref[at, 1] = low


def values_from_tile(tile):
    left = lanes(tile.shape) < 64
    other = swap(tile)
    return jnp.concatenate([jnp.where(left, tile, other), jnp.where(left, other, tile)], axis=0)


def twice(rows, upper):
    left = lanes(rows.shape) < 64
    return jnp.where(left, swap(rows), rows) if upper else jnp.where(left, rows, swap(rows))


def couple(ids, s_ref, x_ref, target):
    zero = jnp.zeros_like(target)
    left = lanes(target.shape) < 64
    lower = jnp.where(left, target, zero)
    upper = jnp.where(left, zero, target)
    spread = jnp.concatenate(
        [
            jnp.concatenate([lower, upper, zero, zero], axis=0),
            jnp.concatenate([zero, zero, lower, upper], axis=0),
        ],
        axis=1,
    )
    group = lanes((64, 128)) // FEATS
    highs, lows = [], []
    for quad in ids:
        s = s_ref[quad[3]]
        for c in (2, 1, 0):
            s = jnp.where(group <= c, s_ref[quad[c]], s)
        square = jnp.maximum(dot(s, spread), 1e-30)
        u = square * lax.rsqrt(square)
        kernel = (u + log2e) * jnp.exp2(-u)
        high, low = halves(kernel)
        highs.append(high)
        lows.append(low)
    k_high = jnp.concatenate(highs, axis=0)
    k_low = jnp.concatenate(lows, axis=0)
    near = lanes((16, 128)) < 64

    def joined(part):
        out = []
        for c in range(COLS):
            pieces = []
            for g in range(0, len(ids) - 1, 2):
                pieces.append(jnp.where(near, x_ref[ids[g][c], part], x_ref[ids[g + 1][c], part]))
            if len(ids) % 2:
                pieces.append(x_ref[ids[-1][c], part][:, :64])
            out.append(jnp.concatenate(pieces, axis=1))
        return jnp.concatenate(out, axis=0)

    x_high, x_low = joined(0), joined(1)
    rows = 16 * COLS
    first = dot(jnp.concatenate([x_high, x_low], axis=0), k_high)
    total = first[:rows] + first[rows:] + dot(x_high, k_low)
    even = total[:16, :128] + total[32:48, 128:]
    odd = total[16:32, :128] + total[48:, 128:]
    return even, odd


def two_targets(first, second):
    left = lanes(first[0].shape) < 64
    return (
        jnp.where(left, first[0], second[1]) + swap(jnp.where(left, second[0], first[1]))
    ) * (1.0 / log2e)


def one_target(pair):
    return (pair[0] + swap(pair[1])) * (1.0 / log2e)


def quads(index, row, count):
    return [[index[row, 4 * g + c] for c in range(4)] for g in range(count)]


def call(kernel, name, out, in_specs, scratch=(), flops=0, data=0, limit=48):
    return pl.pallas_call(
        kernel,
        name=name,
        out_shape=out,
        in_specs=in_specs,
        out_specs=jax.tree.map(lambda _: VM, out),
        scratch_shapes=list(scratch),
        cost_estimate=pl.CostEstimate(flops=flops, bytes_accessed=data, transcendentals=0),
        compiler_params=pltpu.CompilerParams(vmem_limit_bytes=limit * 2**20),
    )


def shape(*dims, kind=f32):
    return jax.ShapeDtypeStruct(dims, kind)


def pack_skeletons(sends, middle_sends, leaf_table, middle_table, out):
    left = lanes((3, 128)) < 64

    def body(b, _):
        rows = []
        for p in range(4):
            rows.append(
                jnp.where(left, leaf_table[sends[b * 8 + 2 * p]], leaf_table[sends[b * 8 + 2 * p + 1]])
            )
        rows.append(
            jnp.where(left, middle_table[middle_sends[2 * b]], middle_table[middle_sends[2 * b + 1]])
        )
        rows.append(jnp.zeros((1, 128), f32))
        out[b] = jnp.concatenate(rows, axis=0)
        return 0

    lax.fori_loop(0, 128, body, 0, unroll=4)


def permute_columns(source, index, out):
    height = source.shape[0] // 8

    def body(j, _):
        where = jnp.broadcast_to(index[pl.ds(j, 1), :], (8, 128))
        inside = where % 128
        tile = where // 128
        found = [jnp.zeros((8, 128), f32)] * height
        for i in range(32):
            match = tile == i
            for r in range(height):
                piece = source[8 * r : 8 * r + 8, 128 * i : 128 * i + 128]
                piece = jnp.take_along_axis(piece, inside, axis=1, mode="promise_in_bounds")
                found[r] = jnp.where(match, piece, found[r])
        for r in range(height):
            out[8 * r : 8 * r + 8, pl.ds(pl.multiple_of(j * 128, 128), 128)] = found[r]
        return 0

    lax.fori_loop(0, 32, body, 0)


def up_leaves(sends, source, order, basis, tree, up, out, tiles):
    permute_columns(source, order, tree)

    def leaf_pair(i, _):
        columns = pl.ds(pl.multiple_of(i * 128, 128), 128)
        x = tree[0:16, columns]
        a = dot3(x[:, :64], basis[2 * i])
        b = dot3(x[:, 64:], basis[2 * i + 1])
        up[:, columns] = jnp.concatenate([a, b], axis=1)
        tiles[2 * i] = jnp.concatenate([a[:8], a[8:]], axis=1)
        tiles[2 * i + 1] = jnp.concatenate([b[:8], b[8:]], axis=1)
        return 0

    lax.fori_loop(0, 32, leaf_pair, 0, unroll=4)

    def slot(s, _):
        out[s] = tiles[sends[s]]
        return 0

    lax.fori_loop(0, 1024, slot, 0, unroll=16)


def up_rest(sends, up, leaf_maps, middle_maps, root_maps, root_rows, middle_out, root_out, tiles):
    parts = []
    for j in range(8):
        part = dot3(up[:, 512 * j : 512 * j + 512], leaf_maps[512 * j : 512 * j + 512, :])
        tiles[j] = jnp.concatenate([part[:8], part[8:]], axis=1)
        parts.append(part)
    middle = jnp.concatenate(parts, axis=1)
    root = dot3(middle, middle_maps[...])
    top = dot3(root, root_maps[...])
    root_out[0:8] = jnp.concatenate([root[:8], root[8:]], axis=1)
    root_out[8:16] = jnp.concatenate([top[:8], top[8:]], axis=1)
    root_out[16:24] = root_rows[...]

    def slot(s, _):
        middle_out[s] = tiles[sends[s]]
        return 0

    lax.fori_loop(0, 256, slot, 0, unroll=16)


def invert(order, inverse):
    def body(i, _):
        inverse[order[i]] = i
        return 0

    lax.fori_loop(0, 4096, body, 0, unroll=32)


def near_field(index, window, out, s_ref, x_ref):
    s_ref[80] = jnp.zeros((64, 128), bf16)
    x_ref[80] = jnp.zeros((2, 16, 128), bf16)

    def prepare(i, _):
        block = window[:, pl.ds(pl.multiple_of(i * 128, 128), 128)]
        source_pair([block[16:17], block[17:18], block[18:19]], s_ref, 2 * i)
        put_values(x_ref, 2 * i, twice(block[:16], False))
        put_values(x_ref, 2 * i + 1, twice(block[:16], True))
        return 0

    lax.fori_loop(0, 40, prepare, 0, unroll=2)

    def pair(i, _):
        block = window[16:24, pl.ds(pl.multiple_of(i * 128 + 512, 128), 128)]
        results = []
        for half in range(2):
            points = twice(block, half == 1)
            target = target_features([points[0:1], points[1:2], points[2:3]])
            l = 2 * i + half
            sources = [l + 8] + [index[l, f] for f in range(26)] + [80]
            ids = [sources[4 * g : 4 * g + 4] for g in range(7)]
            results.append(couple(ids, s_ref, x_ref, target))
        out[:, pl.ds(pl.multiple_of(i * 128, 128), 128)] = two_targets(*results)
        return 0

    lax.fori_loop(0, 32, pair, 0)


def leaf_sources(received, s_ref):
    def prepare(q, _):
        block = received[q]
        for p in range(4):
            rows = [block[3 * p + j : 3 * p + j + 1] for j in range(3)]
            source_pair(rows, s_ref, q * 8 + 2 * p)
        return 0

    lax.fori_loop(0, 128, prepare, 0)


def far_leaves(index, tiles, s_ref, target_rows, out, x_ref):
    def prepare(s, _):
        put_values(x_ref, s, values_from_tile(tiles[s]))
        return 0

    lax.fori_loop(0, 1024, prepare, 0, unroll=8)
    far_pairs(index, s_ref, x_ref, target_rows, out, 32)


def far_pairs(index, s_ref, x_ref, target_rows, out, pairs):
    def pair(i, _):
        results = []
        for half in range(2):
            l = 2 * i + half
            rows = target_rows[l]
            target = target_features([rows[0:1], rows[1:2], rows[2:3]])
            results.append(couple(quads(index, l, 16), s_ref, x_ref, target))
        out[:, pl.ds(pl.multiple_of(i * 128, 128), 128)] = two_targets(*results)
        return 0

    lax.fori_loop(0, pairs, pair, 0)


def far_upper(
    middle_index, root_index, group, skeletons, middle_tiles, roots, middle_rows, top_rows,
    middle_out, root_out, top_out, s_ref, x_ref,
):
    left = lanes((1, 128)) < 64

    def middle_pair(q, _):
        block = skeletons[q]
        source_pair([block[12 + j : 13 + j] for j in range(3)], s_ref, 2 * q)
        put_values(x_ref, 2 * q, values_from_tile(middle_tiles[2 * q]))
        put_values(x_ref, 2 * q + 1, values_from_tile(middle_tiles[2 * q + 1]))
        return 0

    lax.fori_loop(0, 128, middle_pair, 0, unroll=2)
    far_pairs(middle_index, s_ref, x_ref, middle_rows, middle_out, 4)

    def root_pair(q, _):
        a, b = roots[2 * q], roots[2 * q + 1]
        source_pair([jnp.where(left, a[16 + j : 17 + j], b[16 + j : 17 + j]) for j in range(3)], s_ref, 2 * q)
        put_values(x_ref, 2 * q, values_from_tile(a[:8]))
        put_values(x_ref, 2 * q + 1, values_from_tile(b[:8]))
        return 0

    lax.fori_loop(0, 64, root_pair, 0, unroll=2)
    own = roots[group[1]]
    target = target_features([own[16:17], own[17:18], own[18:19]])
    root_out[...] = one_target(couple(quads(root_index, 0, 16), s_ref, x_ref, target))

    for q in range(8):
        a, b = top_rows[2 * q], top_rows[2 * q + 1]
        source_pair([jnp.where(left, a[j : j + 1], b[j : j + 1]) for j in range(3)], s_ref, 2 * q)

    def parent(h, _):
        total = roots[8 * h][8:16]
        for n in range(1, 8):
            total = total + roots[8 * h + n][8:16]
        total = jnp.where(h == group[0], jnp.zeros_like(total), total)
        put_values(x_ref, h, values_from_tile(total))
        return 0

    lax.fori_loop(0, 16, parent, 0)
    mine = top_rows[group[0]]
    target = target_features([mine[0:1], mine[1:2], mine[2:3]])
    ids = [[4 * g + c for c in range(4)] for g in range(4)]
    top_out[...] = one_target(couple(ids, s_ref, x_ref, target))


def down(near, far, far_middle, far_root, top_far, basis, leaf_maps, middle_maps, root_maps, inverse, out, tree):
    root = far_root[:, :64] + dot3(top_far[:, :64], root_maps[...], NT)
    middle = far_middle[...] + dot3(root, middle_maps[...], NT)
    for j in range(8):
        columns = slice(512 * j, 512 * j + 512)
        leaf = far[:, columns] + dot3(middle[:, 64 * j : 64 * j + 64], leaf_maps[columns, :], NT)
        for p in range(4):
            l = 8 * j + 2 * p
            a = dot3(leaf[:, 128 * p : 128 * p + 64], basis[l], NT)
            b = dot3(leaf[:, 128 * p + 64 : 128 * p + 128], basis[l + 1], NT)
            tree[:, 64 * l : 64 * l + 128] = jnp.concatenate([a, b], axis=1) + near[:, 64 * l : 64 * l + 128]
    permute_columns(tree, inverse, out)


def from_behind(block, distance):
    devices = range(lax.axis_size(both))
    return lax.ppermute(block, both, [(i - distance, i) for i in devices if i - distance in devices])


def paired(skeleton):
    rows = skeleton.reshape(-1, 3, RANK)
    return jnp.concatenate([rows, rows], axis=2)


def exchange(x):
    return lax.all_to_all(x, both, split_axis=0, concat_axis=0, tiled=True)


def shards(
    values,
    coords,
    order,
    leaf_basis,
    leaf_transfer,
    middle_transfer,
    root_transfer,
    leaf_skeleton,
    middle_skeleton,
    root_skeleton,
    top_skeleton,
    leaf_far,
    middle_far,
    root_far,
    leaf_near,
    leaf_sends,
    middle_sends,
):
    leaf_rows = paired(leaf_skeleton)
    middle_rows = paired(middle_skeleton)
    root_rows = paired(root_skeleton)[0]
    top_rows = paired(top_skeleton)
    packed = call(pack_skeletons, "pack_skeletons", shape(128, 16, 128), [SM, SM, VM, VM])(
        leaf_sends, middle_sends, leaf_rows, middle_rows
    )
    skeletons = exchange(packed)

    basis = leaf_basis.reshape(64, LEAF, RANK)
    source = jnp.concatenate([values, coords, jnp.zeros((5, values.shape[1]), f32)], axis=0)
    tree, up, outgoing = call(
        up_leaves,
        "up_leaves",
        (shape(24, 4096), shape(16, 4096), shape(1024, 8, 128)),
        [SM, VM, VM, VM],
        [pltpu.VMEM((64, 8, 128), f32)],
        data=8 * 2**20,
    )(leaf_sends, source, order.reshape(32, 128), basis)
    tiles = exchange(outgoing.reshape(128, 64, 128)).reshape(1024, 8, 128)

    before = from_behind(tree[:, 4096 - 512 :], 1)
    after = from_behind(tree[:, :512], -1)

    leaf_maps = leaf_transfer.reshape(64 * RANK, RANK)
    middle_maps = middle_transfer.reshape(8 * RANK, RANK)
    root_maps = root_transfer.reshape(RANK, RANK)
    middle_out, root_out = call(
        up_rest,
        "up_rest",
        (shape(256, 8, 128), shape(24, 128)),
        [SM, VM, VM, VM, VM, VM],
        [pltpu.VMEM((8, 8, 128), f32)],
        data=4 * 2**20,
    )(
        middle_sends, up, leaf_maps, middle_maps, root_maps,
        jnp.concatenate([root_rows, jnp.zeros((5, 128), f32)], axis=0),
    )
    middle_tiles = exchange(middle_out.reshape(128, 16, 128)).reshape(256, 8, 128)
    roots = lax.all_gather(root_out[None], both, axis=0, tiled=True)

    window = jnp.concatenate([before, tree, after], axis=1)
    near = call(
        near_field,
        "near_field",
        shape(16, 4096),
        [SM, VM],
        [pltpu.VMEM((81, 64, 128), bf16), pltpu.VMEM((81, 2, 16, 128), bf16)],
        flops=22 * 10**9,
    )(leaf_near, window)
    inverse = pl.pallas_call(
        invert,
        name="invert",
        out_shape=shape(4096, kind=jnp.int32),
        in_specs=[SM],
        out_specs=SM,
        cost_estimate=pl.CostEstimate(flops=6 * 10**9, bytes_accessed=0, transcendentals=0),
    )(order).reshape(32, 128)
    leaf_table = call(
        leaf_sources, "leaf_sources", shape(1024, 64, 128, kind=bf16), [VM], flops=12 * 10**9
    )(skeletons)
    far = call(
        far_leaves,
        "far_leaves",
        shape(16, 4096),
        [SM, VM, VM, VM],
        [pltpu.VMEM((1024, 2, 16, 128), bf16)],
        flops=50 * 10**9,
    )(leaf_far, tiles, leaf_table, leaf_rows)
    group = jnp.stack([lax.axis_index("gx"), lax.axis_index(both)]).astype(jnp.int32)
    far_middle, far_root, top_far = call(
        far_upper,
        "far_upper",
        (shape(16, 512), shape(16, 128), shape(16, 128)),
        [SM, SM, SM, VM, VM, VM, VM, VM],
        [pltpu.VMEM((256, 64, 128), bf16), pltpu.VMEM((256, 2, 16, 128), bf16)],
        flops=10 * 10**9,
    )(middle_far, root_far, group, skeletons, middle_tiles, roots, middle_rows, top_rows)
    return call(
        down,
        "down",
        shape(16, 4096),
        [VM] * 10,
        [pltpu.VMEM((16, 4096), f32)],
        data=8 * 2**20,
    )(near, far, far_middle, far_root, top_far, basis, leaf_maps, middle_maps, root_maps, inverse)


def solution(mesh):
    split = P(both, None)
    placed = (
        P(None, both),
        P(None, both),
        P(both),
        split,
        split,
        split,
        split,
        split,
        split,
        split,
        P(),
        split,
        split,
        split,
        split,
        P(both),
        P(both),
    )
    return jax.shard_map(
        shards, mesh=mesh, in_specs=placed, out_specs=P(None, both), check_vma=False
    )
```

time: 1060 us -> 295 us (0.28); the launches traced: 1050 us -> 293 us
  matrix products: 327 us -> 0 us
  local copies, waits for them, and re-layouts: 306 us -> 30.4 us
  other arithmetic: 240 us -> 9.4 us
  Pallas kernels: 0 us -> 194 us
  blocking collectives: 111 us -> 0 us
  starting transfers between devices: 60.6 us -> 41.1 us
  between operations: 1.12 us -> 13.6 us
    dot_general x19 -> x0, matrix products: 327 us -> none  [the longest x10 307 us: block_product(): jnp.einsum('nfks,nfsr->nkr', kernel, table_values[chosen], precision=high...]
    reduce_sum x11 -> x0, other arithmetic: 232 us -> none  [matern(): distance = jnp.sqrt(jnp.sum(delta * delta, axis=-3))]
    pallas_call x0 -> x9, Pallas kernels: none -> 194 us  [the longest x1 64.2 us: shards(): call(far_leaves, 'far_leaves', shape(16, 4096), [SM, VM, VM, VM], [pltpu....]
    gather x30 -> x0, local copies, waits for them, and re-layouts: 173 us -> none  [the longest x10 67.3 us: block_product(): table_values[chosen]]
    all_gather x3 -> x0, blocking collectives: 98.9 us -> none  [the longest x1 42.4 us: shards(): lax.all_gather(root_skeleton, ('gx', 'gy'), axis=0, tiled=True)]
    all_to_all x3 -> x0, local copies, waits for them, and re-layouts: 36.8 us -> none  [the longest x1 28.3 us: shards(): lax.all_to_all(outgoing, ('gx', 'gy'), split_axis=0, concat_axis=0, tiled...]
    reshape x13 -> x8, local copies, waits for them, and re-layouts: 44.5 us -> 11.1 us  [the longest x4 3.57 us: paired(): rows = skeleton.reshape(-1, 3, RANK)]
    while x9 -> x0, local copies, waits for them, and re-layouts: 20.9 us -> none  [the longest x1 20.8 us: interact(): lax.map(block_product, (target_points.reshape(count // block, block, 3, i...]
  transfers between devices with their start and end apart: 8 -> 6, of which waited for: 0 -> 2; matrix products, arithmetic and copies ran while one was open for 33% -> 8% of each run, Pallas kernels for 0% -> 40%
where the time goes in v1:
time: 295 us; the launch traced here: 293 us
  Pallas kernels  194 us (66%)
  starting transfers between devices  41.1 us (14%)
  local copies, waits for them, and re-layouts  30.4 us (10%)
  between operations  13.6 us (5%)
  other arithmetic  9.4 us (3%)
  waiting for transfers between devices  5.27 us (2%)
    pallas_call x1, Pallas kernels, shards(): call(far_leaves, 'far_leaves', shape(16, 4096), [SM, VM, VM, VM], [pltpu....  64.2 us
    all_to_all x3, starting transfers between devices, exchange(): return lax.all_to_all(x, both, split_axis=0, concat_axis=0, tiled=True)  35.5 us
    pallas_call x1, Pallas kernels, shards(): call(leaf_sources, 'leaf_sources', shape(1024, 64, 128, kind=bf16), [VM],...  34.9 us
    pallas_call x1, Pallas kernels, shards(): call(near_field, 'near_field', shape(16, 4096), [SM, VM], [pltpu.VMEM((81...  34.3 us
    pallas_call x1, Pallas kernels, shards(): call(far_upper, 'far_upper', (shape(16, 512), shape(16, 128), shape(16, 1...  28 us
    unnamed x59, local copies, waits for them, and re-layouts  17.7 us
    pallas_call x1, Pallas kernels, shards(): call(up_leaves, 'up_leaves', (shape(24, 4096), shape(16, 4096), shape(102...  12.2 us
    pallas_call x1, Pallas kernels, shards(): call(down, 'down', shape(16, 4096), [VM] * 10, [pltpu.VMEM((16, 4096), f3...  8.72 us
  transfers between devices with their start and end apart: 6, of which 2 were waited for; matrix products, arithmetic and copies ran while one was open for 8% of the time, Pallas kernels for 40%

profile of v1, /device:TPU:1, one launch (start us, length us, event | category | flops | bytes accessed | tf_op | source)
XLA Modules:
  0.0 293.4 jit_solution(14914506427336336671)
XLA Ops:
  10.0 3.1 %pack_skeletons.1 = f32[128,16,128]{2,1,0:T(8,128)} custom-call(s32[1024]{0:T(1024)S(1)} %copy-done.14, s32[256]{0:T(256)S(1)} %copy-done.21, f32[64,3,128]{2,1,0:T(4,128)S(1)} %pad_maximum_fusion.1.leaf_table.target_rows, f32[8,3,128]{2,1,0:T(4,128)S(1)} %pad_maximum_fusion.3.middle_table.middle_rows), custom_call_target="tpu_custom_call" | custom-call | tf_op jit(solution)/shard_map/pack_skeletons/pallas_call | solution.py:454
  13.1 11.5 %all-to-all-start.1 = ((f32[128,16,128]{2,1,0:T(8,128)}), f32[128,16,128]{2,1,0:T(8,128)S(1)}, u32[]{:S(2)}, u32[]{:S(2)}) async-start(f32[128,16,128]{2,1,0:T(8,128)} %pack_skeletons.1), calls=%async_computation.1 | async-start | bytes 2097152 | tf_op jit(solution)/shard_map/all_to_all | solution.py:428
  24.6 2.0 reshape.43.basis
  26.6 3.1 %reshape.48.leaf_maps = f32[4096,64]{1,0:T(8,128)} reshape(f32[64,4096]{1,0:T(8,128)} %param.21) | data formatting | bytes 2097152 | tf_op jit(solution)/shard_map/reshape | solution.py:474
  31.3 2.0 reduce.6
  34.8 1.9 reduce.7
  41.5 12.2 %up_leaves.1 = (f32[24,4096]{1,0:T(8,128)S(1)}, f32[16,4096]{1,0:T(8,128)S(1)}, f32[1024,8,128]{2,1,0:T(8,128)}) custom-call(s32[1024]{0:T(1024)S(1)} %copy-done.15, f32[24,4096]{1,0:T(8,128)S(1)} %maximum_maximum_fusion.source, s32[32,128]{1,0:T(8,128)S(1)} %bitcast.13, f32[64,64,64]{2,1,0:T(8,128)S(1)} %reshape.43.basis), custom_call_target="tpu_custom_call" | custom-call | bytes 8388608 | tf_op jit(solution)/shard_map/up_leaves/pallas_call | solution.py:461
  55.9 1.7 up_rest.1
  59.2 10.2 %all-to-all-start.2 = ((f32[128,16,128]{2,1,0:T(8,128)}), f32[128,16,128]{2,1,0:T(8,128)}, u32[]{:S(2)}, u32[]{:S(2)}) async-start(f32[128,16,128]{2,1,0:T(8,128)} %bitcast.12), calls=%async_computation.2 | async-start | bytes 2097152 | tf_op jit(solution)/shard_map/all_to_all | solution.py:428
  69.5 1.5 fusion
  71.0 3.0 %collective-permute-start.1 = (f32[24,512]{1,0:T(8,128)}, f32[24,512]{1,0:T(8,128)}, u32[]{:S(2)}, u32[]{:S(2)}) collective-permute-start(f32[24,512]{1,0:T(8,128)} %get-tuple-element.22), channel_id=1, source_target_pairs={{1,0},{2,1},{3,2},{4,3},{5,4},{6,5},{7,6},{8,7},{9,8},{10,9},{11,1... | collective-permute-start | bytes 147464 | tf_op jit(solution)/shard_map/ppermute | solution.py:419
  74.0 2.5 collective-permute-start
  76.6 1.4 reshape.54
  78.0 1.5 pad_maximum_fusion.2.top_rows
  79.5 6.4 %invert.1 = s32[4096]{0:T(1024)} custom-call(s32[4096]{0:T(1024)} %order.1), custom_call_target="tpu_custom_call" | custom-call | flops 6000000000 | tf_op jit(solution)/shard_map/invert/pallas_call | solution.py:500
  86.6 1.4 copy.19.index
  88.2 13.8 %all-to-all-start = ((f32[128,64,128]{2,1,0:T(8,128)}), f32[128,64,128]{2,1,0:T(8,128)}, u32[]{:S(2)}, u32[]{:S(2)}) async-start(f32[128,64,128]{2,1,0:T(8,128)} %bitcast.16), calls=%async_computation | async-start | bytes 8388608 | tf_op jit(solution)/shard_map/all_to_all | solution.py:428
  103.8 34.3 %near_field.1.near = f32[16,4096]{1,0:T(8,128)S(1)} custom-call(s32[64,26]{1,0:T(8,128)S(1)} %copy-done.10, f32[24,5120]{1,0:T(8,128)S(1)} %pad_maximum_fusion.window), custom_call_target="tpu_custom_call" | custom-call | flops 22000001024 | tf_op jit(solution)/shard_map/near_field/pallas_call | solution.py:492
  138.8 34.9 %leaf_sources.1.s_ref = bf16[1024,64,128]{2,1,0:T(8,128)(2,1)} custom-call(f32[128,16,128]{2,1,0:T(8,128)S(1)} %all-to-all-done.1.received.skeletons), custom_call_target="tpu_custom_call" | custom-call | flops 12000000000 | tf_op jit(solution)/shard_map/leaf_sources/pallas_call | solution.py:508
  173.7 5.1 %all-gather.3.cloned.1.call-done = f32[3072,128]{1,0:T(8,128)} async-done(((f32[24,128]{1,0:T(8,128)}), f32[3072,128]{1,0:T(8,128)}) %all-gather.3.cloned.1.call-update) | async-done | bytes 1572880 | tf_op jit(solution)/shard_map/all_gather | solution.py:489
  179.5 1.4 copy-done.23
  182.9 28.0 %far_upper.1 = (f32[16,512]{1,0:T(8,128)S(1)}, f32[16,128]{1,0:T(8,128)S(1)}, f32[16,128]{1,0:T(8,128)S(1)}) custom-call(s32[8,64]{1,0:T(8,128)S(1)} %copy-done.25, s32[1,64]{1,0:T(1,128)S(1)} %copy-done.26, s32[2]{0:T(128)S(1)} %copy-done.27, f32[128,16,128]{2,1,0:T(8,128)S(1)} %all-to-all-done.1.received.skeletons, f32[256,8,128]{2,1,0:T(8,128)} %bitcast.8.middle_tiles, ...), custom_call_target="tpu_custom_call" | custom-call | flops 10000000000 | tf_op jit(solution)/shard_map/far_upper/pallas_call | solution.py:520
  213.6 64.2 %far_leaves.1.far = f32[16,4096]{1,0:T(8,128)S(1)} custom-call(s32[64,64]{1,0:T(8,128)S(1)} %copy-done.24, f32[1024,8,128]{2,1,0:T(8,128)} %bitcast.2.tiles, bf16[1024,64,128]{2,1,0:T(8,128)(2,1)} %leaf_sources.1.s_ref, f32[64,3,128]{2,1,0:T(4,128)S(1)} %pad_maximum_fusion.1.leaf_table.target_rows), custom_call_target="tpu_custom_call" | custom-call | flops 49999998976 | tf_op jit(solution)/shard_map/far_leaves/pallas_call | solution.py:511
  277.8 8.7 %down.1 = f32[16,4096]{1,0:T(8,128)} custom-call(f32[16,4096]{1,0:T(8,128)S(1)} %copy-done.7, f32[16,4096]{1,0:T(8,128)S(1)} %far_leaves.1.far, f32[16,512]{1,0:T(8,128)S(1)} %copy-done.9, f32[16,128]{1,0:T(8,128)S(1)} %copy-done.18, f32[16,128]{1,0:T(8,128)S(1)} %copy-done.20, f32[64,64,64]{2,1,0:T(8,128)S(1)} %reshape.43.basis, f32[4096,64]{1,0:T(8,128)S(1)} %copy-done.1, ...), custom_call_target="tpu_custom_call" | custom-call | bytes 8388608 | tf_op jit(solution)/shard_map/down/pallas_call | solution.py:528
  (78 shorter events, 23.8 us)
Async XLA Ops:
  8.6 0.7 copy-start.14
  13.1 46.1 %all-to-all-start.1 = ((f32[128,16,128]{2,1,0:T(8,128)}), f32[128,16,128]{2,1,0:T(8,128)S(1)}, u32[]{:S(2)}, u32[]{:S(2)}) async-start(f32[128,16,128]{2,1,0:T(8,128)} %pack_skeletons.1), calls=%async_computation.1 | async-start | bytes 2097152 | tf_op jit(solution)/shard_map/all_to_all | solution.py:428
  38.0 16.5 %copy-start = (f32[4096,64]{1,0:T(8,128)S(1)}, f32[4096,64]{1,0:T(8,128)}, u32[]{:S(2)}) copy-start(f32[4096,64]{1,0:T(8,128)} %reshape.48.leaf_maps) | copy-start | bytes 3145732
  40.1 0.7 copy-start.12
  53.7 0.7 copy-start.3
  54.4 0.8 copy-start.4
  57.6 1.0 copy-start.2
  59.2 28.9 %all-to-all-start.2 = ((f32[128,16,128]{2,1,0:T(8,128)}), f32[128,16,128]{2,1,0:T(8,128)}, u32[]{:S(2)}, u32[]{:S(2)}) async-start(f32[128,16,128]{2,1,0:T(8,128)} %bitcast.12), calls=%async_computation.2 | async-start | bytes 2097152 | tf_op jit(solution)/shard_map/all_to_all | solution.py:428
  69.5 109.3 %all-gather.3.cloned.1.call-start = ((), (), s32[]{:S(2)}) async-start(), calls=%async_computation.3 | async-start | bytes 1585152 | tf_op jit(solution)/shard_map/all_gather | solution.py:489
  71.0 31.0 %collective-permute-start.1 = (f32[24,512]{1,0:T(8,128)}, f32[24,512]{1,0:T(8,128)}, u32[]{:S(2)}, u32[]{:S(2)}) collective-permute-start(f32[24,512]{1,0:T(8,128)} %get-tuple-element.22), channel_id=1, source_target_pairs={{1,0},{2,1},{3,2},{4,3},{5,4},{6,5},{7,6},{8,7},{9,8},{10,9},{11,1... | collective-permute-start | bytes 147464 | tf_op jit(solution)/shard_map/ppermute | solution.py:419
  74.0 28.0 %collective-permute-start = (f32[24,512]{1,0:T(8,128)}, f32[24,512]{1,0:T(8,128)}, u32[]{:S(2)}, u32[]{:S(2)}) collective-permute-start(f32[24,512]{1,0:T(8,128)} %get-tuple-element.21), channel_id=1, source_target_pairs={{0,1},{1,2},{2,3},{3,4},{4,5},{5,6},{6,7},{7,8},{8,9},{9,10},{10,1... | collective-permute-start | bytes 147464 | tf_op jit(solution)/shard_map/ppermute | solution.py:419
  88.2 124.6 %all-to-all-start = ((f32[128,64,128]{2,1,0:T(8,128)}), f32[128,64,128]{2,1,0:T(8,128)}, u32[]{:S(2)}, u32[]{:S(2)}) async-start(f32[128,64,128]{2,1,0:T(8,128)} %bitcast.16), calls=%async_computation | async-start | bytes 8388608 | tf_op jit(solution)/shard_map/all_to_all | solution.py:428
  103.0 0.8 copy-start.10
  138.1 0.7 copy-start.6
  178.8 0.8 copy-start.11
  179.5 1.4 copy-start.23
  212.8 0.8 copy-start.24
  213.5 64.2 %copy-start.1 = (f32[4096,64]{1,0:T(8,128)S(1)}, f32[4096,64]{1,0:T(8,128)}, u32[]{:S(2)}) copy-start(f32[4096,64]{1,0:T(8,128)} %reshape.48.leaf_maps) | copy-start | bytes 3145732
  213.5 64.2 %copy-start.5 = (f32[64,64]{1,0:T(8,128)S(1)}, f32[64,64]{1,0:T(8,128)}, u32[]{:S(2)}) copy-start(f32[64,64]{1,0:T(8,128)} %reshape.50.root_maps) | copy-start | bytes 49156
  213.5 64.2 %copy-start.7 = (f32[16,4096]{1,0:T(8,128)S(1)}, f32[16,4096]{1,0:T(8,128)}, u32[]{:S(2)}) copy-start(f32[16,4096]{1,0:T(8,128)} %copy-done.6) | copy-start | bytes 786436
  213.5 64.2 %copy-start.9 = (f32[16,512]{1,0:T(8,128)S(1)}, f32[16,512]{1,0:T(8,128)}, u32[]{:S(2)}) copy-start(f32[16,512]{1,0:T(8,128)} %copy-done.8) | copy-start | bytes 98308
  213.5 64.2 %copy-start.13 = (s32[4096]{0:T(1024)S(1)}, s32[4096]{0:T(1024)}, u32[]{:S(2)}) copy-start(s32[4096]{0:T(1024)} %invert.1) | copy-start | bytes 49156
  213.5 64.2 %copy-start.18 = (f32[16,128]{1,0:T(8,128)S(1)}, f32[16,128]{1,0:T(8,128)}, u32[]{:S(2)}) copy-start(f32[16,128]{1,0:T(8,128)} %copy-done.17) | copy-start | bytes 24580
  213.6 64.2 %copy-start.20 = (f32[16,128]{1,0:T(8,128)S(1)}, f32[16,128]{1,0:T(8,128)}, u32[]{:S(2)}) copy-start(f32[16,128]{1,0:T(8,128)} %copy-done.19) | copy-start | bytes 24580
  (10 other events, 6.5 us)
Sparse Core Ops, SparseCore 0:
  76.7 102.0 all-gather.2

commit v2 on v1

v2 whole, which is shorter than its diff:
```python
import math

import jax
import jax.numpy as jnp
from jax import lax
from jax.experimental import pallas as pl
from jax.experimental.pallas import tpu as pltpu
from jax.sharding import PartitionSpec as P

LEAF = 64
RANK = 64
RHS = 16
FEATS = 32
COLS = 4

both = ("gx", "gy")
f32 = jnp.float32
bf16 = jnp.bfloat16
log2e = 1.0 / math.log(2.0)
scale = math.sqrt(3.0) / 0.3 * log2e

VM = pl.BlockSpec(memory_space=pltpu.VMEM)
SM = pl.BlockSpec(memory_space=pltpu.SMEM)


def lanes(shape):
    return lax.broadcasted_iota(jnp.int32, shape, len(shape) - 1)


def swap(x):
    return pltpu.roll(x, 64, axis=x.ndim - 1)


def halves(x):
    high = x.astype(bf16)
    return high, (x - high.astype(f32)).astype(bf16)


def thirds(x):
    first = x.astype(bf16).astype(f32)
    rest = x - first
    second = rest.astype(bf16).astype(f32)
    return first, second, (rest - second).astype(bf16).astype(f32)


NN = (((1,), (0,)), ((), ()))
NT = (((1,), (1,)), ((), ()))


def dot(a, b, dims=NN):
    return lax.dot_general(a, b, dims, preferred_element_type=f32)


def dot3(a, b, dims=NN):
    ah, al = halves(a)
    bh, bl = halves(b)
    rows = a.shape[0]
    first = dot(jnp.concatenate([ah, al], axis=0), bh, dims)
    return first[:rows] + first[rows:] + dot(ah, bl, dims)


def stacked(rows, norm_row, one_row, factor):
    x, y, z = [(jnp.broadcast_to(r, (8, 128)) - 0.5) * scale for r in rows]
    norm = x * x + y * y + z * z
    sub = lax.broadcasted_iota(jnp.int32, (8, 128), 0)
    out = jnp.where(sub < 2, x, jnp.where(sub < 4, y, z)) * factor
    out = jnp.where(sub == norm_row, norm, out)
    return jnp.where(sub == one_row, 1.0, out), sub


def target_features(rows):
    base, sub = stacked(rows, 6, 7, -2.0)
    first, second, third = thirds(base)
    even = sub % 2 == 0
    last = jnp.where(sub == 7, 1.0, jnp.where(even, third, second))
    return jnp.concatenate(
        [first, jnp.where(even, second, first), last, jnp.zeros_like(first)], axis=0
    ).astype(bf16)


def source_features(rows):
    base, sub = stacked(rows, 7, 6, 1.0)
    first, second, third = thirds(base)
    even = sub % 2 == 0
    norm = sub == 7
    return jnp.concatenate(
        [
            jnp.where(even | norm, first, second),
            jnp.where(even, first, jnp.where(norm, second, third)),
            jnp.where(even, first, jnp.where(norm, third, second)),
            jnp.zeros_like(first),
        ],
        axis=0,
    ).astype(bf16)


def source_row(v, column):
    return (v & -8) + ((v & 1) << 2) + ((column - (v >> 1)) & 3)


def source_eight(pairs, s_ref, at):
    tall = jnp.concatenate([source_features(rows) for rows in pairs], axis=0)
    eye = (lax.broadcasted_iota(jnp.int32, (128, 128), 0) == lanes((128, 128))).astype(f32).astype(bf16)
    turned = dot(eye, tall, NT)
    for k in range(COLS):
        moved = (turned if k == 0 else pltpu.roll(turned, FEATS * k, axis=1)).astype(bf16)
        s_ref[at + k] = moved[:64]
        s_ref[at + COLS + k] = moved[64:]


def put_values(x_ref, at, wide):
    high, low = halves(wide)
    x_ref[at, 0] = high
    x_ref[at, 1] = low


def values_from_tile(tile):
    left = lanes(tile.shape) < 64
    other = swap(tile)
    return jnp.concatenate([jnp.where(left, tile, other), jnp.where(left, other, tile)], axis=0)


def twice(rows, upper):
    left = lanes(rows.shape) < 64
    return jnp.where(left, swap(rows), rows) if upper else jnp.where(left, rows, swap(rows))


def make_kernel(ids, start, s_ref, spread, k_ref):
    stop = min(start + 4, len(ids) // COLS)
    group = lanes((64, 128)) // FEATS
    stack = []
    for g in range(start, stop):
        quad = ids[4 * g : 4 * g + 4]
        s = s_ref[source_row(quad[3], 3)]
        for c in (2, 1, 0):
            s = jnp.where(group <= c, s_ref[source_row(quad[c], c)], s)
        stack.append(s)
    square = jnp.maximum(dot(jnp.concatenate(stack, axis=0), spread), 1e-30)
    u = square * lax.rsqrt(square)
    high, low = halves((u + log2e) * jnp.exp2(-u))
    k_ref[0, 64 * start : 64 * stop] = high
    k_ref[1, 64 * start : 64 * stop] = low


def apply_kernel(ids, start, x_ref, k_ref, total):
    count = len(ids) // COLS
    stop = min(start + 4, count)
    near = lanes((16, 128)) < 64

    def joined(part):
        out = []
        for c in range(COLS):
            pieces = []
            for g in range(start, stop, 2):
                first = x_ref[ids[4 * g + c], part]
                if g + 1 < count:
                    pieces.append(jnp.where(near, first, x_ref[ids[4 * g + 4 + c], part]))
                else:
                    pieces.append(first[:, :64])
            out.append(jnp.concatenate(pieces, axis=1))
        return jnp.concatenate(out, axis=0)

    x_high, x_low = joined(0), joined(1)
    rows = slice(64 * start, 64 * stop)
    first = dot(jnp.concatenate([x_high, x_low], axis=0), k_ref[0, rows])
    second = dot(x_high, k_ref[1, rows])
    return (first, second) if total is None else (total[0] + first, total[1] + second)


def summed(total):
    rows = 16 * COLS
    whole = total[0][:rows] + total[0][rows:] + total[1]
    return whole[:16, :128] + whole[32:48, 128:], whole[16:32, :128] + whole[48:, 128:]


def spread_target(target):
    zero = jnp.zeros_like(target)
    left = lanes(target.shape) < 64
    lower = jnp.where(left, target, zero)
    upper = jnp.where(left, zero, target)
    return jnp.concatenate(
        [
            jnp.concatenate([lower, upper, zero, zero], axis=0),
            jnp.concatenate([zero, zero, lower, upper], axis=0),
        ],
        axis=1,
    )


def couple(ids, s_ref, x_ref, target, k_ref):
    spread = spread_target(target)
    total = None
    for q in range(0, len(ids) // COLS, 4):
        make_kernel(ids, q, s_ref, spread, k_ref)
        total = apply_kernel(ids, q, x_ref, k_ref, total)
    return summed(total)


def couple_all(count, ids, target, s_ref, x_ref, out, ka, kb, unroll=1):
    def advance(new, k_new, old, k_old):
        made, used = ids(new), ids(old)
        spread = spread_target(target(new))
        total = None
        for q in range(0, len(made) // COLS, 4):
            make_kernel(made, q, s_ref, spread, k_new)
            total = apply_kernel(used, q, x_ref, k_old, total)
        return summed(total)

    first = ids(0)
    spread = spread_target(target(0))
    for q in range(0, len(first) // COLS, 4):
        make_kernel(first, q, s_ref, spread, ka)

    def pair(i, _):
        lower = advance(2 * i + 1, kb, 2 * i, ka)
        upper = advance(jnp.minimum(2 * i + 2, count - 1), ka, 2 * i + 1, kb)
        out[:, pl.ds(pl.multiple_of(i * 128, 128), 128)] = two_targets(lower, upper)
        return 0

    lax.fori_loop(0, count // 2, pair, 0, unroll=unroll)


def two_targets(first, second):
    left = lanes(first[0].shape) < 64
    return (
        jnp.where(left, first[0], second[1]) + swap(jnp.where(left, second[0], first[1]))
    ) * (1.0 / log2e)


def one_target(pair):
    return (pair[0] + swap(pair[1])) * (1.0 / log2e)


HBM = pl.BlockSpec(memory_space=pl.ANY)


def call(kernel, name, out, in_specs, scratch=(), flops=0, data=0, limit=60):
    return pl.pallas_call(
        kernel,
        name=name,
        out_shape=out,
        in_specs=in_specs,
        out_specs=jax.tree.map(lambda _: VM, out),
        scratch_shapes=list(scratch),
        cost_estimate=pl.CostEstimate(flops=flops, bytes_accessed=data, transcendentals=0),
        compiler_params=pltpu.CompilerParams(vmem_limit_bytes=limit * 2**20),
    )


def shape(*dims, kind=f32):
    return jax.ShapeDtypeStruct(dims, kind)


def put_rows(skeleton, table):
    first = skeleton[:, :128]
    table[0] = twice(first, False)
    table[1] = twice(first, True)
    last = skeleton[:, 128:]
    table[2] = jnp.concatenate([last, last], axis=1)


def rows_of(table, at):
    return [table[j, pl.ds(at, 1), :] for j in range(3)]


def pair_rows(table, a, b):
    left = lanes((1, 128)) < 64
    return [jnp.where(left, x, y) for x, y in zip(rows_of(table, a), rows_of(table, b))]


def pack_skeletons(sends, middle_sends, leaf_skeleton, middle_skeleton, out, leaf_table, middle_table):
    put_rows(leaf_skeleton, leaf_table)
    put_rows(middle_skeleton, middle_table)

    def body(b, _):
        rows = []
        for p in range(4):
            rows += pair_rows(leaf_table, sends[b * 8 + 2 * p], sends[b * 8 + 2 * p + 1])
        rows += pair_rows(middle_table, middle_sends[2 * b], middle_sends[2 * b + 1])
        rows.append(jnp.zeros((1, 128), f32))
        out[b] = jnp.concatenate(rows, axis=0)
        return 0

    lax.fori_loop(0, 128, body, 0, unroll=4)


def take(x, index):
    pieces = [
        jnp.take_along_axis(x[r : r + 8], index, axis=1, mode="promise_in_bounds")
        for r in range(0, x.shape[0], 8)
    ]
    return pieces[0] if len(pieces) == 1 else jnp.concatenate(pieces, axis=0)


def even_first():
    i = lanes((8, 128))
    return (i & 64) + 2 * (i & 31) + ((i >> 5) & 1)


def evens_odds():
    i = lanes((8, 128))
    return ((i & 32) << 1) + 2 * (i & 31) + (i >> 6)


def evens_odds_back():
    i = lanes((8, 128))
    return ((i & 1) << 6) + ((i >> 6) << 5) + ((i & 63) >> 1)


def permute_columns(source, index, out, halved):
    height = source.shape[0] // 8

    def body(j, _):
        where = jnp.broadcast_to(index[pl.ds(j, 1), :], (8, 128))
        if halved:
            where = take(where, even_first())
        inside = where & 127
        tile = where >> 7
        found = [jnp.zeros((8, 128), f32)] * height
        for i in range(32):
            match = tile == i
            for r in range(height):
                piece = source[8 * r : 8 * r + 8, 128 * i : 128 * i + 128]
                found[r] = jnp.where(match, take(piece, inside), found[r])
        for r in range(height):
            out[8 * r : 8 * r + 8, pl.ds(pl.multiple_of(j * 128, 128), 128)] = found[r]
        return 0

    lax.fori_loop(0, 32, body, 0, unroll=2)


def pair_halves(result):
    return result[:16] + swap(result[16:])


def as_tile(x):
    left = lanes((8, 128)) < 64
    return jnp.where(left, x[:8], swap(x[8:]))


def side_by_side(a, b):
    return jnp.where(lanes(a.shape) < 64, a, swap(b))


def even_odd_rows(blocks):
    left = lanes((16, 128)) < 64
    even, odd = [], []
    for v, w in zip(blocks[::2], blocks[1::2]):
        even.append(jnp.where(left, v, swap(w)))
        odd.append(jnp.where(left, swap(v), w))
    return jnp.concatenate([jnp.concatenate(even, axis=1), jnp.concatenate(odd, axis=1)], axis=0)


def tree_order(values, coords, order, tree, first_leaves, last_leaves, source):
    source[0:16] = values[...]
    source[16:19] = coords[...]
    source[19:24] = jnp.zeros((5, 4096), f32)
    permute_columns(source, order, tree, True)
    first_leaves[...] = tree[:, :512]
    last_leaves[...] = tree[:, 3584:]


def up_pass(
    sends, middle_sends, tree, root_skeleton, basis, leaf_maps, middle_maps, root_maps,
    out, root_out, basis_rows, leaf_rows, middle_rows, root_rows,
    split, tiles, middle_tiles, root_table, sems,
):
    copies = []
    for m, (whole, rows) in enumerate(
        ((basis, basis_rows), (leaf_maps, leaf_rows), (middle_maps, middle_rows), (root_maps, root_rows))
    ):
        copies.append(
            [
                pltpu.make_async_copy(whole.at[:, pl.ds(128 * t, 128)], rows.at[:, t, :], sems.at[m, t])
                for t in range(32)
            ]
        )
    for group in copies:
        for copy in group:
            copy.start()
    for copy in copies[0]:
        copy.wait()

    def leaf_pair(i, _):
        columns = pl.ds(pl.multiple_of(i * 128, 128), 128)
        x = tree[0:16, columns]
        a = pair_halves(dot3(jnp.concatenate([x[:, :32], x[:, 32:64]], axis=0), basis_rows[2 * i]))
        b = pair_halves(dot3(jnp.concatenate([x[:, 64:96], x[:, 96:]], axis=0), basis_rows[2 * i + 1]))
        split[:, columns] = take(side_by_side(a, b), evens_odds())
        tiles[2 * i] = as_tile(a)
        tiles[2 * i + 1] = as_tile(b)
        return 0

    lax.fori_loop(0, 32, leaf_pair, 0, unroll=4)

    def slots(b, _):
        for c in range(8):
            out[b, 8 * c : 8 * c + 8] = tiles[sends[8 * b + c]]
        return 0

    lax.fori_loop(0, 128, slots, 0, unroll=2)
    for group in copies[1:]:
        for copy in group:
            copy.wait()
    middles = []
    for j in range(8):
        blocks = [split[:, 512 * j + 128 * p : 512 * j + 128 * p + 128] for p in range(4)]
        part = pair_halves(dot3(even_odd_rows(blocks), leaf_rows[8 * j : 8 * j + 8].reshape(256, 128)))
        middle_tiles[j] = as_tile(part)
        middles.append(part)
    blocks = [take(side_by_side(middles[2 * p], middles[2 * p + 1]), evens_odds()) for p in range(4)]
    root = pair_halves(dot3(even_odd_rows(blocks), middle_rows[...].reshape(256, 128)))
    turned = take(root, evens_odds())
    top = pair_halves(dot3(jnp.concatenate([turned[:, :32], turned[:, 64:96]], axis=0), root_rows[0]))
    put_rows(root_skeleton, root_table)
    root_out[0:8] = as_tile(root)
    root_out[8:16] = as_tile(top)
    root_out[16:24] = jnp.concatenate(rows_of(root_table, 0) + [jnp.zeros((5, 128), f32)], axis=0)

    def middle_slots(b, _):
        for c in range(2):
            out[b, 64 + 8 * c : 72 + 8 * c] = middle_tiles[middle_sends[2 * b + c]]
        return 0

    lax.fori_loop(0, 128, middle_slots, 0, unroll=4)


def invert(order, inverse):
    def body(b, _):
        for p in range(64):
            inverse[order[b * 64 + p]] = b * 64 + (p % 2) * 32 + p // 2
        return 0

    lax.fori_loop(0, 64, body, 0)


def near_field(index, before, tree, after, out, window, s_ref, x_ref, ka, kb):
    window[:, :512] = before[...]
    window[:, 512:4608] = tree[...]
    window[:, 4608:] = after[...]
    for k in range(8):
        s_ref[80 + k] = jnp.zeros((64, 128), bf16)
    x_ref[80] = jnp.zeros((2, 16, 128), bf16)

    def prepare(i, _):
        pairs = []
        for p in range(4):
            block = window[:, pl.ds(pl.multiple_of(i * 512 + p * 128, 128), 128)]
            pairs.append([block[16:17], block[17:18], block[18:19]])
            put_values(x_ref, 8 * i + 2 * p, twice(block[:16], False))
            put_values(x_ref, 8 * i + 2 * p + 1, twice(block[:16], True))
        source_eight(pairs, s_ref, 8 * i)
        return 0

    lax.fori_loop(0, 10, prepare, 0, unroll=2)

    def ids(l):
        return [l + 8] + [index[f, l] for f in range(26)] + [80]

    def target(l):
        block = window[16:24, pl.ds(pl.multiple_of((l >> 1) * 128 + 512, 128), 128)]
        left = lanes(block.shape) < 64
        points = jnp.where(left == (l % 2 == 0), block, swap(block))
        return target_features([points[0:1], points[1:2], points[2:3]])

    couple_all(64, ids, target, s_ref, x_ref, out, ka, kb, unroll=2)


def sources(received, s_ref, middle_ref):
    def prepare(q, _):
        block = received[q]
        source_eight([[block[3 * p + j : 3 * p + j + 1] for j in range(3)] for p in range(4)], s_ref, q * 8)
        return 0

    lax.fori_loop(0, 128, prepare, 0, unroll=4)

    def middle(q, _):
        source_eight(
            [[received[4 * q + p, 12 + j : 13 + j] for j in range(3)] for p in range(4)], middle_ref, q * 8
        )
        return 0

    lax.fori_loop(0, 32, middle, 0, unroll=4)


def far_ids(index):
    return lambda l: [index[l, f] for f in range(64)]


def far_leaves(index, skeleton, received, table, out, s_ref, tiles, x_ref, rows, ka, kb, sems):
    parts = [
        pltpu.make_async_copy(
            received.at[pl.ds(32 * p, 32), pl.ds(0, 64), :], tiles.at[pl.ds(32 * p, 32)], sems.at[p]
        )
        for p in range(4)
    ]
    for part in parts:
        part.start()
    loaded = pltpu.make_async_copy(table, s_ref, sems.at[4])
    loaded.start()
    put_rows(skeleton, rows)
    for p in range(4):
        parts[p].wait()

        def prepare(q, _):
            for c in range(8):
                put_values(x_ref, 8 * q + c, values_from_tile(tiles[q, 8 * c : 8 * c + 8]))
            return 0

        lax.fori_loop(32 * p, 32 * p + 32, prepare, 0)
    loaded.wait()
    couple_all(
        64, far_ids(index), lambda l: target_features(rows_of(rows, l)), s_ref, x_ref, out, ka, kb
    )


def lifted(x, rows):
    left = lanes(x.shape) < 64
    zero = jnp.zeros_like(x)
    wide = jnp.concatenate([jnp.where(left, x, zero), jnp.where(left, zero, swap(x))], axis=0)
    return dot3(wide, rows, NT)


def natural(result, p):
    part = slice(64 * p, 64 * p + 64)
    return take(jnp.concatenate([result[:16, part], result[16:, part]], axis=1), evens_odds_back())


def finish(
    middle_index, root_index, received, middle_table, roots, middle_skeleton, top_skeleton,
    near, far, basis_rows, leaf_rows, middle_rows, root_rows, inverse,
    out, far_middle, x_ref, s_ref, ka, kb, middle_points, top_points, tree,
):
    left = lanes((1, 128)) < 64
    put_rows(middle_skeleton, middle_points)
    put_rows(top_skeleton, top_points)
    group = lax.axis_index("gx")

    def middle_values(q, _):
        for c in range(2):
            put_values(x_ref, 2 * q + c, values_from_tile(received[q, 8 * c : 8 * c + 8]))
        return 0

    lax.fori_loop(0, 128, middle_values, 0, unroll=4)
    couple_all(
        8, far_ids(middle_index), lambda l: target_features(rows_of(middle_points, l)),
        middle_table, x_ref, far_middle, ka, kb,
    )

    def root_sources(q, _):
        pairs = []
        for p in range(4):
            a, b = roots[8 * q + 2 * p], roots[8 * q + 2 * p + 1]
            pairs.append([jnp.where(left, a[16 + j : 17 + j], b[16 + j : 17 + j]) for j in range(3)])
            put_values(x_ref, 8 * q + 2 * p, values_from_tile(a[:8]))
            put_values(x_ref, 8 * q + 2 * p + 1, values_from_tile(b[:8]))
        source_eight(pairs, s_ref, 8 * q)
        return 0

    lax.fori_loop(0, 16, root_sources, 0, unroll=2)
    own = roots[lax.axis_index(both)]
    target = target_features([own[16:17], own[17:18], own[18:19]])
    far_root = one_target(couple(far_ids(root_index)(0), s_ref, x_ref, target, ka))

    for q in range(2):
        source_eight([pair_rows(top_points, 8 * q + 2 * p, 8 * q + 2 * p + 1) for p in range(4)], s_ref, 8 * q)

    def parent(h, _):
        total = roots[8 * h][8:16]
        for n in range(1, 8):
            total = total + roots[8 * h + n][8:16]
        total = jnp.where(h == group, jnp.zeros_like(total), total)
        put_values(x_ref, h, values_from_tile(total))
        return 0

    lax.fori_loop(0, 16, parent, 0, unroll=2)
    target = target_features(rows_of(top_points, group))
    top_far = one_target(couple(list(range(16)), s_ref, x_ref, target, ka))

    raised = lifted(top_far, root_rows[0])
    gap = jnp.zeros((16, 32), f32)
    root = far_root + take(
        jnp.concatenate([raised[:16], gap, raised[16:], gap], axis=1), evens_odds_back()
    )
    raised = lifted(root, middle_rows[...].reshape(256, 128))
    for p in range(4):
        columns = slice(128 * p, 128 * p + 128)
        far_middle[:, columns] = far_middle[:, columns] + natural(raised, p)

    def one_middle(i, _):
        pair = far_middle[:, pl.ds(pl.multiple_of(i * 128, 128), 128)]
        for half in range(2):
            at = 16 * i + 8 * half
            raised = lifted(swap(pair) if half else pair, leaf_rows[pl.ds(at, 8)].reshape(256, 128))
            for p in range(4):
                columns = pl.ds(pl.multiple_of(i * 1024 + half * 512 + 128 * p, 128), 128)
                leaf = far[:, columns] + natural(raised, p)
                a = lifted(leaf, basis_rows[at + 2 * p])
                b = lifted(swap(leaf), basis_rows[at + 2 * p + 1])
                tree[:, columns] = near[:, columns] + jnp.concatenate([a[:16], a[16:], b[:16], b[16:]], axis=1)
        return 0

    lax.fori_loop(0, 4, one_middle, 0)
    permute_columns(tree, inverse, out, False)


def from_behind(block, distance):
    devices = range(lax.axis_size(both))
    return lax.ppermute(block, both, [(i - distance, i) for i in devices if i - distance in devices])


def exchange(x):
    return lax.all_to_all(x, both, split_axis=0, concat_axis=0, tiled=True)


def shards(
    values,
    coords,
    order,
    leaf_basis,
    leaf_transfer,
    middle_transfer,
    root_transfer,
    leaf_skeleton,
    middle_skeleton,
    root_skeleton,
    top_skeleton,
    leaf_far,
    middle_far,
    root_far,
    leaf_near,
    leaf_sends,
    middle_sends,
):
    tree, first_leaves, last_leaves = call(
        tree_order,
        "tree_order",
        (shape(24, 4096), shape(24, 512), shape(24, 512)),
        [VM, VM, VM],
        [pltpu.VMEM((24, 4096), f32)],
    )(values, coords, order.reshape(32, 128))
    before = from_behind(last_leaves, 1)
    after = from_behind(first_leaves, -1)
    packed = call(
        pack_skeletons,
        "pack_skeletons",
        shape(128, 16, 128),
        [SM, SM, VM, VM],
        [pltpu.VMEM((3, 64, 128), f32), pltpu.VMEM((3, 8, 128), f32)],
    )(leaf_sends, middle_sends, leaf_skeleton, middle_skeleton)
    skeletons = exchange(packed)

    outgoing, root_out, basis_rows, leaf_rows, middle_rows, root_rows = call(
        up_pass,
        "up_pass",
        (
            shape(128, 80, 128), shape(24, 128),
            shape(64, 32, 128), shape(64, 32, 128), shape(8, 32, 128), shape(1, 32, 128),
        ),
        [SM, SM, VM, VM, HBM, HBM, HBM, HBM],
        [
            pltpu.VMEM((16, 4096), f32),
            pltpu.VMEM((64, 8, 128), f32),
            pltpu.VMEM((8, 8, 128), f32),
            pltpu.VMEM((3, 1, 128), f32),
            pltpu.SemaphoreType.DMA((4, 32)),
        ],
        flops=8 * 10**9,
    )(
        leaf_sends, middle_sends, tree, root_skeleton,
        leaf_basis, leaf_transfer, middle_transfer, root_transfer,
    )
    outgoing, before, after = lax.optimization_barrier((outgoing, before, after))
    received = exchange(outgoing)
    roots = lax.all_gather(root_out[None], both, axis=0, tiled=True)

    kernels = [pltpu.VMEM((2, 1024, 256), bf16)] * 2
    near = call(
        near_field,
        "near_field",
        shape(16, 4096),
        [SM, VM, VM, VM],
        [
            pltpu.VMEM((24, 5120), f32),
            pltpu.VMEM((88, 64, 128), bf16),
            pltpu.VMEM((81, 2, 16, 128), bf16),
            pltpu.VMEM((2, 448, 256), bf16),
            pltpu.VMEM((2, 448, 256), bf16),
        ],
        flops=22 * 10**9,
    )(leaf_near.T, before, tree, after)
    inverse = pl.pallas_call(
        invert,
        name="invert",
        out_shape=shape(4096, kind=jnp.int32),
        in_specs=[SM],
        out_specs=SM,
        cost_estimate=pl.CostEstimate(flops=6 * 10**9, bytes_accessed=0, transcendentals=0),
    )(order).reshape(32, 128)
    leaf_table, middle_table = call(
        sources,
        "sources",
        (shape(1024, 64, 128, kind=bf16), shape(256, 64, 128, kind=bf16)),
        [VM],
        flops=16 * 10**9,
    )(skeletons)
    far = call(
        far_leaves,
        "far_leaves",
        shape(16, 4096),
        [SM, VM, HBM, HBM],
        [
            pltpu.VMEM((1024, 64, 128), bf16),
            pltpu.VMEM((128, 64, 128), f32),
            pltpu.VMEM((1024, 2, 16, 128), bf16),
            pltpu.VMEM((3, 64, 128), f32),
            *kernels,
            pltpu.SemaphoreType.DMA((5,)),
        ],
        flops=50 * 10**9,
    )(leaf_far, leaf_skeleton, received, leaf_table)
    return call(
        finish,
        "finish",
        shape(16, 4096),
        [SM, SM, VM, VM, VM, VM, VM, VM, VM, VM, VM, VM, VM, VM],
        [
            pltpu.VMEM((16, 512), f32),
            pltpu.VMEM((256, 2, 16, 128), bf16),
            pltpu.VMEM((128, 64, 128), bf16),
            *kernels,
            pltpu.VMEM((3, 8, 128), f32),
            pltpu.VMEM((3, 16, 128), f32),
            pltpu.VMEM((16, 4096), f32),
        ],
        flops=10 * 10**9,
    )(
        middle_far, root_far, received[:, 64:], middle_table, roots, middle_skeleton, top_skeleton,
        near, far, basis_rows, leaf_rows, middle_rows, root_rows, inverse,
    )


def solution(mesh):
    split = P(both, None)
    placed = (
        P(None, both),
        P(None, both),
        P(both),
        split,
        split,
        split,
        split,
        split,
        split,
        split,
        P(),
        split,
        split,
        split,
        split,
        P(both),
        P(both),
    )
    return jax.shard_map(
        shards, mesh=mesh, in_specs=placed, out_specs=P(None, both), check_vma=False
    )
```

time: 295 us -> 216 us (0.73)
  Pallas kernels: 194 us -> 160 us
  local copies, waits for them, and re-layouts: 30.4 us -> 2.89 us
  starting transfers between devices: 41.1 us -> 27.2 us
  other arithmetic: 9.4 us -> 0 us
  waiting for transfers between devices: 5.27 us -> 12.3 us
    pallas_call x7 -> x6, Pallas kernels: 184 us -> 149 us  [the longest x1 54.2 us: shards(): call(far_leaves, 'far_leaves', shape(16, 4096), [SM, VM, HBM, HBM], [pltp...]
    unnamed x59 -> x6, local copies, waits for them, and re-layouts: 17.7 us -> 0.6 us
    all_to_all x3 -> x2, starting transfers between devices: 35.5 us -> 21.8 us  [exchange(): return lax.all_to_all(x, both, split_axis=0, concat_axis=0, tiled=True)]
    all_to_all x3 -> x2, waiting for transfers between devices: 0.19 us -> 11.6 us  [exchange(): return lax.all_to_all(x, both, split_axis=0, concat_axis=0, tiled=True)]
    reshape x8 -> x0, local copies, waits for them, and re-layouts: 11.1 us -> none  [the longest x4 3.57 us: paired(): rows = skeleton.reshape(-1, 3, RANK)]
    all_gather x1, waiting for transfers between devices: 5.06 us -> 0.02 us  [shards(): roots = lax.all_gather(root_out[None], both, axis=0, tiled=True)]
    unnamed x2 -> x0, other arithmetic: 3.93 us -> none
    concatenate x5 -> x0, other arithmetic: 3.88 us -> none  [the longest x3 1.73 us: paired(): return jnp.concatenate([rows, rows], axis=2)]
  transfers between devices with their start and end apart: 6 -> 5, of which waited for: 2 -> 1; matrix products, arithmetic and copies ran while one was open for 8% -> 1% of each run, Pallas kernels for 40% -> 60%
where the time goes in v2:
time: 216 us
  Pallas kernels  160 us (74%)
  starting transfers between devices  27.2 us (13%)
  between operations  13.5 us (6%)
  waiting for transfers between devices  12.3 us (6%)
  local copies, waits for them, and re-layouts  2.89 us (1%)
    pallas_call x1, Pallas kernels, shards(): call(far_leaves, 'far_leaves', shape(16, 4096), [SM, VM, HBM, HBM], [pltp...  54.2 us
    pallas_call x1, Pallas kernels, shards(): call(finish, 'finish', shape(16, 4096), [SM, SM, VM, VM, VM, VM, VM, VM,...  26.4 us
    pallas_call x1, Pallas kernels, shards(): call(near_field, 'near_field', shape(16, 4096), [SM, VM, VM, VM], [pltpu....  23.9 us
    pallas_call x1, Pallas kernels, shards(): call(sources, 'sources', (shape(1024, 64, 128, kind=bf16), shape(256, 64,...  21.9 us
    all_to_all x2, starting transfers between devices, exchange(): return lax.all_to_all(x, both, split_axis=0, concat_axis=0, tiled=True)  21.8 us
    pallas_call x1, Pallas kernels, shards(): call(up_pass, 'up_pass', (shape(128, 80, 128), shape(24, 128), shape(64,...  14.1 us
    all_to_all x2, waiting for transfers between devices, exchange(): return lax.all_to_all(x, both, split_axis=0, concat_axis=0, tiled=True)  11.6 us
    pallas_call x1, Pallas kernels, shards(): call(tree_order, 'tree_order', (shape(24, 4096), shape(24, 512), shape(24...  8.63 us
  transfers between devices with their start and end apart: 5, of which 1 were waited for; matrix products, arithmetic and copies ran while one was open for 1% of the time, Pallas kernels for 60%

profile of v2, /device:TPU:1, one launch (start us, length us, event | category | flops | bytes accessed | tf_op | source)
XLA Modules:
  0.0 215.6 jit_solution(10566706662644057643)
XLA Ops:
  6.5 4.0 %pack_skeletons.1 = f32[128,16,128]{2,1,0:T(8,128)} custom-call(s32[1024]{0:T(1024)} %sends.3, s32[256]{0:T(256)} %middle_sends.3, f32[64,192]{1,0:T(8,128)} %skeleton.1, f32[8,192]{1,0:T(8,128)} %middle_skeleton.3), custom_call_target="tpu_custom_call" | custom-call | tf_op jit(solution)/shard_map/pack_skeletons/pallas_call | solution.py:644
  10.5 11.5 %all-to-all-start.1 = ((f32[128,16,128]{2,1,0:T(8,128)}), f32[128,16,128]{2,1,0:T(8,128)S(1)}, u32[]{:S(2)}, u32[]{:S(2)}) async-start(f32[128,16,128]{2,1,0:T(8,128)} %pack_skeletons.1), calls=%async_computation.1 | async-start | bytes 2097152 | tf_op jit(solution)/shard_map/all_to_all | solution.py:613
  22.0 8.6 %tree_order.1 = (f32[24,4096]{1,0:T(8,128)}, f32[24,512]{1,0:T(8,128)}, f32[24,512]{1,0:T(8,128)}) custom-call(f32[16,4096]{1,0:T(8,128)} %values.1, f32[3,4096]{1,0:T(4,128)} %coords.1, s32[32,128]{1,0:T(8,128)} %bitcast.4), custom_call_target="tpu_custom_call" | custom-call | tf_op jit(solution)/shard_map/tree_order/pallas_call | solution.py:635
  30.6 3.5 %collective-permute-start = (f32[24,512]{1,0:T(8,128)}, f32[24,512]{1,0:T(8,128)S(1)}, u32[]{:S(2)}, u32[]{:S(2)}) collective-permute-start(f32[24,512]{1,0:T(8,128)} %get-tuple-element.21), channel_id=1, source_target_pairs={{0,1},{1,2},{2,3},{3,4},{4,5},{5,6},{6,7},{7,8},{8,9},{9,10},{10,1... | collective-permute-start | bytes 147464 | tf_op jit(solution)/shard_map/ppermute | solution.py:609
  34.2 1.9 collective-permute-start.1
  36.1 14.1 %up_pass.1 = (f32[128,80,128]{2,1,0:T(8,128)}, f32[24,128]{1,0:T(8,128)}, f32[64,32,128]{2,1,0:T(8,128)}, f32[64,32,128]{2,1,0:T(8,128)}, f32[8,32,128]{2,1,0:T(8,128)}, /*index=5*/f32[1,32,128]{2,1,0:T(8,128)}) custom-call(s32[1024]{0:T(1024)} %sends.3, s32[256]{0:T(256)} %middle_sends.3, f32[24,4096]{1,0:T(8,128)} %get-tuple-element.19.tree, ...), custom_call_target="tpu_custom_call" | custom-call | flops 8000000000 | tf_op jit(solution)/shard_map/up_pass/pallas_call | solution.py:653
  50.2 0.0 collective-permute-done.before
  50.2 0.0 collective-permute-done.1.after
  50.2 0.0 copy-start.2
  50.2 0.0 all-to-all-done.1.received
  50.3 0.6 copy-done.1
  50.8 0.0 copy-done.2
  50.9 10.3 %all-to-all-start = ((f32[128,80,128]{2,1,0:T(8,128)}), f32[128,80,128]{2,1,0:T(8,128)}, u32[]{:S(2)}, u32[]{:S(2)}) async-start(f32[128,80,128]{2,1,0:T(8,128)} %get-tuple-element.23), calls=%async_computation | async-start | bytes 10485760 | tf_op jit(solution)/shard_map/all_to_all | solution.py:613
  61.1 0.0 all-gather.3.cloned.1.call-start
  61.2 0.0 copy-done
  61.2 0.7 all-gather.3.cloned.1.call-update
  61.9 6.5 %invert.1 = s32[4096]{0:T(1024)} custom-call(s32[4096]{0:T(1024)} %order.1), custom_call_target="tpu_custom_call" | custom-call | flops 6000000000 | tf_op jit(solution)/shard_map/invert/pallas_call | solution.py:692
  68.4 23.9 %near_field.1.near = f32[16,4096]{1,0:T(8,128)} custom-call(s32[26,64]{1,0:T(8,128)} %bitcast.6, f32[24,512]{1,0:T(8,128)} %copy-done.1, f32[24,4096]{1,0:T(8,128)} %get-tuple-element.19.tree, f32[24,512]{1,0:T(8,128)} %copy-done.2), custom_call_target="tpu_custom_call" | custom-call | flops 22000001024 | tf_op jit(solution)/shard_map/near_field/pallas_call | solution.py:678
  92.3 21.9 %sources.1 = (bf16[1024,64,128]{2,1,0:T(8,128)(2,1)}, bf16[256,64,128]{2,1,0:T(8,128)(2,1)}) custom-call(f32[128,16,128]{2,1,0:T(8,128)} %copy-done), custom_call_target="tpu_custom_call" | custom-call | flops 16000000000 | tf_op jit(solution)/shard_map/sources/pallas_call | solution.py:700
  114.2 11.6 %all-to-all-done.received = f32[128,80,128]{2,1,0:T(8,128)} async-done(((f32[128,80,128]{2,1,0:T(8,128)}), f32[128,80,128]{2,1,0:T(8,128)}, u32[]{:S(2)}, u32[]{:S(2)}) %all-to-all-start) | async-done | bytes 5242912 | tf_op jit(solution)/shard_map/all_to_all | solution.py:613
  125.8 2.3 %slice.4.received = f32[128,16,128]{2,1,0:T(8,128)} slice(f32[128,80,128]{2,1,0:T(8,128)} %all-to-all-done.received), slice={[0:128], [64:80], [0:128]} | slice | bytes 2097152 | tf_op jit(solution)/shard_map/slice | solution.py:738
  128.1 54.2 %far_leaves.1.far = f32[16,4096]{1,0:T(8,128)} custom-call(s32[64,64]{1,0:T(8,128)} %index.1, f32[64,192]{1,0:T(8,128)} %skeleton.1, f32[128,80,128]{2,1,0:T(8,128)} %all-to-all-done.received, bf16[1024,64,128]{2,1,0:T(8,128)(2,1)} %get-tuple-element.28.table), custom_call_target="tpu_custom_call" | custom-call | flops 49999998976 | tf_op jit(solution)/shard_map/far_leaves/pallas_call | solution.py:707
  182.3 0.0 all-gather.3.cloned.1.call-done
  182.4 26.4 %finish.1 = f32[16,4096]{1,0:T(8,128)} custom-call(s32[8,64]{1,0:T(8,128)} %middle_index.1, s32[1,64]{1,0:T(1,128)} %root_index.1, f32[128,16,128]{2,1,0:T(8,128)} %slice.4.received, bf16[256,64,128]{2,1,0:T(8,128)(2,1)} %get-tuple-element.24.middle_table, f32[128,24,128]{2,1,0:T(8,128)} %bitcast.5, f32[8,192]{1,0:T(8,128)} %middle_skeleton.3, ...), custom_call_target="tpu_custom_call" | custom-call | flops 10000000000 | tf_op jit(solution)/shard_map/finish/pallas_call | solution.py:722
  (2 shorter events, 0.0 us)
Async XLA Ops:
  10.5 39.7 %all-to-all-start.1 = ((f32[128,16,128]{2,1,0:T(8,128)}), f32[128,16,128]{2,1,0:T(8,128)S(1)}, u32[]{:S(2)}, u32[]{:S(2)}) async-start(f32[128,16,128]{2,1,0:T(8,128)} %pack_skeletons.1), calls=%async_computation.1 | async-start | bytes 2097152 | tf_op jit(solution)/shard_map/all_to_all | solution.py:613
  30.6 19.6 %collective-permute-start = (f32[24,512]{1,0:T(8,128)}, f32[24,512]{1,0:T(8,128)S(1)}, u32[]{:S(2)}, u32[]{:S(2)}) collective-permute-start(f32[24,512]{1,0:T(8,128)} %get-tuple-element.21), channel_id=1, source_target_pairs={{0,1},{1,2},{2,3},{3,4},{4,5},{5,6},{6,7},{7,8},{8,9},{9,10},{10,1... | collective-permute-start | bytes 147464 | tf_op jit(solution)/shard_map/ppermute | solution.py:609
  34.2 16.1 %collective-permute-start.1 = (f32[24,512]{1,0:T(8,128)}, f32[24,512]{1,0:T(8,128)S(1)}, u32[]{:S(2)}, u32[]{:S(2)}) collective-permute-start(f32[24,512]{1,0:T(8,128)} %get-tuple-element.22), channel_id=1, source_target_pairs={{1,0},{2,1},{3,2},{4,3},{5,4},{6,5},{7,6},{8,7},{9,8},{10,9},{11,1... | collective-permute-start | bytes 147464 | tf_op jit(solution)/shard_map/ppermute | solution.py:609
  50.2 0.6 copy-start.1
  50.2 0.6 copy-start.2
  50.3 10.9 %copy-start = (f32[128,16,128]{2,1,0:T(8,128)}, f32[128,16,128]{2,1,0:T(8,128)S(1)}, u32[]{:S(2)}) copy-start(f32[128,16,128]{2,1,0:T(8,128)S(1)} %all-to-all-done.1.received) | copy-start | bytes 3145732
  50.9 75.0 %all-to-all-start = ((f32[128,80,128]{2,1,0:T(8,128)}), f32[128,80,128]{2,1,0:T(8,128)}, u32[]{:S(2)}, u32[]{:S(2)}) async-start(f32[128,80,128]{2,1,0:T(8,128)} %get-tuple-element.23), calls=%async_computation | async-start | bytes 10485760 | tf_op jit(solution)/shard_map/all_to_all | solution.py:613
  61.1 121.2 %all-gather.3.cloned.1.call-start = ((), (), s32[]{:S(2)}) async-start(), calls=%async_computation.2 | async-start | bytes 1585152 | tf_op jit(solution)/shard_map/all_gather | solution.py:675
Sparse Core Ops, SparseCore 0:
  64.8 101.8 all-gather.2

commit v3 on v2

--- a/solution.py
+++ b/solution.py
@@ -187,13 +187,18 @@
     )
 
 
-def couple(ids, s_ref, x_ref, target, k_ref):
-    spread = spread_target(target)
-    total = None
-    for q in range(0, len(ids) // COLS, 4):
-        make_kernel(ids, q, s_ref, spread, k_ref)
-        total = apply_kernel(ids, q, x_ref, k_ref, total)
-    return summed(total)
+def couple(parts, s_ref, x_ref, k_refs):
+    for (ids, target), k_ref in zip(parts, k_refs):
+        spread = spread_target(target)
+        for q in range(0, len(ids) // COLS, 4):
+            make_kernel(ids, q, s_ref, spread, k_ref)
+    sums = []
+    for (ids, _), k_ref in zip(parts, k_refs):
+        total = None
+        for q in range(0, len(ids) // COLS, 4):
+            total = apply_kernel(ids, q, x_ref, k_ref, total)
+        sums.append(one_target(summed(total)))
+    return sums
 
 
 def couple_all(count, ids, target, s_ref, x_ref, out, ka, kb, unroll=1):
@@ -234,13 +239,13 @@
 HBM = pl.BlockSpec(memory_space=pl.ANY)
 
 
-def call(kernel, name, out, in_specs, scratch=(), flops=0, data=0, limit=60):
+def call(kernel, name, out, in_specs, scratch=(), flops=0, data=0, limit=60, outs=None):
     return pl.pallas_call(
         kernel,
         name=name,
         out_shape=out,
         in_specs=in_specs,
-        out_specs=jax.tree.map(lambda _: VM, out),
+        out_specs=jax.tree.map(lambda _: VM, out) if outs is None else outs,
         scratch_shapes=list(scratch),
         cost_estimate=pl.CostEstimate(flops=flops, bytes_accessed=data, transcendentals=0),
         compiler_params=pltpu.CompilerParams(vmem_limit_bytes=limit * 2**20),
@@ -268,17 +273,38 @@
     return [jnp.where(left, x, y) for x, y in zip(rows_of(table, a), rows_of(table, b))]
 
 
-def pack_skeletons(sends, middle_sends, leaf_skeleton, middle_skeleton, out, leaf_table, middle_table):
+PAIR_ROWS = (0, 3, 8, 11)
+MIDDLE_ROWS = (6, 7, 14)
+
+
+def pack_skeletons(
+    sends, middle_sends, leaf_skeleton, middle_skeleton,
+    out, leaf_table, middle_table, early, late, middles, lasts,
+):
     put_rows(leaf_skeleton, leaf_table)
     put_rows(middle_skeleton, middle_table)
 
+    def spot(l, _):
+        tile = jnp.concatenate(rows_of(leaf_table, l) + [jnp.zeros((5, 128), f32)], axis=0)
+        early[l] = tile
+        late[l] = pltpu.roll(tile, 3, axis=0)
+        return 0
+
+    lax.fori_loop(0, 64, spot, 0, unroll=4)
+    for m in range(8):
+        x, y, z = rows_of(middle_table, m)
+        middles[m] = jnp.concatenate([jnp.zeros((6, 128), f32), x, y], axis=0)
+        lasts[m] = jnp.concatenate([jnp.zeros((6, 128), f32), z, jnp.zeros((1, 128), f32)], axis=0)
+    left = lanes((8, 128)) < 64
+
     def body(b, _):
-        rows = []
-        for p in range(4):
-            rows += pair_rows(leaf_table, sends[b * 8 + 2 * p], sends[b * 8 + 2 * p + 1])
-        rows += pair_rows(middle_table, middle_sends[2 * b], middle_sends[2 * b + 1])
-        rows.append(jnp.zeros((1, 128), f32))
-        out[b] = jnp.concatenate(rows, axis=0)
+        slot = [sends[b * 8 + c] for c in range(8)]
+        m, n = middle_sends[2 * b], middle_sends[2 * b + 1]
+        for half, third in ((0, middles), (1, lasts)):
+            c = 4 * half
+            first = early[slot[c]] + late[slot[c + 2]] + third[m]
+            second = early[slot[c + 1]] + late[slot[c + 3]] + third[n]
+            out[b, 8 * half : 8 * half + 8] = jnp.where(left, first, second)
         return 0
 
     lax.fori_loop(0, 128, body, 0, unroll=4)
@@ -307,7 +333,7 @@
     return ((i & 1) << 6) + ((i >> 6) << 5) + ((i & 63) >> 1)
 
 
-def permute_columns(source, index, out, halved):
+def permute_columns(source, index, out, halved, tiles=(0, 32), shift=0):
     height = source.shape[0] // 8
 
     def body(j, _):
@@ -323,10 +349,10 @@
                 piece = source[8 * r : 8 * r + 8, 128 * i : 128 * i + 128]
                 found[r] = jnp.where(match, take(piece, inside), found[r])
         for r in range(height):
-            out[8 * r : 8 * r + 8, pl.ds(pl.multiple_of(j * 128, 128), 128)] = found[r]
-        return 0
-
-    lax.fori_loop(0, 32, body, 0, unroll=2)
+            out[8 * r : 8 * r + 8, pl.ds(pl.multiple_of((j + shift) * 128, 128), 128)] = found[r]
+        return 0
+
+    lax.fori_loop(*tiles, body, 0, unroll=2)
 
 
 def pair_halves(result):
@@ -351,19 +377,24 @@
     return jnp.concatenate([jnp.concatenate(even, axis=1), jnp.concatenate(odd, axis=1)], axis=0)
 
 
+def pad_points(coords, source):
+    source[0:3] = coords[...]
+    source[3:8] = jnp.zeros((5, 4096), f32)
+
+
 def tree_order(values, coords, order, tree, first_leaves, last_leaves, source):
-    source[0:16] = values[...]
-    source[16:19] = coords[...]
-    source[19:24] = jnp.zeros((5, 4096), f32)
-    permute_columns(source, order, tree, True)
-    first_leaves[...] = tree[:, :512]
-    last_leaves[...] = tree[:, 3584:]
+    pad_points(coords, source)
+    permute_columns(values, order, tree, True)
+    permute_columns(source, order, first_leaves.at[16:24], True, (0, 4))
+    permute_columns(source, order, last_leaves.at[16:24], True, (28, 32), -28)
+    first_leaves[0:16] = tree[:, :512]
+    last_leaves[0:16] = tree[:, 3584:]
 
 
 def up_pass(
     sends, middle_sends, tree, root_skeleton, basis, leaf_maps, middle_maps, root_maps,
     out, root_out, basis_rows, leaf_rows, middle_rows, root_rows,
-    split, tiles, middle_tiles, root_table, sems,
+    message, split, tiles, middle_tiles, root_table, sems, out_sems,
 ):
     copies = []
     for m, (whole, rows) in enumerate(
@@ -383,7 +414,7 @@
 
     def leaf_pair(i, _):
         columns = pl.ds(pl.multiple_of(i * 128, 128), 128)
-        x = tree[0:16, columns]
+        x = tree[:, columns]
         a = pair_halves(dot3(jnp.concatenate([x[:, :32], x[:, 32:64]], axis=0), basis_rows[2 * i]))
         b = pair_halves(dot3(jnp.concatenate([x[:, 64:96], x[:, 96:]], axis=0), basis_rows[2 * i + 1]))
         split[:, columns] = take(side_by_side(a, b), evens_odds())
@@ -395,10 +426,15 @@
 
     def slots(b, _):
         for c in range(8):
-            out[b, 8 * c : 8 * c + 8] = tiles[sends[8 * b + c]]
-        return 0
-
-    lax.fori_loop(0, 128, slots, 0, unroll=2)
+            message[b, 8 * c : 8 * c + 8] = tiles[sends[8 * b + c]]
+        return 0
+
+    sent = []
+    for p in range(4):
+        lax.fori_loop(32 * p, 32 * p + 32, slots, 0, unroll=2)
+        part = (pl.ds(32 * p, 32), pl.ds(0, 64))
+        sent.append(pltpu.make_async_copy(message.at[part], out.at[part], out_sems.at[p]))
+        sent[-1].start()
     for group in copies[1:]:
         for copy in group:
             copy.wait()
@@ -419,10 +455,15 @@
 
     def middle_slots(b, _):
         for c in range(2):
-            out[b, 64 + 8 * c : 72 + 8 * c] = middle_tiles[middle_sends[2 * b + c]]
+            message[b, 64 + 8 * c : 72 + 8 * c] = middle_tiles[middle_sends[2 * b + c]]
         return 0
 
     lax.fori_loop(0, 128, middle_slots, 0, unroll=4)
+    part = (pl.ds(0, 128), pl.ds(64, 16))
+    sent.append(pltpu.make_async_copy(message.at[part], out.at[part], out_sems.at[4]))
+    sent[-1].start()
+    for copy in sent:
+        copy.wait()
 
 
 def invert(order, inverse):
@@ -434,10 +475,12 @@
     lax.fori_loop(0, 64, body, 0)
 
 
-def near_field(index, before, tree, after, out, window, s_ref, x_ref, ka, kb):
+def near_field(index, before, tree, after, coords, order, out, window, source, s_ref, x_ref, ka, kb):
     window[:, :512] = before[...]
-    window[:, 512:4608] = tree[...]
+    window[0:16, 512:4608] = tree[...]
     window[:, 4608:] = after[...]
+    pad_points(coords, source)
+    permute_columns(source, order, window.at[16:24], True, (0, 32), 4)
     for k in range(8):
         s_ref[80 + k] = jnp.zeros((64, 128), bf16)
     x_ref[80] = jnp.zeros((2, 16, 128), bf16)
@@ -469,14 +512,14 @@
 def sources(received, s_ref, middle_ref):
     def prepare(q, _):
         block = received[q]
-        source_eight([[block[3 * p + j : 3 * p + j + 1] for j in range(3)] for p in range(4)], s_ref, q * 8)
+        source_eight([[block[r + j : r + j + 1] for j in range(3)] for r in PAIR_ROWS], s_ref, q * 8)
         return 0
 
     lax.fori_loop(0, 128, prepare, 0, unroll=4)
 
     def middle(q, _):
         source_eight(
-            [[received[4 * q + p, 12 + j : 13 + j] for j in range(3)] for p in range(4)], middle_ref, q * 8
+            [[received[4 * q + p, r : r + 1] for r in MIDDLE_ROWS] for p in range(4)], middle_ref, q * 8
         )
         return 0
 
@@ -507,10 +550,10 @@
                 put_values(x_ref, 8 * q + c, values_from_tile(tiles[q, 8 * c : 8 * c + 8]))
             return 0
 
-        lax.fori_loop(32 * p, 32 * p + 32, prepare, 0)
+        lax.fori_loop(32 * p, 32 * p + 32, prepare, 0, unroll=2)
     loaded.wait()
     couple_all(
-        64, far_ids(index), lambda l: target_features(rows_of(rows, l)), s_ref, x_ref, out, ka, kb
+        64, far_ids(index), lambda l: target_features(rows_of(rows, l)), s_ref, x_ref, out, ka, kb, 2
     )
 
 
@@ -527,25 +570,43 @@
 
 
 def finish(
-    middle_index, root_index, received, middle_table, roots, middle_skeleton, top_skeleton,
-    near, far, basis_rows, leaf_rows, middle_rows, root_rows, inverse,
-    out, far_middle, x_ref, s_ref, ka, kb, middle_points, top_points, tree,
+    middle_index, root_index, received, middle_table_far, roots_far, middle_skeleton, top_skeleton,
+    near, far, basis_far, leaf_far, middle_rows, root_rows, inverse,
+    out, far_middle, values, middle_table, roots, basis_rows, leaf_rows,
+    x_ref, s_ref, ka, kb, middle_points, top_points, tree, sems,
 ):
+    loads = [
+        pltpu.make_async_copy(source, target, sems.at[i])
+        for i, (source, target) in enumerate(
+            (
+                (received.at[pl.ds(0, 128), pl.ds(64, 16)], values),
+                (middle_table_far, middle_table),
+                (roots_far, roots),
+                (leaf_far, leaf_rows),
+                (basis_far, basis_rows),
+            )
+        )
+    ]
+    for load in loads:
+        load.start()
     left = lanes((1, 128)) < 64
     put_rows(middle_skeleton, middle_points)
     put_rows(top_skeleton, top_points)
     group = lax.axis_index("gx")
+    loads[0].wait()
 
     def middle_values(q, _):
         for c in range(2):
-            put_values(x_ref, 2 * q + c, values_from_tile(received[q, 8 * c : 8 * c + 8]))
+            put_values(x_ref, 2 * q + c, values_from_tile(values[q, 8 * c : 8 * c + 8]))
         return 0
 
     lax.fori_loop(0, 128, middle_values, 0, unroll=4)
+    loads[1].wait()
     couple_all(
         8, far_ids(middle_index), lambda l: target_features(rows_of(middle_points, l)),
         middle_table, x_ref, far_middle, ka, kb,
     )
+    loads[2].wait()
 
     def root_sources(q, _):
         pairs = []
@@ -557,25 +618,33 @@
         source_eight(pairs, s_ref, 8 * q)
         return 0
 
-    lax.fori_loop(0, 16, root_sources, 0, unroll=2)
-    own = roots[lax.axis_index(both)]
-    target = target_features([own[16:17], own[17:18], own[18:19]])
-    far_root = one_target(couple(far_ids(root_index)(0), s_ref, x_ref, target, ka))
-
+    lax.fori_loop(0, 16, root_sources, 0, unroll=4)
     for q in range(2):
-        source_eight([pair_rows(top_points, 8 * q + 2 * p, 8 * q + 2 * p + 1) for p in range(4)], s_ref, 8 * q)
+        source_eight(
+            [pair_rows(top_points, 8 * q + 2 * p, 8 * q + 2 * p + 1) for p in range(4)], s_ref, 128 + 8 * q
+        )
 
     def parent(h, _):
         total = roots[8 * h][8:16]
         for n in range(1, 8):
             total = total + roots[8 * h + n][8:16]
         total = jnp.where(h == group, jnp.zeros_like(total), total)
-        put_values(x_ref, h, values_from_tile(total))
-        return 0
-
-    lax.fori_loop(0, 16, parent, 0, unroll=2)
-    target = target_features(rows_of(top_points, group))
-    top_far = one_target(couple(list(range(16)), s_ref, x_ref, target, ka))
+        put_values(x_ref, 128 + h, values_from_tile(total))
+        return 0
+
+    lax.fori_loop(0, 16, parent, 0, unroll=4)
+    own = roots[lax.axis_index(both)]
+    far_root, top_far = couple(
+        [
+            (far_ids(root_index)(0), target_features([own[16:17], own[17:18], own[18:19]])),
+            (list(range(128, 144)), target_features(rows_of(top_points, group))),
+        ],
+        s_ref,
+        x_ref,
+        (ka, kb),
+    )
+    loads[3].wait()
+    loads[4].wait()
 
     raised = lifted(top_far, root_rows[0])
     gap = jnp.zeros((16, 32), f32)
@@ -600,7 +669,7 @@
                 tree[:, columns] = near[:, columns] + jnp.concatenate([a[:16], a[16:], b[:16], b[16:]], axis=1)
         return 0
 
-    lax.fori_loop(0, 4, one_middle, 0)
+    lax.fori_loop(0, 4, one_middle, 0, unroll=2)
     permute_columns(tree, inverse, out, False)
 
 
@@ -632,13 +701,14 @@
     leaf_sends,
     middle_sends,
 ):
+    order_rows = order.reshape(32, 128)
     tree, first_leaves, last_leaves = call(
         tree_order,
         "tree_order",
-        (shape(24, 4096), shape(24, 512), shape(24, 512)),
+        (shape(16, 4096), shape(24, 512), shape(24, 512)),
         [VM, VM, VM],
-        [pltpu.VMEM((24, 4096), f32)],
-    )(values, coords, order.reshape(32, 128))
+        [pltpu.VMEM((8, 4096), f32)],
+    )(values, coords, order_rows)
     before = from_behind(last_leaves, 1)
     after = from_behind(first_leaves, -1)
     packed = call(
@@ -646,7 +716,14 @@
         "pack_skeletons",
         shape(128, 16, 128),
         [SM, SM, VM, VM],
-        [pltpu.VMEM((3, 64, 128), f32), pltpu.VMEM((3, 8, 128), f32)],
+        [
+            pltpu.VMEM((3, 64, 128), f32),
+            pltpu.VMEM((3, 8, 128), f32),
+            pltpu.VMEM((64, 8, 128), f32),
+            pltpu.VMEM((64, 8, 128), f32),
+            pltpu.VMEM((8, 8, 128), f32),
+            pltpu.VMEM((8, 8, 128), f32),
+        ],
     )(leaf_sends, middle_sends, leaf_skeleton, middle_skeleton)
     skeletons = exchange(packed)
 
@@ -659,13 +736,16 @@
         ),
         [SM, SM, VM, VM, HBM, HBM, HBM, HBM],
         [
+            pltpu.VMEM((128, 80, 128), f32),
             pltpu.VMEM((16, 4096), f32),
             pltpu.VMEM((64, 8, 128), f32),
             pltpu.VMEM((8, 8, 128), f32),
             pltpu.VMEM((3, 1, 128), f32),
             pltpu.SemaphoreType.DMA((4, 32)),
+            pltpu.SemaphoreType.DMA((5,)),
         ],
         flops=8 * 10**9,
+        outs=(HBM, VM, VM, VM, VM, VM),
     )(
         leaf_sends, middle_sends, tree, root_skeleton,
         leaf_basis, leaf_transfer, middle_transfer, root_transfer,
@@ -679,16 +759,17 @@
         near_field,
         "near_field",
         shape(16, 4096),
-        [SM, VM, VM, VM],
+        [SM, VM, VM, VM, VM, VM],
         [
             pltpu.VMEM((24, 5120), f32),
+            pltpu.VMEM((8, 4096), f32),
             pltpu.VMEM((88, 64, 128), bf16),
             pltpu.VMEM((81, 2, 16, 128), bf16),
             pltpu.VMEM((2, 448, 256), bf16),
             pltpu.VMEM((2, 448, 256), bf16),
         ],
         flops=22 * 10**9,
-    )(leaf_near.T, before, tree, after)
+    )(leaf_near.T, before, tree, after, coords, order_rows)
     inverse = pl.pallas_call(
         invert,
         name="invert",
@@ -723,19 +804,25 @@
         finish,
         "finish",
         shape(16, 4096),
-        [SM, SM, VM, VM, VM, VM, VM, VM, VM, VM, VM, VM, VM, VM],
+        [SM, SM, HBM, HBM, HBM, VM, VM, VM, VM, HBM, HBM, VM, VM, VM],
         [
             pltpu.VMEM((16, 512), f32),
+            pltpu.VMEM((128, 16, 128), f32),
+            pltpu.VMEM((256, 64, 128), bf16),
+            pltpu.VMEM((128, 24, 128), f32),
+            pltpu.VMEM((64, 32, 128), f32),
+            pltpu.VMEM((64, 32, 128), f32),
             pltpu.VMEM((256, 2, 16, 128), bf16),
-            pltpu.VMEM((128, 64, 128), bf16),
+            pltpu.VMEM((144, 64, 128), bf16),
             *kernels,
             pltpu.VMEM((3, 8, 128), f32),
             pltpu.VMEM((3, 16, 128), f32),
             pltpu.VMEM((16, 4096), f32),
+            pltpu.SemaphoreType.DMA((5,)),
         ],
         flops=10 * 10**9,
     )(
-        middle_far, root_far, received[:, 64:], middle_table, roots, middle_skeleton, top_skeleton,
+        middle_far, root_far, received, middle_table, roots, middle_skeleton, top_skeleton,
         near, far, basis_rows, leaf_rows, middle_rows, root_rows, inverse,
     )
 

time: 216 us -> 201 us (0.931)
  Pallas kernels: 160 us -> 150 us
  waiting for transfers between devices: 12.3 us -> 8.64 us
  local copies, waits for them, and re-layouts: 2.89 us -> 0.6 us
    pallas_call x1, Pallas kernels: 54.2 us -> 47.5 us  [shards(): call(far_leaves, 'far_leaves', shape(16, 4096), [SM, VM, HBM, HBM], [pltp...]
    all_to_all x2, waiting for transfers between devices: 11.6 us -> 8.12 us  [exchange(): return lax.all_to_all(x, both, split_axis=0, concat_axis=0, tiled=True)]
    slice x1 -> x0, local copies, waits for them, and re-layouts: 2.29 us -> none  [shards(): received[:, 64:]]
  transfers between devices with their start and end apart: 5 -> 5, of which waited for: 1 -> 1; matrix products, arithmetic and copies ran while one was open for 1% -> 0% of each run, Pallas kernels for 60% -> 62%
where the time goes in v3:
time: 201 us; the launch traced here: 200 us
  Pallas kernels  150 us (75%)
  starting transfers between devices  27.4 us (14%)
  between operations  13.5 us (7%)
  waiting for transfers between devices  8.64 us (4%)
    pallas_call x1, Pallas kernels, shards(): call(far_leaves, 'far_leaves', shape(16, 4096), [SM, VM, HBM, HBM], [pltp...  47.5 us
    pallas_call x1, Pallas kernels, shards(): call(near_field, 'near_field', shape(16, 4096), [SM, VM, VM, VM, VM, VM],...  27.4 us
    pallas_call x1, Pallas kernels, shards(): call(finish, 'finish', shape(16, 4096), [SM, SM, HBM, HBM, HBM, VM, VM, V...  22.6 us
    pallas_call x1, Pallas kernels, shards(): call(sources, 'sources', (shape(1024, 64, 128, kind=bf16), shape(256, 64,...  21.9 us
    all_to_all x2, starting transfers between devices, exchange(): return lax.all_to_all(x, both, split_axis=0, concat_axis=0, tiled=True)  21.8 us
    pallas_call x1, Pallas kernels, shards(): call(up_pass, 'up_pass', (shape(128, 80, 128), shape(24, 128), shape(64,...  13.5 us
    all_to_all x2, waiting for transfers between devices, exchange(): return lax.all_to_all(x, both, split_axis=0, concat_axis=0, tiled=True)  8.12 us
    pallas_call x1, Pallas kernels, shards(): call(tree_order, 'tree_order', (shape(16, 4096), shape(24, 512), shape(24...  7.11 us
  transfers between devices with their start and end apart: 5, of which 1 were waited for; matrix products, arithmetic and copies ran while one was open for 0% of the time, Pallas kernels for 62%

profile of v3, /device:TPU:1, one launch (start us, length us, event | category | flops | bytes accessed | tf_op | source)
XLA Modules:
  0.0 200.4 jit_solution(823671690788561748)
XLA Ops:
  6.5 3.7 %pack_skeletons.1 = f32[128,16,128]{2,1,0:T(8,128)} custom-call(s32[1024]{0:T(1024)} %sends.3, s32[256]{0:T(256)} %middle_sends.3, f32[64,192]{1,0:T(8,128)} %skeleton.1, f32[8,192]{1,0:T(8,128)} %middle_skeleton.3), custom_call_target="tpu_custom_call" | custom-call | tf_op jit(solution)/shard_map/pack_skeletons/pallas_call | solution.py:714
  10.2 11.5 %all-to-all-start.1 = ((f32[128,16,128]{2,1,0:T(8,128)}), f32[128,16,128]{2,1,0:T(8,128)S(1)}, u32[]{:S(2)}, u32[]{:S(2)}) async-start(f32[128,16,128]{2,1,0:T(8,128)} %pack_skeletons.1), calls=%async_computation.1 | async-start | bytes 2097152 | tf_op jit(solution)/shard_map/all_to_all | solution.py:682
  21.7 7.1 %tree_order.1 = (f32[16,4096]{1,0:T(8,128)}, f32[24,512]{1,0:T(8,128)}, f32[24,512]{1,0:T(8,128)}) custom-call(f32[16,4096]{1,0:T(8,128)} %values.1, f32[3,4096]{1,0:T(4,128)} %coords.3, s32[32,128]{1,0:T(8,128)} %bitcast.4), custom_call_target="tpu_custom_call" | custom-call | tf_op jit(solution)/shard_map/tree_order/pallas_call | solution.py:705
  28.9 3.5 %collective-permute-start = (f32[24,512]{1,0:T(8,128)}, f32[24,512]{1,0:T(8,128)S(1)}, u32[]{:S(2)}, u32[]{:S(2)}) collective-permute-start(f32[24,512]{1,0:T(8,128)} %get-tuple-element.21), channel_id=1, source_target_pairs={{0,1},{1,2},{2,3},{3,4},{4,5},{5,6},{6,7},{7,8},{8,9},{9,10},{10,1... | collective-permute-start | bytes 147464 | tf_op jit(solution)/shard_map/ppermute | solution.py:678
  32.4 1.9 collective-permute-start.1
  34.3 13.5 %up_pass.1 = (f32[128,80,128]{2,1,0:T(8,128)}, f32[24,128]{1,0:T(8,128)}, f32[64,32,128]{2,1,0:T(8,128)}, f32[64,32,128]{2,1,0:T(8,128)}, f32[8,32,128]{2,1,0:T(8,128)}, /*index=5*/f32[1,32,128]{2,1,0:T(8,128)}) custom-call(s32[1024]{0:T(1024)} %sends.3, s32[256]{0:T(256)} %middle_sends.3, f32[16,4096]{1,0:T(8,128)} %get-tuple-element.19.tree, ...), custom_call_target="tpu_custom_call" | custom-call | flops 8000000000 | tf_op jit(solution)/shard_map/up_pass/pallas_call | solution.py:730
  47.8 0.0 collective-permute-done.before
  47.8 0.0 copy-start.1
  47.9 0.0 collective-permute-done.1.after
  47.9 0.0 copy-start.2
  47.9 0.0 all-to-all-done.1.received
  47.9 0.0 copy-start
  47.9 0.6 copy-done.1
  48.5 0.0 copy-done.2
  48.5 10.3 %all-to-all-start = ((f32[128,80,128]{2,1,0:T(8,128)}), f32[128,80,128]{2,1,0:T(8,128)}, u32[]{:S(2)}, u32[]{:S(2)}) async-start(f32[128,80,128]{2,1,0:T(8,128)} %get-tuple-element.23), calls=%async_computation | async-start | bytes 10485760 | tf_op jit(solution)/shard_map/all_to_all | solution.py:682
  58.8 0.2 all-gather.3.cloned.1.call-start
  59.0 0.5 all-gather.3.cloned.1.call-update
  59.5 6.5 %invert.1 = s32[4096]{0:T(1024)} custom-call(s32[4096]{0:T(1024)} %order.1), custom_call_target="tpu_custom_call" | custom-call | flops 6000000000 | tf_op jit(solution)/shard_map/invert/pallas_call | solution.py:773
  66.0 27.4 %near_field.1.near = f32[16,4096]{1,0:T(8,128)} custom-call(s32[26,64]{1,0:T(8,128)} %bitcast.7, f32[24,512]{1,0:T(8,128)} %copy-done.1, f32[16,4096]{1,0:T(8,128)} %get-tuple-element.19.tree, f32[24,512]{1,0:T(8,128)} %copy-done.2, f32[3,4096]{1,0:T(4,128)} %coords.3, s32[32,128]{1,0:T(8,128)} %bitcast.5), custom_call_target="tpu_custom_call" | custom-call | flops 22000001024 | tf_op jit(solution)/shard_map/near_field/pallas_call | solution.py:758
  93.4 21.9 %sources.1 = (bf16[1024,64,128]{2,1,0:T(8,128)(2,1)}, bf16[256,64,128]{2,1,0:T(8,128)(2,1)}) custom-call(f32[128,16,128]{2,1,0:T(8,128)} %copy-done), custom_call_target="tpu_custom_call" | custom-call | flops 16000000000 | tf_op jit(solution)/shard_map/sources/pallas_call | solution.py:781
  115.3 8.1 %all-to-all-done.received = f32[128,80,128]{2,1,0:T(8,128)} async-done(((f32[128,80,128]{2,1,0:T(8,128)}), f32[128,80,128]{2,1,0:T(8,128)}, u32[]{:S(2)}, u32[]{:S(2)}) %all-to-all-start) | async-done | bytes 5242912 | tf_op jit(solution)/shard_map/all_to_all | solution.py:682
  123.4 47.5 %far_leaves.1.far = f32[16,4096]{1,0:T(8,128)} custom-call(s32[64,64]{1,0:T(8,128)} %index.1, f32[64,192]{1,0:T(8,128)} %skeleton.1, f32[128,80,128]{2,1,0:T(8,128)} %all-to-all-done.received, bf16[1024,64,128]{2,1,0:T(8,128)(2,1)} %get-tuple-element.28.table), custom_call_target="tpu_custom_call" | custom-call | flops 49999998976 | tf_op jit(solution)/shard_map/far_leaves/pallas_call | solution.py:788
  171.0 0.0 all-gather.3.cloned.1.call-done
  171.0 22.6 %finish.1 = f32[16,4096]{1,0:T(8,128)} custom-call(s32[8,64]{1,0:T(8,128)} %middle_index.1, s32[1,64]{1,0:T(1,128)} %root_index.1, f32[128,80,128]{2,1,0:T(8,128)} %all-to-all-done.received, bf16[256,64,128]{2,1,0:T(8,128)(2,1)} %get-tuple-element.24.middle_table_far, f32[128,24,128]{2,1,0:T(8,128)} %bitcast.6, f32[8,192]{1,0:T(8,128)} %middle_skeleton.3, ...), custom_call_target="tpu_custom_call" | custom-call | flops 10000000000 | tf_op jit(solution)/shard_map/finish/pallas_call | solution.py:803
  (1 shorter events, 0.0 us)
Async XLA Ops:
  10.2 37.6 %all-to-all-start.1 = ((f32[128,16,128]{2,1,0:T(8,128)}), f32[128,16,128]{2,1,0:T(8,128)S(1)}, u32[]{:S(2)}, u32[]{:S(2)}) async-start(f32[128,16,128]{2,1,0:T(8,128)} %pack_skeletons.1), calls=%async_computation.1 | async-start | bytes 2097152 | tf_op jit(solution)/shard_map/all_to_all | solution.py:682
  28.9 19.0 %collective-permute-start = (f32[24,512]{1,0:T(8,128)}, f32[24,512]{1,0:T(8,128)S(1)}, u32[]{:S(2)}, u32[]{:S(2)}) collective-permute-start(f32[24,512]{1,0:T(8,128)} %get-tuple-element.21), channel_id=1, source_target_pairs={{0,1},{1,2},{2,3},{3,4},{4,5},{5,6},{6,7},{7,8},{8,9},{9,10},{10,1... | collective-permute-start | bytes 147464 | tf_op jit(solution)/shard_map/ppermute | solution.py:678
  32.4 15.5 %collective-permute-start.1 = (f32[24,512]{1,0:T(8,128)}, f32[24,512]{1,0:T(8,128)S(1)}, u32[]{:S(2)}, u32[]{:S(2)}) collective-permute-start(f32[24,512]{1,0:T(8,128)} %get-tuple-element.22), channel_id=1, source_target_pairs={{1,0},{2,1},{3,2},{4,3},{5,4},{6,5},{7,6},{8,7},{9,8},{10,9},{11,1... | collective-permute-start | bytes 147464 | tf_op jit(solution)/shard_map/ppermute | solution.py:678
  47.8 0.6 copy-start.1
  47.9 0.6 copy-start.2
  47.9 11.1 %copy-start = (f32[128,16,128]{2,1,0:T(8,128)}, f32[128,16,128]{2,1,0:T(8,128)S(1)}, u32[]{:S(2)}) copy-start(f32[128,16,128]{2,1,0:T(8,128)S(1)} %all-to-all-done.1.received) | copy-start | bytes 3145732
  48.5 75.0 %all-to-all-start = ((f32[128,80,128]{2,1,0:T(8,128)}), f32[128,80,128]{2,1,0:T(8,128)}, u32[]{:S(2)}, u32[]{:S(2)}) async-start(f32[128,80,128]{2,1,0:T(8,128)} %get-tuple-element.23), calls=%async_computation | async-start | bytes 10485760 | tf_op jit(solution)/shard_map/all_to_all | solution.py:682
  58.8 112.2 %all-gather.3.cloned.1.call-start = ((), (), s32[]{:S(2)}) async-start(), calls=%async_computation.2 | async-start | bytes 1585152 | tf_op jit(solution)/shard_map/all_gather | solution.py:755
Sparse Core Ops, SparseCore 0:
  62.4 101.6 all-gather.2

commit v4 on v3

--- a/solution.py
+++ b/solution.py
@@ -201,7 +201,7 @@
     return sums
 
 
-def couple_all(count, ids, target, s_ref, x_ref, out, ka, kb, unroll=1):
+def couple_all(count, ids, target, s_ref, x_ref, out, ka, kb, unroll=1, beside=None):
     def advance(new, k_new, old, k_old):
         made, used = ids(new), ids(old)
         spread = spread_target(target(new))
@@ -217,6 +217,8 @@
         make_kernel(first, q, s_ref, spread, ka)
 
     def pair(i, _):
+        if beside is not None:
+            beside(i)
         lower = advance(2 * i + 1, kb, 2 * i, ka)
         upper = advance(jnp.minimum(2 * i + 2, count - 1), ka, 2 * i + 1, kb)
         out[:, pl.ds(pl.multiple_of(i * 128, 128), 128)] = two_targets(lower, upper)
@@ -382,35 +384,36 @@
     source[3:8] = jnp.zeros((5, 4096), f32)
 
 
-def tree_order(values, coords, order, tree, first_leaves, last_leaves, source):
+def tree_order(
+    values, coords, order, basis, leaf_maps, middle_maps, root_maps,
+    tree, first_leaves, last_leaves, basis_rows, leaf_rows, middle_rows, root_rows, source, sems,
+):
+    copies = []
+    for m, (whole, rows) in enumerate(
+        ((basis, basis_rows), (leaf_maps, leaf_rows), (middle_maps, middle_rows), (root_maps, root_rows))
+    ):
+        copies += [
+            pltpu.make_async_copy(whole.at[:, pl.ds(128 * t, 128)], rows.at[:, t, :], sems.at[m, t])
+            for t in range(32)
+        ]
+    for copy in copies:
+        copy.start()
     pad_points(coords, source)
     permute_columns(values, order, tree, True)
     permute_columns(source, order, first_leaves.at[16:24], True, (0, 4))
     permute_columns(source, order, last_leaves.at[16:24], True, (28, 32), -28)
     first_leaves[0:16] = tree[:, :512]
     last_leaves[0:16] = tree[:, 3584:]
+    for copy in copies:
+        copy.wait()
 
 
 def up_pass(
-    sends, middle_sends, tree, root_skeleton, basis, leaf_maps, middle_maps, root_maps,
-    out, root_out, basis_rows, leaf_rows, middle_rows, root_rows,
-    message, split, tiles, middle_tiles, root_table, sems, out_sems,
+    sends, middle_sends, tree, root_skeleton, basis_rows, leaf_far, middle_rows, root_rows,
+    out, upper_out, message, upper, split, tiles, middle_tiles, root_table, leaf_rows, sems,
 ):
-    copies = []
-    for m, (whole, rows) in enumerate(
-        ((basis, basis_rows), (leaf_maps, leaf_rows), (middle_maps, middle_rows), (root_maps, root_rows))
-    ):
-        copies.append(
-            [
-                pltpu.make_async_copy(whole.at[:, pl.ds(128 * t, 128)], rows.at[:, t, :], sems.at[m, t])
-                for t in range(32)
-            ]
-        )
-    for group in copies:
-        for copy in group:
-            copy.start()
-    for copy in copies[0]:
-        copy.wait()
+    load = pltpu.make_async_copy(leaf_far, leaf_rows, sems.at[4])
+    load.start()
 
     def leaf_pair(i, _):
         columns = pl.ds(pl.multiple_of(i * 128, 128), 128)
@@ -432,12 +435,10 @@
     sent = []
     for p in range(4):
         lax.fori_loop(32 * p, 32 * p + 32, slots, 0, unroll=2)
-        part = (pl.ds(32 * p, 32), pl.ds(0, 64))
-        sent.append(pltpu.make_async_copy(message.at[part], out.at[part], out_sems.at[p]))
+        part = pl.ds(32 * p, 32)
+        sent.append(pltpu.make_async_copy(message.at[part], out.at[part], sems.at[p]))
         sent[-1].start()
-    for group in copies[1:]:
-        for copy in group:
-            copy.wait()
+    load.wait()
     middles = []
     for j in range(8):
         blocks = [split[:, 512 * j + 128 * p : 512 * j + 128 * p + 128] for p in range(4)]
@@ -449,33 +450,26 @@
     turned = take(root, evens_odds())
     top = pair_halves(dot3(jnp.concatenate([turned[:, :32], turned[:, 64:96]], axis=0), root_rows[0]))
     put_rows(root_skeleton, root_table)
-    root_out[0:8] = as_tile(root)
-    root_out[8:16] = as_tile(top)
-    root_out[16:24] = jnp.concatenate(rows_of(root_table, 0) + [jnp.zeros((5, 128), f32)], axis=0)
+    block = jnp.concatenate(
+        [as_tile(root), as_tile(top)] + rows_of(root_table, 0) + [jnp.zeros((5, 128), f32)], axis=0
+    )
 
     def middle_slots(b, _):
         for c in range(2):
-            message[b, 64 + 8 * c : 72 + 8 * c] = middle_tiles[middle_sends[2 * b + c]]
+            upper[b, 8 * c : 8 * c + 8] = middle_tiles[middle_sends[2 * b + c]]
+        upper[b, 16:40] = block
         return 0
 
     lax.fori_loop(0, 128, middle_slots, 0, unroll=4)
-    part = (pl.ds(0, 128), pl.ds(64, 16))
-    sent.append(pltpu.make_async_copy(message.at[part], out.at[part], out_sems.at[4]))
+    sent.append(pltpu.make_async_copy(upper, upper_out, sems.at[5]))
     sent[-1].start()
     for copy in sent:
         copy.wait()
 
 
-def invert(order, inverse):
-    def body(b, _):
-        for p in range(64):
-            inverse[order[b * 64 + p]] = b * 64 + (p % 2) * 32 + p // 2
-        return 0
-
-    lax.fori_loop(0, 64, body, 0)
-
-
-def near_field(index, before, tree, after, coords, order, out, window, source, s_ref, x_ref, ka, kb):
+def near_field(
+    index, order_list, before, tree, after, coords, order, out, inverse, window, source, s_ref, x_ref, ka, kb
+):
     window[:, :512] = before[...]
     window[0:16, 512:4608] = tree[...]
     window[:, 4608:] = after[...]
@@ -506,7 +500,12 @@
         points = jnp.where(left == (l % 2 == 0), block, swap(block))
         return target_features([points[0:1], points[1:2], points[2:3]])
 
-    couple_all(64, ids, target, s_ref, x_ref, out, ka, kb, unroll=2)
+    def invert(i):
+        for l in (2 * i, 2 * i + 1):
+            for p in range(64):
+                inverse[order_list[l * 64 + p]] = l * 64 + (p % 2) * 32 + p // 2
+
+    couple_all(64, ids, target, s_ref, x_ref, out, ka, kb, unroll=2, beside=invert)
 
 
 def sources(received, s_ref, middle_ref):
@@ -533,7 +532,7 @@
 def far_leaves(index, skeleton, received, table, out, s_ref, tiles, x_ref, rows, ka, kb, sems):
     parts = [
         pltpu.make_async_copy(
-            received.at[pl.ds(32 * p, 32), pl.ds(0, 64), :], tiles.at[pl.ds(32 * p, 32)], sems.at[p]
+            received.at[pl.ds(32 * p, 32)], tiles.at[pl.ds(32 * p, 32)], sems.at[p]
         )
         for p in range(4)
     ]
@@ -570,7 +569,7 @@
 
 
 def finish(
-    middle_index, root_index, received, middle_table_far, roots_far, middle_skeleton, top_skeleton,
+    middle_index, root_index, received, middle_table_far, middle_skeleton, top_skeleton,
     near, far, basis_far, leaf_far, middle_rows, root_rows, inverse,
     out, far_middle, values, middle_table, roots, basis_rows, leaf_rows,
     x_ref, s_ref, ka, kb, middle_points, top_points, tree, sems,
@@ -579,9 +578,9 @@
         pltpu.make_async_copy(source, target, sems.at[i])
         for i, (source, target) in enumerate(
             (
-                (received.at[pl.ds(0, 128), pl.ds(64, 16)], values),
+                (received.at[pl.ds(0, 128), pl.ds(0, 16)], values),
                 (middle_table_far, middle_table),
-                (roots_far, roots),
+                (received.at[pl.ds(0, 128), pl.ds(16, 24)], roots),
                 (leaf_far, leaf_rows),
                 (basis_far, basis_rows),
             )
@@ -702,13 +701,17 @@
     middle_sends,
 ):
     order_rows = order.reshape(32, 128)
-    tree, first_leaves, last_leaves = call(
+    tree, first_leaves, last_leaves, basis_rows, leaf_rows, middle_rows, root_rows = call(
         tree_order,
         "tree_order",
-        (shape(16, 4096), shape(24, 512), shape(24, 512)),
-        [VM, VM, VM],
-        [pltpu.VMEM((8, 4096), f32)],
-    )(values, coords, order_rows)
+        (
+            shape(16, 4096), shape(24, 512), shape(24, 512),
+            shape(64, 32, 128), shape(64, 32, 128), shape(8, 32, 128), shape(1, 32, 128),
+        ),
+        [VM, VM, VM, HBM, HBM, HBM, HBM],
+        [pltpu.VMEM((8, 4096), f32), pltpu.SemaphoreType.DMA((4, 32))],
+        flops=4 * 10**9,
+    )(values, coords, order_rows, leaf_basis, leaf_transfer, middle_transfer, root_transfer)
     before = from_behind(last_leaves, 1)
     after = from_behind(first_leaves, -1)
     packed = call(
@@ -727,39 +730,33 @@
     )(leaf_sends, middle_sends, leaf_skeleton, middle_skeleton)
     skeletons = exchange(packed)
 
-    outgoing, root_out, basis_rows, leaf_rows, middle_rows, root_rows = call(
+    outgoing, upper = call(
         up_pass,
         "up_pass",
-        (
-            shape(128, 80, 128), shape(24, 128),
-            shape(64, 32, 128), shape(64, 32, 128), shape(8, 32, 128), shape(1, 32, 128),
-        ),
-        [SM, SM, VM, VM, HBM, HBM, HBM, HBM],
+        (shape(128, 64, 128), shape(128, 40, 128)),
+        [SM, SM, VM, VM, VM, HBM, VM, VM],
         [
-            pltpu.VMEM((128, 80, 128), f32),
+            pltpu.VMEM((128, 64, 128), f32),
+            pltpu.VMEM((128, 40, 128), f32),
             pltpu.VMEM((16, 4096), f32),
             pltpu.VMEM((64, 8, 128), f32),
             pltpu.VMEM((8, 8, 128), f32),
             pltpu.VMEM((3, 1, 128), f32),
-            pltpu.SemaphoreType.DMA((4, 32)),
-            pltpu.SemaphoreType.DMA((5,)),
+            pltpu.VMEM((64, 32, 128), f32),
+            pltpu.SemaphoreType.DMA((6,)),
         ],
         flops=8 * 10**9,
-        outs=(HBM, VM, VM, VM, VM, VM),
-    )(
-        leaf_sends, middle_sends, tree, root_skeleton,
-        leaf_basis, leaf_transfer, middle_transfer, root_transfer,
-    )
+        outs=(HBM, HBM),
+    )(leaf_sends, middle_sends, tree, root_skeleton, basis_rows, leaf_rows, middle_rows, root_rows)
     outgoing, before, after = lax.optimization_barrier((outgoing, before, after))
     received = exchange(outgoing)
-    roots = lax.all_gather(root_out[None], both, axis=0, tiled=True)
 
     kernels = [pltpu.VMEM((2, 1024, 256), bf16)] * 2
-    near = call(
+    near, inverse = call(
         near_field,
         "near_field",
-        shape(16, 4096),
-        [SM, VM, VM, VM, VM, VM],
+        (shape(16, 4096), shape(4096, kind=jnp.int32)),
+        [SM, SM, VM, VM, VM, VM, VM],
         [
             pltpu.VMEM((24, 5120), f32),
             pltpu.VMEM((8, 4096), f32),
@@ -769,15 +766,11 @@
             pltpu.VMEM((2, 448, 256), bf16),
         ],
         flops=22 * 10**9,
-    )(leaf_near.T, before, tree, after, coords, order_rows)
-    inverse = pl.pallas_call(
-        invert,
-        name="invert",
-        out_shape=shape(4096, kind=jnp.int32),
-        in_specs=[SM],
-        out_specs=SM,
-        cost_estimate=pl.CostEstimate(flops=6 * 10**9, bytes_accessed=0, transcendentals=0),
-    )(order).reshape(32, 128)
+        outs=(VM, SM),
+    )(leaf_near.T, order, before, tree, after, coords, order_rows)
+    inverse = inverse.reshape(32, 128)
+    upper, near = lax.optimization_barrier((upper, near))
+    upper_received = exchange(upper)
     leaf_table, middle_table = call(
         sources,
         "sources",
@@ -804,7 +797,7 @@
         finish,
         "finish",
         shape(16, 4096),
-        [SM, SM, HBM, HBM, HBM, VM, VM, VM, VM, HBM, HBM, VM, VM, VM],
+        [SM, SM, HBM, HBM, VM, VM, VM, VM, HBM, HBM, VM, VM, VM],
         [
             pltpu.VMEM((16, 512), f32),
             pltpu.VMEM((128, 16, 128), f32),
@@ -822,7 +815,7 @@
         ],
         flops=10 * 10**9,
     )(
-        middle_far, root_far, received, middle_table, roots, middle_skeleton, top_skeleton,
+        middle_far, root_far, upper_received, middle_table, middle_skeleton, top_skeleton,
         near, far, basis_rows, leaf_rows, middle_rows, root_rows, inverse,
     )
 

time: 201 us -> 187 us (0.930)
  between operations: 13.5 us -> 0.31 us
  starting transfers between devices: 27.4 us -> 37 us
  waiting for transfers between devices: 8.64 us -> 0.01 us
  Pallas kernels: 150 us -> 147 us
    all_to_all x2 -> x3, starting transfers between devices: 21.8 us -> 31.6 us  [exchange(): return lax.all_to_all(x, both, split_axis=0, concat_axis=0, tiled=True)]
    all_to_all x2 -> x3, waiting for transfers between devices: 8.12 us -> 0.01 us  [exchange(): return lax.all_to_all(x, both, split_axis=0, concat_axis=0, tiled=True)]
    pallas_call x4 -> x3, Pallas kernels: 70 us -> 64.4 us  [the longest x1 31.3 us: shards(): call(near_field, 'near_field', (shape(16, 4096), shape(4096, kind=jnp.int...]
    pallas_call x1, Pallas kernels: 7.11 us -> 9.64 us  [shards(): call(tree_order, 'tree_order', (shape(16, 4096), shape(24, 512), shape(24...]
  transfers between devices with their start and end apart: 5 -> 5, of which waited for: 1 -> 0; matrix products, arithmetic and copies ran while one was open for 0% -> 0% of each run, Pallas kernels for 62% -> 65%
where the time goes in v4:
time: 187 us; the launch traced here: 186 us
  Pallas kernels  147 us (79%)
  starting transfers between devices  37 us (20%)
  local copies, waits for them, and re-layouts  2.1 us (1%)
    pallas_call x1, Pallas kernels, shards(): call(far_leaves, 'far_leaves', shape(16, 4096), [SM, VM, HBM, HBM], [pltp...  47.5 us
    all_to_all x3, starting transfers between devices, exchange(): return lax.all_to_all(x, both, split_axis=0, concat_axis=0, tiled=True)  31.6 us
    pallas_call x1, Pallas kernels, shards(): call(near_field, 'near_field', (shape(16, 4096), shape(4096, kind=jnp.int...  31.3 us
    pallas_call x1, Pallas kernels, shards(): call(finish, 'finish', shape(16, 4096), [SM, SM, HBM, HBM, VM, VM, VM, VM...  22.6 us
    pallas_call x1, Pallas kernels, shards(): call(sources, 'sources', (shape(1024, 64, 128, kind=bf16), shape(256, 64,...  21.7 us
    pallas_call x1, Pallas kernels, shards(): call(up_pass, 'up_pass', (shape(128, 64, 128), shape(128, 40, 128)), [SM,...  10.5 us
    pallas_call x1, Pallas kernels, shards(): call(tree_order, 'tree_order', (shape(16, 4096), shape(24, 512), shape(24...  9.64 us
    ppermute x2, starting transfers between devices, from_behind(): lax.ppermute(block, both, [(i - distance, i) for i in devices if i - dist...  5.46 us
  transfers between devices with their start and end apart: 5, of which 0 were waited for; matrix products, arithmetic and copies ran while one was open for 0% of the time, Pallas kernels for 65%

profile of v4, /device:TPU:1, one launch (start us, length us, event | category | flops | bytes accessed | tf_op | source)
XLA Modules:
  0.0 186.4 jit_solution(15291731774813831783)
XLA Ops:
  0.0 3.7 %pack_skeletons.1 = f32[128,16,128]{2,1,0:T(8,128)} custom-call(s32[1024]{0:T(1024)} %sends.3, s32[256]{0:T(256)} %middle_sends.3, f32[64,192]{1,0:T(8,128)} %skeleton.1, f32[8,192]{1,0:T(8,128)} %middle_skeleton.3), custom_call_target="tpu_custom_call" | custom-call | tf_op jit(solution)/shard_map/pack_skeletons/pallas_call | solution.py:717
  3.7 11.5 %all-to-all-start.1 = ((f32[128,16,128]{2,1,0:T(8,128)}), f32[128,16,128]{2,1,0:T(8,128)S(1)}, u32[]{:S(2)}, u32[]{:S(2)}) async-start(f32[128,16,128]{2,1,0:T(8,128)} %pack_skeletons.1), calls=%async_computation.1 | async-start | bytes 2097152 | tf_op jit(solution)/shard_map/all_to_all | solution.py:681
  15.2 9.6 %tree_order.1 = (f32[16,4096]{1,0:T(8,128)}, f32[24,512]{1,0:T(8,128)}, f32[24,512]{1,0:T(8,128)}, f32[64,32,128]{2,1,0:T(8,128)}, f32[64,32,128]{2,1,0:T(8,128)...) custom-call(f32[16,4096]{1,0:T(8,128)} %values.1, f32[3,4096]{1,0:T(4,128)} %coords.3, s32[32,128]{1,0:T(8,128)} %bitcast.3, ...), custom_call_target="tpu_custom_call" | custom-call | flops 4000000000 | tf_op jit(solution)/shard_map/tree_order/pallas_call | solution.py:704
  24.8 3.5 %collective-permute-start = (f32[24,512]{1,0:T(8,128)}, f32[24,512]{1,0:T(8,128)S(1)}, u32[]{:S(2)}, u32[]{:S(2)}) collective-permute-start(f32[24,512]{1,0:T(8,128)} %get-tuple-element.30), channel_id=1, source_target_pairs={{0,1},{1,2},{2,3},{3,4},{4,5},{5,6},{6,7},{7,8},{8,9},{9,10},{10,1... | collective-permute-start | bytes 147464 | tf_op jit(solution)/shard_map/ppermute | solution.py:677
  28.4 1.9 %collective-permute-start.1 = (f32[24,512]{1,0:T(8,128)}, f32[24,512]{1,0:T(8,128)S(1)}, u32[]{:S(2)}, u32[]{:S(2)}) collective-permute-start(f32[24,512]{1,0:T(8,128)} %get-tuple-element.31), channel_id=1, source_target_pairs={{1,0},{2,1},{3,2},{4,3},{5,4},{6,5},{7,6},{8,7},{9,8},{10,9},{11,1... | collective-permute-start | bytes 147464 | tf_op jit(solution)/shard_map/ppermute | solution.py:677
  30.3 10.5 %up_pass.1 = (f32[128,64,128]{2,1,0:T(8,128)}, f32[128,40,128]{2,1,0:T(8,128)}) custom-call(s32[1024]{0:T(1024)} %sends.3, s32[256]{0:T(256)} %middle_sends.3, f32[16,4096]{1,0:T(8,128)} %get-tuple-element.23.tree, f32[1,192]{1,0:T(1,128)} %root_skeleton.1, f32[64,32,128]{2,1,0:T(8,128)} %get-tuple-element.24.basis_rows.basis_far, ...), custom_call_target="tpu_custom_call" | custom-call | flops 8000000000 | tf_op jit(solution)/shard_map/up_pass/pallas_call | solution.py:733
  40.8 0.0 collective-permute-done.before
  40.8 0.0 copy-start.2
  40.8 0.0 collective-permute-done.1.after
  40.8 0.0 copy-start.3
  40.8 0.0 all-to-all-done.1.received
  40.8 0.0 copy-start.1
  40.9 0.6 copy-done.2
  41.4 0.0 copy-done.3
  41.5 10.3 %all-to-all-start.2 = ((f32[128,64,128]{2,1,0:T(8,128)}), f32[128,64,128]{2,1,0:T(8,128)}, u32[]{:S(2)}, u32[]{:S(2)}) async-start(f32[128,64,128]{2,1,0:T(8,128)} %get-tuple-element.38), calls=%async_computation.2 | async-start | bytes 8388608 | tf_op jit(solution)/shard_map/all_to_all | solution.py:681
  51.8 0.0 copy-done.1
  51.8 31.3 %near_field.1 = (f32[16,4096]{1,0:T(8,128)}, s32[4096]{0:T(1024)}) custom-call(s32[26,64]{1,0:T(8,128)} %bitcast.5, s32[4096]{0:T(1024)} %order_list.1, f32[24,512]{1,0:T(8,128)} %copy-done.2, f32[16,4096]{1,0:T(8,128)} %get-tuple-element.23.tree, f32[24,512]{1,0:T(8,128)} %copy-done.3, f32[3,4096]{1,0:T(4,128)} %coords.3, s32[32,128]{1,0:T(8,128)} %bitcast.4), custom_call_target="tpu_custom_call" | custom-call | flops 22000001024 | tf_op jit(solution)/shard_map/near_field/pallas_call | solution.py:755
  83.1 21.7 %sources.1 = (bf16[1024,64,128]{2,1,0:T(8,128)(2,1)}, bf16[256,64,128]{2,1,0:T(8,128)(2,1)}) custom-call(f32[128,16,128]{2,1,0:T(8,128)} %copy-done.1), custom_call_target="tpu_custom_call" | custom-call | flops 16000000000 | tf_op jit(solution)/shard_map/sources/pallas_call | solution.py:774
  104.9 0.0 all-to-all-done.2.received
  104.9 9.8 %all-to-all-start = ((f32[128,40,128]{2,1,0:T(8,128)}), f32[128,40,128]{2,1,0:T(8,128)S(1)}, u32[]{:S(2)}, u32[]{:S(2)}) async-start(f32[128,40,128]{2,1,0:T(8,128)} %get-tuple-element.35), calls=%async_computation | async-start | bytes 5242880 | tf_op jit(solution)/shard_map/all_to_all | solution.py:681
  114.7 47.5 %far_leaves.1.far = f32[16,4096]{1,0:T(8,128)} custom-call(s32[64,64]{1,0:T(8,128)} %index.1, f32[64,192]{1,0:T(8,128)} %skeleton.1, f32[128,64,128]{2,1,0:T(8,128)} %all-to-all-done.2.received, bf16[1024,64,128]{2,1,0:T(8,128)(2,1)} %get-tuple-element.39.table), custom_call_target="tpu_custom_call" | custom-call | flops 49999998976 | tf_op jit(solution)/shard_map/far_leaves/pallas_call | solution.py:781
  162.2 0.0 all-to-all-done.received
  162.2 1.5 copy-done
  163.7 22.6 %finish.1 = f32[16,4096]{1,0:T(8,128)} custom-call(s32[8,64]{1,0:T(8,128)} %middle_index.1, s32[1,64]{1,0:T(1,128)} %root_index.1, f32[128,40,128]{2,1,0:T(8,128)} %copy-done, bf16[256,64,128]{2,1,0:T(8,128)(2,1)} %get-tuple-element.36.middle_table_far, f32[8,192]{1,0:T(8,128)} %middle_skeleton.3, f32[16,192]{1,0:T(8,128)} %top_skeleton.1, ...), custom_call_target="tpu_custom_call" | custom-call | flops 10000000000 | tf_op jit(solution)/shard_map/finish/pallas_call | solution.py:796
  (1 shorter events, 0.0 us)
Async XLA Ops:
  3.7 37.2 %all-to-all-start.1 = ((f32[128,16,128]{2,1,0:T(8,128)}), f32[128,16,128]{2,1,0:T(8,128)S(1)}, u32[]{:S(2)}, u32[]{:S(2)}) async-start(f32[128,16,128]{2,1,0:T(8,128)} %pack_skeletons.1), calls=%async_computation.1 | async-start | bytes 2097152 | tf_op jit(solution)/shard_map/all_to_all | solution.py:681
  24.8 16.0 %collective-permute-start = (f32[24,512]{1,0:T(8,128)}, f32[24,512]{1,0:T(8,128)S(1)}, u32[]{:S(2)}, u32[]{:S(2)}) collective-permute-start(f32[24,512]{1,0:T(8,128)} %get-tuple-element.30), channel_id=1, source_target_pairs={{0,1},{1,2},{2,3},{3,4},{4,5},{5,6},{6,7},{7,8},{8,9},{9,10},{10,1... | collective-permute-start | bytes 147464 | tf_op jit(solution)/shard_map/ppermute | solution.py:677
  28.4 12.4 %collective-permute-start.1 = (f32[24,512]{1,0:T(8,128)}, f32[24,512]{1,0:T(8,128)S(1)}, u32[]{:S(2)}, u32[]{:S(2)}) collective-permute-start(f32[24,512]{1,0:T(8,128)} %get-tuple-element.31), channel_id=1, source_target_pairs={{1,0},{2,1},{3,2},{4,3},{5,4},{6,5},{7,6},{8,7},{9,8},{10,9},{11,1... | collective-permute-start | bytes 147464 | tf_op jit(solution)/shard_map/ppermute | solution.py:677
  40.8 0.6 copy-start.2
  40.8 0.6 copy-start.3
  40.8 10.9 %copy-start.1 = (f32[128,16,128]{2,1,0:T(8,128)}, f32[128,16,128]{2,1,0:T(8,128)S(1)}, u32[]{:S(2)}) copy-start(f32[128,16,128]{2,1,0:T(8,128)S(1)} %all-to-all-done.1.received) | copy-start | bytes 3145732
  41.5 63.4 %all-to-all-start.2 = ((f32[128,64,128]{2,1,0:T(8,128)}), f32[128,64,128]{2,1,0:T(8,128)}, u32[]{:S(2)}, u32[]{:S(2)}) async-start(f32[128,64,128]{2,1,0:T(8,128)} %get-tuple-element.38), calls=%async_computation.2 | async-start | bytes 8388608 | tf_op jit(solution)/shard_map/all_to_all | solution.py:681
  104.9 57.3 %all-to-all-start = ((f32[128,40,128]{2,1,0:T(8,128)}), f32[128,40,128]{2,1,0:T(8,128)S(1)}, u32[]{:S(2)}, u32[]{:S(2)}) async-start(f32[128,40,128]{2,1,0:T(8,128)} %get-tuple-element.35), calls=%async_computation | async-start | bytes 5242880 | tf_op jit(solution)/shard_map/all_to_all | solution.py:681
  162.2 1.5 copy-start

commit v5 on v4

--- a/solution.py
+++ b/solution.py
@@ -468,7 +468,7 @@
 
 
 def near_field(
-    index, order_list, before, tree, after, coords, order, out, inverse, window, source, s_ref, x_ref, ka, kb
+    index, before, tree, after, coords, order, out, window, source, s_ref, x_ref, ka, kb
 ):
     window[:, :512] = before[...]
     window[0:16, 512:4608] = tree[...]
@@ -500,21 +500,14 @@
         points = jnp.where(left == (l % 2 == 0), block, swap(block))
         return target_features([points[0:1], points[1:2], points[2:3]])
 
-    def invert(i):
-        for l in (2 * i, 2 * i + 1):
-            for p in range(64):
-                inverse[order_list[l * 64 + p]] = l * 64 + (p % 2) * 32 + p // 2
-
-    couple_all(64, ids, target, s_ref, x_ref, out, ka, kb, unroll=2, beside=invert)
-
-
-def sources(received, s_ref, middle_ref):
+    couple_all(64, ids, target, s_ref, x_ref, out, ka, kb, unroll=2)
+
+
+def sources(received, out, middle_out, s_ref, middle_ref, sems):
     def prepare(q, _):
         block = received[q]
         source_eight([[block[r + j : r + j + 1] for j in range(3)] for r in PAIR_ROWS], s_ref, q * 8)
         return 0
-
-    lax.fori_loop(0, 128, prepare, 0, unroll=4)
 
     def middle(q, _):
         source_eight(
@@ -522,14 +515,24 @@
         )
         return 0
 
-    lax.fori_loop(0, 32, middle, 0, unroll=4)
+    sent = []
+    for table, whole, body, count in ((s_ref, out, prepare, 8), (middle_ref, middle_out, middle, 2)):
+        for p in range(count):
+            lax.fori_loop(16 * p, 16 * p + 16, body, 0, unroll=4)
+            part = pl.ds(128 * p, 128)
+            sent.append(pltpu.make_async_copy(table.at[part], whole.at[part], sems.at[len(sent)]))
+            sent[-1].start()
+    for copy in sent:
+        copy.wait()
 
 
 def far_ids(index):
     return lambda l: [index[l, f] for f in range(64)]
 
 
-def far_leaves(index, skeleton, received, table, out, s_ref, tiles, x_ref, rows, ka, kb, sems):
+def far_leaves(
+    index, order_list, skeleton, received, table, out, inverse, s_ref, tiles, x_ref, rows, ka, kb, sems
+):
     parts = [
         pltpu.make_async_copy(
             received.at[pl.ds(32 * p, 32)], tiles.at[pl.ds(32 * p, 32)], sems.at[p]
@@ -551,8 +554,14 @@
 
         lax.fori_loop(32 * p, 32 * p + 32, prepare, 0, unroll=2)
     loaded.wait()
+
+    def invert(i):
+        for l in (2 * i, 2 * i + 1):
+            for p in range(64):
+                inverse[order_list[l * 64 + p]] = l * 64 + (p % 2) * 32 + p // 2
+
     couple_all(
-        64, far_ids(index), lambda l: target_features(rows_of(rows, l)), s_ref, x_ref, out, ka, kb, 2
+        64, far_ids(index), lambda l: target_features(rows_of(rows, l)), s_ref, x_ref, out, ka, kb, 2, invert
     )
 
 
@@ -752,11 +761,11 @@
     received = exchange(outgoing)
 
     kernels = [pltpu.VMEM((2, 1024, 256), bf16)] * 2
-    near, inverse = call(
+    near = call(
         near_field,
         "near_field",
-        (shape(16, 4096), shape(4096, kind=jnp.int32)),
-        [SM, SM, VM, VM, VM, VM, VM],
+        shape(16, 4096),
+        [SM, VM, VM, VM, VM, VM],
         [
             pltpu.VMEM((24, 5120), f32),
             pltpu.VMEM((8, 4096), f32),
@@ -766,23 +775,27 @@
             pltpu.VMEM((2, 448, 256), bf16),
         ],
         flops=22 * 10**9,
-        outs=(VM, SM),
-    )(leaf_near.T, order, before, tree, after, coords, order_rows)
-    inverse = inverse.reshape(32, 128)
-    upper, near = lax.optimization_barrier((upper, near))
+    )(leaf_near.T, before, tree, after, coords, order_rows)
+    upper, near, skeletons = lax.optimization_barrier((upper, near, skeletons))
     upper_received = exchange(upper)
     leaf_table, middle_table = call(
         sources,
         "sources",
         (shape(1024, 64, 128, kind=bf16), shape(256, 64, 128, kind=bf16)),
         [VM],
+        [
+            pltpu.VMEM((1024, 64, 128), bf16),
+            pltpu.VMEM((256, 64, 128), bf16),
+            pltpu.SemaphoreType.DMA((10,)),
+        ],
         flops=16 * 10**9,
+        outs=(HBM, HBM),
     )(skeletons)
-    far = call(
+    far, inverse = call(
         far_leaves,
         "far_leaves",
-        shape(16, 4096),
-        [SM, VM, HBM, HBM],
+        (shape(16, 4096), shape(4096, kind=jnp.int32)),
+        [SM, SM, VM, HBM, HBM],
         [
             pltpu.VMEM((1024, 64, 128), bf16),
             pltpu.VMEM((128, 64, 128), f32),
@@ -792,7 +805,9 @@
             pltpu.SemaphoreType.DMA((5,)),
         ],
         flops=50 * 10**9,
-    )(leaf_far, leaf_skeleton, received, leaf_table)
+        outs=(VM, SM),
+    )(leaf_far, order, leaf_skeleton, received, leaf_table)
+    inverse = inverse.reshape(32, 128)
     return call(
         finish,
         "finish",

time: 187 us -> 185 us (0.989)
  waiting for transfers between devices: 0.01 us -> 8.63 us
  Pallas kernels: 147 us -> 141 us
  starting transfers between devices: 37 us -> 32.9 us
    all_to_all x3, waiting for transfers between devices: 0.01 us -> 8.62 us  [exchange(): return lax.all_to_all(x, both, split_axis=0, concat_axis=0, tiled=True)]
    pallas_call x1, Pallas kernels: 21.7 us -> 16.5 us  [shards(): call(sources, 'sources', (shape(1024, 64, 128, kind=bf16), shape(256, 64,...]
    all_to_all x3, starting transfers between devices: 31.6 us -> 27.4 us  [exchange(): return lax.all_to_all(x, both, split_axis=0, concat_axis=0, tiled=True)]
  transfers between devices with their start and end apart: 5 -> 5, of which waited for: 0 -> 1; matrix products, arithmetic and copies ran while one was open for 0% -> 0% of each run, Pallas kernels for 65% -> 62%
where the time goes in v5:
time: 185 us
  Pallas kernels  141 us (76%)
  starting transfers between devices  32.9 us (18%)
  waiting for transfers between devices  8.63 us (5%)
  local copies, waits for them, and re-layouts  2.1 us (1%)
    pallas_call x1, Pallas kernels, shards(): call(far_leaves, 'far_leaves', (shape(16, 4096), shape(4096, kind=jnp.int...  50.6 us
    all_to_all x3, starting transfers between devices, exchange(): return lax.all_to_all(x, both, split_axis=0, concat_axis=0, tiled=True)  27.4 us
    pallas_call x1, Pallas kernels, shards(): call(near_field, 'near_field', shape(16, 4096), [SM, VM, VM, VM, VM, VM],...  27.4 us
    pallas_call x1, Pallas kernels, shards(): call(finish, 'finish', shape(16, 4096), [SM, SM, HBM, HBM, VM, VM, VM, VM...  22.6 us
    pallas_call x1, Pallas kernels, shards(): call(sources, 'sources', (shape(1024, 64, 128, kind=bf16), shape(256, 64,...  16.5 us
    pallas_call x1, Pallas kernels, shards(): call(up_pass, 'up_pass', (shape(128, 64, 128), shape(128, 40, 128)), [SM,...  10.5 us
    pallas_call x1, Pallas kernels, shards(): call(tree_order, 'tree_order', (shape(16, 4096), shape(24, 512), shape(24...  9.64 us
    all_to_all x3, waiting for transfers between devices, exchange(): return lax.all_to_all(x, both, split_axis=0, concat_axis=0, tiled=True)  8.62 us
  transfers between devices with their start and end apart: 5, of which 1 were waited for; matrix products, arithmetic and copies ran while one was open for 0% of the time, Pallas kernels for 62%

profile of v5, /device:TPU:1, one launch (start us, length us, event | category | flops | bytes accessed | tf_op | source)
XLA Modules:
  0.0 184.8 jit_solution(7371160580648872917)
XLA Ops:
  0.0 3.7 %pack_skeletons.1 = f32[128,16,128]{2,1,0:T(8,128)} custom-call(s32[1024]{0:T(1024)} %sends.3, s32[256]{0:T(256)} %middle_sends.3, f32[64,192]{1,0:T(8,128)} %skeleton.1, f32[8,192]{1,0:T(8,128)} %middle_skeleton.3), custom_call_target="tpu_custom_call" | custom-call | tf_op jit(solution)/shard_map/pack_skeletons/pallas_call | solution.py:726
  3.7 11.5 %all-to-all-start = ((f32[128,16,128]{2,1,0:T(8,128)}), f32[128,16,128]{2,1,0:T(8,128)S(1)}, u32[]{:S(2)}, u32[]{:S(2)}) async-start(f32[128,16,128]{2,1,0:T(8,128)} %pack_skeletons.1), calls=%async_computation | async-start | bytes 2097152 | tf_op jit(solution)/shard_map/all_to_all | solution.py:690
  15.2 9.6 %tree_order.1 = (f32[16,4096]{1,0:T(8,128)}, f32[24,512]{1,0:T(8,128)}, f32[24,512]{1,0:T(8,128)}, f32[64,32,128]{2,1,0:T(8,128)}, f32[64,32,128]{2,1,0:T(8,128)...) custom-call(f32[16,4096]{1,0:T(8,128)} %values.1, f32[3,4096]{1,0:T(4,128)} %coords.3, s32[32,128]{1,0:T(8,128)} %bitcast.4, ...), custom_call_target="tpu_custom_call" | custom-call | flops 4000000000 | tf_op jit(solution)/shard_map/tree_order/pallas_call | solution.py:713
  24.8 3.5 %collective-permute-start = (f32[24,512]{1,0:T(8,128)}, f32[24,512]{1,0:T(8,128)S(1)}, u32[]{:S(2)}, u32[]{:S(2)}) collective-permute-start(f32[24,512]{1,0:T(8,128)} %get-tuple-element.31), channel_id=1, source_target_pairs={{0,1},{1,2},{2,3},{3,4},{4,5},{5,6},{6,7},{7,8},{8,9},{9,10},{10,1... | collective-permute-start | bytes 147464 | tf_op jit(solution)/shard_map/ppermute | solution.py:686
  28.4 1.9 %collective-permute-start.1 = (f32[24,512]{1,0:T(8,128)}, f32[24,512]{1,0:T(8,128)S(1)}, u32[]{:S(2)}, u32[]{:S(2)}) collective-permute-start(f32[24,512]{1,0:T(8,128)} %get-tuple-element.32), channel_id=1, source_target_pairs={{1,0},{2,1},{3,2},{4,3},{5,4},{6,5},{7,6},{8,7},{9,8},{10,9},{11,1... | collective-permute-start | bytes 147464 | tf_op jit(solution)/shard_map/ppermute | solution.py:686
  30.3 10.5 %up_pass.1 = (f32[128,64,128]{2,1,0:T(8,128)}, f32[128,40,128]{2,1,0:T(8,128)}) custom-call(s32[1024]{0:T(1024)} %sends.3, s32[256]{0:T(256)} %middle_sends.3, f32[16,4096]{1,0:T(8,128)} %get-tuple-element.24.tree, f32[1,192]{1,0:T(1,128)} %root_skeleton.1, f32[64,32,128]{2,1,0:T(8,128)} %get-tuple-element.25.basis_rows.basis_far, ...), custom_call_target="tpu_custom_call" | custom-call | flops 8000000000 | tf_op jit(solution)/shard_map/up_pass/pallas_call | solution.py:742
  40.8 0.0 collective-permute-done.before
  40.8 0.0 copy-start.2
  40.8 0.0 collective-permute-done.1.after
  40.8 0.0 copy-start.3
  40.8 0.0 all-to-all-done.received
  40.8 0.0 copy-start.1
  40.9 0.6 copy-done.2
  41.4 0.0 copy-done.3
  41.5 10.3 %all-to-all-start.2 = ((f32[128,64,128]{2,1,0:T(8,128)}), f32[128,64,128]{2,1,0:T(8,128)}, u32[]{:S(2)}, u32[]{:S(2)}) async-start(f32[128,64,128]{2,1,0:T(8,128)} %get-tuple-element.39), calls=%async_computation.2 | async-start | bytes 8388608 | tf_op jit(solution)/shard_map/all_to_all | solution.py:690
  51.8 0.0 copy-done.1
  51.8 27.4 %near_field.1.near = f32[16,4096]{1,0:T(8,128)} custom-call(s32[26,64]{1,0:T(8,128)} %bitcast.3, f32[24,512]{1,0:T(8,128)} %copy-done.2, f32[16,4096]{1,0:T(8,128)} %get-tuple-element.24.tree, f32[24,512]{1,0:T(8,128)} %copy-done.3, f32[3,4096]{1,0:T(4,128)} %coords.3, s32[32,128]{1,0:T(8,128)} %bitcast.5), custom_call_target="tpu_custom_call" | custom-call | flops 22000001024 | tf_op jit(solution)/shard_map/near_field/pallas_call | solution.py:764
  79.2 16.5 %sources.1 = (bf16[1024,64,128]{2,1,0:T(8,128)(2,1)}, bf16[256,64,128]{2,1,0:T(8,128)(2,1)}) custom-call(f32[128,16,128]{2,1,0:T(8,128)} %copy-done.1), custom_call_target="tpu_custom_call" | custom-call | flops 16000000000 | tf_op jit(solution)/shard_map/sources/pallas_call | solution.py:781
  95.7 8.6 %all-to-all-done.2.received = f32[128,64,128]{2,1,0:T(8,128)} async-done(((f32[128,64,128]{2,1,0:T(8,128)}), f32[128,64,128]{2,1,0:T(8,128)}, u32[]{:S(2)}, u32[]{:S(2)}) %all-to-all-start.2) | async-done | bytes 4194336 | tf_op jit(solution)/shard_map/all_to_all | solution.py:690
  104.3 5.6 %all-to-all-start.1 = ((f32[128,40,128]{2,1,0:T(8,128)}), f32[128,40,128]{2,1,0:T(8,128)S(1)}, u32[]{:S(2)}, u32[]{:S(2)}) async-start(f32[128,40,128]{2,1,0:T(8,128)} %get-tuple-element.35), calls=%async_computation.1 | async-start | bytes 5242880 | tf_op jit(solution)/shard_map/all_to_all | solution.py:690
  109.9 50.6 %far_leaves.1 = (f32[16,4096]{1,0:T(8,128)}, s32[4096]{0:T(1024)}) custom-call(s32[64,64]{1,0:T(8,128)} %index.1, s32[4096]{0:T(1024)} %order_list.1, f32[64,192]{1,0:T(8,128)} %skeleton.1, f32[128,64,128]{2,1,0:T(8,128)} %all-to-all-done.2.received, bf16[1024,64,128]{2,1,0:T(8,128)(2,1)} %get-tuple-element.40.table), custom_call_target="tpu_custom_call" | custom-call | flops 49999998976 | tf_op jit(solution)/shard_map/far_leaves/pallas_call | solution.py:794
  160.6 0.0 all-to-all-done.1.received
  160.6 1.5 copy-done
  162.1 22.6 %finish.1 = f32[16,4096]{1,0:T(8,128)} custom-call(s32[8,64]{1,0:T(8,128)} %middle_index.1, s32[1,64]{1,0:T(1,128)} %root_index.1, f32[128,40,128]{2,1,0:T(8,128)} %copy-done, bf16[256,64,128]{2,1,0:T(8,128)(2,1)} %get-tuple-element.37.middle_table_far, f32[8,192]{1,0:T(8,128)} %middle_skeleton.3, f32[16,192]{1,0:T(8,128)} %top_skeleton.1, ...), custom_call_target="tpu_custom_call" | custom-call | flops 10000000000 | tf_op jit(solution)/shard_map/finish/pallas_call | solution.py:811
  (1 shorter events, 0.0 us)
Async XLA Ops:
  3.7 37.2 %all-to-all-start = ((f32[128,16,128]{2,1,0:T(8,128)}), f32[128,16,128]{2,1,0:T(8,128)S(1)}, u32[]{:S(2)}, u32[]{:S(2)}) async-start(f32[128,16,128]{2,1,0:T(8,128)} %pack_skeletons.1), calls=%async_computation | async-start | bytes 2097152 | tf_op jit(solution)/shard_map/all_to_all | solution.py:690
  24.8 16.0 %collective-permute-start = (f32[24,512]{1,0:T(8,128)}, f32[24,512]{1,0:T(8,128)S(1)}, u32[]{:S(2)}, u32[]{:S(2)}) collective-permute-start(f32[24,512]{1,0:T(8,128)} %get-tuple-element.31), channel_id=1, source_target_pairs={{0,1},{1,2},{2,3},{3,4},{4,5},{5,6},{6,7},{7,8},{8,9},{9,10},{10,1... | collective-permute-start | bytes 147464 | tf_op jit(solution)/shard_map/ppermute | solution.py:686
  28.4 12.4 %collective-permute-start.1 = (f32[24,512]{1,0:T(8,128)}, f32[24,512]{1,0:T(8,128)S(1)}, u32[]{:S(2)}, u32[]{:S(2)}) collective-permute-start(f32[24,512]{1,0:T(8,128)} %get-tuple-element.32), channel_id=1, source_target_pairs={{1,0},{2,1},{3,2},{4,3},{5,4},{6,5},{7,6},{8,7},{9,8},{10,9},{11,1... | collective-permute-start | bytes 147464 | tf_op jit(solution)/shard_map/ppermute | solution.py:686
  40.8 0.6 copy-start.2
  40.8 0.6 copy-start.3
  40.8 10.9 %copy-start.1 = (f32[128,16,128]{2,1,0:T(8,128)}, f32[128,16,128]{2,1,0:T(8,128)S(1)}, u32[]{:S(2)}) copy-start(f32[128,16,128]{2,1,0:T(8,128)S(1)} %all-to-all-done.received) | copy-start | bytes 3145732
  41.5 62.9 %all-to-all-start.2 = ((f32[128,64,128]{2,1,0:T(8,128)}), f32[128,64,128]{2,1,0:T(8,128)}, u32[]{:S(2)}, u32[]{:S(2)}) async-start(f32[128,64,128]{2,1,0:T(8,128)} %get-tuple-element.39), calls=%async_computation.2 | async-start | bytes 8388608 | tf_op jit(solution)/shard_map/all_to_all | solution.py:690
  104.3 56.3 %all-to-all-start.1 = ((f32[128,40,128]{2,1,0:T(8,128)}), f32[128,40,128]{2,1,0:T(8,128)S(1)}, u32[]{:S(2)}, u32[]{:S(2)}) async-start(f32[128,40,128]{2,1,0:T(8,128)} %get-tuple-element.35), calls=%async_computation.1 | async-start | bytes 5242880 | tf_op jit(solution)/shard_map/all_to_all | solution.py:690
  160.6 1.5 copy-start

commit v6 on v5

--- a/solution.py
+++ b/solution.py
@@ -384,18 +384,17 @@
     source[3:8] = jnp.zeros((5, 4096), f32)
 
 
+def row_copies(whole, rows, sems):
+    return [
+        pltpu.make_async_copy(whole.at[:, pl.ds(128 * t, 128)], rows.at[:, t, :], sems.at[t])
+        for t in range(32)
+    ]
+
+
 def tree_order(
-    values, coords, order, basis, leaf_maps, middle_maps, root_maps,
-    tree, first_leaves, last_leaves, basis_rows, leaf_rows, middle_rows, root_rows, source, sems,
+    values, coords, order, basis, tree, first_leaves, last_leaves, basis_rows, source, sems
 ):
-    copies = []
-    for m, (whole, rows) in enumerate(
-        ((basis, basis_rows), (leaf_maps, leaf_rows), (middle_maps, middle_rows), (root_maps, root_rows))
-    ):
-        copies += [
-            pltpu.make_async_copy(whole.at[:, pl.ds(128 * t, 128)], rows.at[:, t, :], sems.at[m, t])
-            for t in range(32)
-        ]
+    copies = row_copies(basis, basis_rows, sems)
     for copy in copies:
         copy.start()
     pad_points(coords, source)
@@ -409,11 +408,17 @@
 
 
 def up_pass(
-    sends, middle_sends, tree, root_skeleton, basis_rows, leaf_far, middle_rows, root_rows,
-    out, upper_out, message, upper, split, tiles, middle_tiles, root_table, leaf_rows, sems,
+    sends, middle_sends, tree, root_skeleton, basis_rows, leaf_maps, middle_maps, root_maps,
+    out, upper_out, leaf_rows, middle_rows, root_rows,
+    message, upper, split, tiles, middle_tiles, root_table, sems, row_sems,
 ):
-    load = pltpu.make_async_copy(leaf_far, leaf_rows, sems.at[4])
-    load.start()
+    copies = (
+        row_copies(leaf_maps, leaf_rows, row_sems.at[0])
+        + row_copies(middle_maps, middle_rows, row_sems.at[1])
+        + row_copies(root_maps, root_rows, row_sems.at[2])
+    )
+    for copy in copies:
+        copy.start()
 
     def leaf_pair(i, _):
         columns = pl.ds(pl.multiple_of(i * 128, 128), 128)
@@ -438,7 +443,8 @@
         part = pl.ds(32 * p, 32)
         sent.append(pltpu.make_async_copy(message.at[part], out.at[part], sems.at[p]))
         sent[-1].start()
-    load.wait()
+    for copy in copies:
+        copy.wait()
     middles = []
     for j in range(8):
         blocks = [split[:, 512 * j + 128 * p : 512 * j + 128 * p + 128] for p in range(4)]
@@ -461,7 +467,7 @@
         return 0
 
     lax.fori_loop(0, 128, middle_slots, 0, unroll=4)
-    sent.append(pltpu.make_async_copy(upper, upper_out, sems.at[5]))
+    sent.append(pltpu.make_async_copy(upper, upper_out, sems.at[4]))
     sent[-1].start()
     for copy in sent:
         copy.wait()
@@ -710,17 +716,14 @@
     middle_sends,
 ):
     order_rows = order.reshape(32, 128)
-    tree, first_leaves, last_leaves, basis_rows, leaf_rows, middle_rows, root_rows = call(
+    tree, first_leaves, last_leaves, basis_rows = call(
         tree_order,
         "tree_order",
-        (
-            shape(16, 4096), shape(24, 512), shape(24, 512),
-            shape(64, 32, 128), shape(64, 32, 128), shape(8, 32, 128), shape(1, 32, 128),
-        ),
-        [VM, VM, VM, HBM, HBM, HBM, HBM],
-        [pltpu.VMEM((8, 4096), f32), pltpu.SemaphoreType.DMA((4, 32))],
+        (shape(16, 4096), shape(24, 512), shape(24, 512), shape(64, 32, 128)),
+        [VM, VM, VM, HBM],
+        [pltpu.VMEM((8, 4096), f32), pltpu.SemaphoreType.DMA((32,))],
         flops=4 * 10**9,
-    )(values, coords, order_rows, leaf_basis, leaf_transfer, middle_transfer, root_transfer)
+    )(values, coords, order_rows, leaf_basis)
     before = from_behind(last_leaves, 1)
     after = from_behind(first_leaves, -1)
     packed = call(
@@ -739,11 +742,14 @@
     )(leaf_sends, middle_sends, leaf_skeleton, middle_skeleton)
     skeletons = exchange(packed)
 
-    outgoing, upper = call(
+    outgoing, upper, leaf_rows, middle_rows, root_rows = call(
         up_pass,
         "up_pass",
-        (shape(128, 64, 128), shape(128, 40, 128)),
-        [SM, SM, VM, VM, VM, HBM, VM, VM],
+        (
+            shape(128, 64, 128), shape(128, 40, 128),
+            shape(64, 32, 128), shape(8, 32, 128), shape(1, 32, 128),
+        ),
+        [SM, SM, VM, VM, VM, HBM, HBM, HBM],
         [
             pltpu.VMEM((128, 64, 128), f32),
             pltpu.VMEM((128, 40, 128), f32),
@@ -751,12 +757,15 @@
             pltpu.VMEM((64, 8, 128), f32),
             pltpu.VMEM((8, 8, 128), f32),
             pltpu.VMEM((3, 1, 128), f32),
-            pltpu.VMEM((64, 32, 128), f32),
-            pltpu.SemaphoreType.DMA((6,)),
+            pltpu.SemaphoreType.DMA((5,)),
+            pltpu.SemaphoreType.DMA((3, 32)),
         ],
         flops=8 * 10**9,
-        outs=(HBM, HBM),
-    )(leaf_sends, middle_sends, tree, root_skeleton, basis_rows, leaf_rows, middle_rows, root_rows)
+        outs=(HBM, HBM, VM, VM, VM),
+    )(
+        leaf_sends, middle_sends, tree, root_skeleton, basis_rows,
+        leaf_transfer, middle_transfer, root_transfer,
+    )
     outgoing, before, after = lax.optimization_barrier((outgoing, before, after))
     received = exchange(outgoing)
 
@@ -776,7 +785,7 @@
         ],
         flops=22 * 10**9,
     )(leaf_near.T, before, tree, after, coords, order_rows)
-    upper, near, skeletons = lax.optimization_barrier((upper, near, skeletons))
+    upper, near = lax.optimization_barrier((upper, near))
     upper_received = exchange(upper)
     leaf_table, middle_table = call(
         sources,
@@ -829,6 +838,7 @@
             pltpu.SemaphoreType.DMA((5,)),
         ],
         flops=10 * 10**9,
+        limit=36,
     )(
         middle_far, root_far, upper_received, middle_table, middle_skeleton, top_skeleton,
         near, far, basis_rows, leaf_rows, middle_rows, root_rows, inverse,

time: 185 us -> 190 us (1.027)
  local copies, waits for them, and re-layouts: 2.1 us -> 6.92 us
    unnamed x8 -> x30, local copies, waits for them, and re-layouts: 2.1 us -> 6.92 us
    pallas_call x1, Pallas kernels: 10.5 us -> 12.7 us  [shards(): call(up_pass, 'up_pass', (shape(128, 64, 128), shape(128, 40, 128), shape...]
  transfers between devices with their start and end apart: 5 -> 5, of which waited for: 1 -> 1; matrix products, arithmetic and copies ran while one was open for 0% -> 0% of each run, Pallas kernels for 62% -> 61%
where the time goes in v6:
time: 190 us; the launch traced here: 189 us
  Pallas kernels  141 us (74%)
  starting transfers between devices  32.9 us (17%)
  waiting for transfers between devices  8.59 us (5%)
  local copies, waits for them, and re-layouts  6.92 us (4%)
    pallas_call x1, Pallas kernels, shards(): call(far_leaves, 'far_leaves', (shape(16, 4096), shape(4096, kind=jnp.int...  50.8 us
    all_to_all x3, starting transfers between devices, exchange(): return lax.all_to_all(x, both, split_axis=0, concat_axis=0, tiled=True)  27.4 us
    pallas_call x1, Pallas kernels, shards(): call(near_field, 'near_field', shape(16, 4096), [SM, VM, VM, VM, VM, VM],...  27.4 us
    pallas_call x1, Pallas kernels, shards(): call(finish, 'finish', shape(16, 4096), [SM, SM, HBM, HBM, VM, VM, VM, VM...  21.5 us
    pallas_call x1, Pallas kernels, shards(): call(sources, 'sources', (shape(1024, 64, 128, kind=bf16), shape(256, 64,...  16.6 us
    pallas_call x1, Pallas kernels, shards(): call(up_pass, 'up_pass', (shape(128, 64, 128), shape(128, 40, 128), shape...  12.7 us
    all_to_all x3, waiting for transfers between devices, exchange(): return lax.all_to_all(x, both, split_axis=0, concat_axis=0, tiled=True)  8.59 us
    pallas_call x1, Pallas kernels, shards(): call(tree_order, 'tree_order', (shape(16, 4096), shape(24, 512), shape(24...  8.04 us
  transfers between devices with their start and end apart: 5, of which 1 were waited for; matrix products, arithmetic and copies ran while one was open for 0% of the time, Pallas kernels for 61%

profile of v6, /device:TPU:1, one launch (start us, length us, event | category | flops | bytes accessed | tf_op | source)
XLA Modules:
  0.0 189.4 jit_solution(17991367256308318071)
XLA Ops:
  0.0 3.7 %pack_skeletons.1 = f32[128,16,128]{2,1,0:T(8,128)} custom-call(s32[1024]{0:T(1024)} %sends.3, s32[256]{0:T(256)} %middle_sends.3, f32[64,192]{1,0:T(8,128)} %skeleton.1, f32[8,192]{1,0:T(8,128)} %middle_skeleton.3), custom_call_target="tpu_custom_call" | custom-call | tf_op jit(solution)/shard_map/pack_skeletons/pallas_call | solution.py:729
  3.7 11.5 %all-to-all-start.1 = ((f32[128,16,128]{2,1,0:T(8,128)}), f32[128,16,128]{2,1,0:T(8,128)S(1)}, u32[]{:S(2)}, u32[]{:S(2)}) async-start(f32[128,16,128]{2,1,0:T(8,128)} %pack_skeletons.1), calls=%async_computation.1 | async-start | bytes 2097152 | tf_op jit(solution)/shard_map/all_to_all | solution.py:696
  15.2 8.0 %tree_order.1 = (f32[16,4096]{1,0:T(8,128)}, f32[24,512]{1,0:T(8,128)}, f32[24,512]{1,0:T(8,128)}, f32[64,32,128]{2,1,0:T(8,128)}) custom-call(f32[16,4096]{1,0:T(8,128)} %values.1, f32[3,4096]{1,0:T(4,128)} %coords.3, s32[32,128]{1,0:T(8,128)} %bitcast.5, f32[64,4096]{1,0:T(8,128)} %basis.1), custom_call_target="tpu_custom_call" | custom-call | flops 4000000000 | tf_op jit(solution)/shard_map/tree_order/pallas_call | solution.py:719
  23.2 3.5 %collective-permute-start = (f32[24,512]{1,0:T(8,128)}, f32[24,512]{1,0:T(8,128)S(1)}, u32[]{:S(2)}, u32[]{:S(2)}) collective-permute-start(f32[24,512]{1,0:T(8,128)} %get-tuple-element.27), channel_id=1, source_target_pairs={{0,1},{1,2},{2,3},{3,4},{4,5},{5,6},{6,7},{7,8},{8,9},{9,10},{10,1... | collective-permute-start | bytes 147464 | tf_op jit(solution)/shard_map/ppermute | solution.py:692
  26.8 1.9 %collective-permute-start.1 = (f32[24,512]{1,0:T(8,128)}, f32[24,512]{1,0:T(8,128)S(1)}, u32[]{:S(2)}, u32[]{:S(2)}) collective-permute-start(f32[24,512]{1,0:T(8,128)} %get-tuple-element.28), channel_id=1, source_target_pairs={{1,0},{2,1},{3,2},{4,3},{5,4},{6,5},{7,6},{8,7},{9,8},{10,9},{11,1... | collective-permute-start | bytes 147464 | tf_op jit(solution)/shard_map/ppermute | solution.py:692
  28.7 12.7 %up_pass.1 = (f32[128,64,128]{2,1,0:T(8,128)}, f32[128,40,128]{2,1,0:T(8,128)}, f32[64,32,128]{2,1,0:T(8,128)}, f32[8,32,128]{2,1,0:T(8,128)}, f32[1,32,128]{2,1,0:T(8,128)}) custom-call(s32[1024]{0:T(1024)} %sends.3, s32[256]{0:T(256)} %middle_sends.3, f32[16,4096]{1,0:T(8,128)} %get-tuple-element.23.tree, f32[1,192]{1,0:T(1,128)} %root_skeleton.1, ...), custom_call_target="tpu_custom_call" | custom-call | flops 8000000000 | tf_op jit(solution)/shard_map/up_pass/pallas_call | solution.py:745
  41.5 0.6 copy-done.13
  42.0 0.0 copy-done.14
  42.0 10.3 %all-to-all-start.2 = ((f32[128,64,128]{2,1,0:T(8,128)}), f32[128,64,128]{2,1,0:T(8,128)}, u32[]{:S(2)}, u32[]{:S(2)}) async-start(f32[128,64,128]{2,1,0:T(8,128)} %get-tuple-element.34), calls=%async_computation.2 | async-start | bytes 8388608 | tf_op jit(solution)/shard_map/all_to_all | solution.py:696
  52.4 27.4 %near_field.1.near = f32[16,4096]{1,0:T(8,128)} custom-call(s32[26,64]{1,0:T(8,128)} %bitcast.4, f32[24,512]{1,0:T(8,128)} %copy-done.13, f32[16,4096]{1,0:T(8,128)} %get-tuple-element.23.tree, f32[24,512]{1,0:T(8,128)} %copy-done.14, f32[3,4096]{1,0:T(4,128)} %coords.3, s32[32,128]{1,0:T(8,128)} %bitcast.6), custom_call_target="tpu_custom_call" | custom-call | flops 22000001024 | tf_op jit(solution)/shard_map/near_field/pallas_call | solution.py:773
  79.8 16.6 %sources.1 = (bf16[1024,64,128]{2,1,0:T(8,128)(2,1)}, bf16[256,64,128]{2,1,0:T(8,128)(2,1)}) custom-call(f32[128,16,128]{2,1,0:T(8,128)} %copy-done.12), custom_call_target="tpu_custom_call" | custom-call | flops 16000000000 | tf_op jit(solution)/shard_map/sources/pallas_call | solution.py:790
  96.3 8.6 %all-to-all-done.2.received = f32[128,64,128]{2,1,0:T(8,128)} async-done(((f32[128,64,128]{2,1,0:T(8,128)}), f32[128,64,128]{2,1,0:T(8,128)}, u32[]{:S(2)}, u32[]{:S(2)}) %all-to-all-start.2) | async-done | bytes 4194336 | tf_op jit(solution)/shard_map/all_to_all | solution.py:696
  104.9 5.6 %all-to-all-start = ((f32[128,40,128]{2,1,0:T(8,128)}), f32[128,40,128]{2,1,0:T(8,128)S(1)}, u32[]{:S(2)}, u32[]{:S(2)}) async-start(f32[128,40,128]{2,1,0:T(8,128)} %get-tuple-element.31), calls=%async_computation | async-start | bytes 5242880 | tf_op jit(solution)/shard_map/all_to_all | solution.py:696
  110.5 0.0 copy-start
  110.5 0.0 copy-start.1
  110.5 0.0 copy-start.2
  110.6 0.0 copy-start.3
  110.6 50.8 %far_leaves.1 = (f32[16,4096]{1,0:T(8,128)}, s32[4096]{0:T(1024)}) custom-call(s32[64,64]{1,0:T(8,128)} %index.1, s32[4096]{0:T(1024)} %order_list.1, f32[64,192]{1,0:T(8,128)} %skeleton.1, f32[128,64,128]{2,1,0:T(8,128)} %all-to-all-done.2.received, bf16[1024,64,128]{2,1,0:T(8,128)(2,1)} %get-tuple-element.35.table), custom_call_target="tpu_custom_call" | custom-call | flops 49999998976 | tf_op jit(solution)/shard_map/far_leaves/pallas_call | solution.py:803
  161.5 0.7 copy-done.4
  162.2 1.2 copy-done.5
  163.4 2.2 %copy-done.6 = bf16[256,64,128]{2,1,0:T(8,128)(2,1)S(1)} copy-done((bf16[256,64,128]{2,1,0:T(8,128)(2,1)S(1)}, bf16[256,64,128]{2,1,0:T(8,128)(2,1)}, u32[]{:S(2)}) %copy-start.6) | copy-done | bytes 4194328
  165.6 1.2 copy-done.7
  166.8 0.9 copy-done.9
  167.8 21.5 %finish.1 = f32[16,4096]{1,0:T(8,128)} custom-call(s32[8,64]{1,0:T(8,128)S(1)} %copy-done.2, s32[1,64]{1,0:T(1,128)S(1)} %copy-done.3, f32[128,40,128]{2,1,0:T(8,128)S(1)} %all-to-all-done.received, bf16[256,64,128]{2,1,0:T(8,128)(2,1)S(1)} %copy-done.6, f32[8,192]{1,0:T(8,128)S(1)} %copy-done, f32[16,192]{1,0:T(8,128)S(1)} %copy-done.1, ...), custom_call_target="tpu_custom_call" | custom-call | flops 10000000000 | tf_op jit(solution)/shard_map/finish/pallas_call | solution.py:820
  (23 shorter events, 0.0 us)
Async XLA Ops:
  3.7 37.8 %all-to-all-start.1 = ((f32[128,16,128]{2,1,0:T(8,128)}), f32[128,16,128]{2,1,0:T(8,128)S(1)}, u32[]{:S(2)}, u32[]{:S(2)}) async-start(f32[128,16,128]{2,1,0:T(8,128)} %pack_skeletons.1), calls=%async_computation.1 | async-start | bytes 2097152 | tf_op jit(solution)/shard_map/all_to_all | solution.py:696
  23.2 18.2 %collective-permute-start = (f32[24,512]{1,0:T(8,128)}, f32[24,512]{1,0:T(8,128)S(1)}, u32[]{:S(2)}, u32[]{:S(2)}) collective-permute-start(f32[24,512]{1,0:T(8,128)} %get-tuple-element.27), channel_id=1, source_target_pairs={{0,1},{1,2},{2,3},{3,4},{4,5},{5,6},{6,7},{7,8},{8,9},{9,10},{10,1... | collective-permute-start | bytes 147464 | tf_op jit(solution)/shard_map/ppermute | solution.py:692
  26.8 14.6 %collective-permute-start.1 = (f32[24,512]{1,0:T(8,128)}, f32[24,512]{1,0:T(8,128)S(1)}, u32[]{:S(2)}, u32[]{:S(2)}) collective-permute-start(f32[24,512]{1,0:T(8,128)} %get-tuple-element.28), channel_id=1, source_target_pairs={{1,0},{2,1},{3,2},{4,3},{5,4},{6,5},{7,6},{8,7},{9,8},{10,9},{11,1... | collective-permute-start | bytes 147464 | tf_op jit(solution)/shard_map/ppermute | solution.py:692
  41.4 0.6 copy-start.13
  41.4 0.6 copy-start.14
  41.5 10.9 %copy-start.12 = (f32[128,16,128]{2,1,0:T(8,128)}, f32[128,16,128]{2,1,0:T(8,128)S(1)}, u32[]{:S(2)}) copy-start(f32[128,16,128]{2,1,0:T(8,128)S(1)} %all-to-all-done.1.received) | copy-start | bytes 3145732
  42.0 62.9 %all-to-all-start.2 = ((f32[128,64,128]{2,1,0:T(8,128)}), f32[128,64,128]{2,1,0:T(8,128)}, u32[]{:S(2)}, u32[]{:S(2)}) async-start(f32[128,64,128]{2,1,0:T(8,128)} %get-tuple-element.34), calls=%async_computation.2 | async-start | bytes 8388608 | tf_op jit(solution)/shard_map/all_to_all | solution.py:696
  104.9 56.5 %all-to-all-start = ((f32[128,40,128]{2,1,0:T(8,128)}), f32[128,40,128]{2,1,0:T(8,128)S(1)}, u32[]{:S(2)}, u32[]{:S(2)}) async-start(f32[128,40,128]{2,1,0:T(8,128)} %get-tuple-element.31), calls=%async_computation | async-start | bytes 5242880 | tf_op jit(solution)/shard_map/all_to_all | solution.py:696
  110.5 50.9 %copy-start = (f32[8,192]{1,0:T(8,128)S(1)}, f32[8,192]{1,0:T(8,128)}, u32[]{:S(2)}) copy-start(f32[8,192]{1,0:T(8,128)} %middle_skeleton.3) | copy-start | bytes 18436
  110.5 50.9 %copy-start.1 = (f32[16,192]{1,0:T(8,128)S(1)}, f32[16,192]{1,0:T(8,128)}, u32[]{:S(2)}) copy-start(f32[16,192]{1,0:T(8,128)} %top_skeleton.1) | copy-start | bytes 36868
  110.5 50.9 %copy-start.2 = (s32[8,64]{1,0:T(8,128)S(1)}, s32[8,64]{1,0:T(8,128)}, u32[]{:S(2)}) copy-start(s32[8,64]{1,0:T(8,128)} %middle_index.1) | copy-start | bytes 6148
  110.6 50.9 %copy-start.3 = (s32[1,64]{1,0:T(1,128)S(1)}, s32[1,64]{1,0:T(1,128)}, u32[]{:S(2)}) copy-start(s32[1,64]{1,0:T(1,128)} %root_index.1) | copy-start | bytes 772
  110.6 50.8 %copy-start.8 = (f32[16,4096]{1,0:T(8,128)S(1)}, f32[16,4096]{1,0:T(8,128)}, u32[]{:S(2)}) copy-start(f32[16,4096]{1,0:T(8,128)} %near_field.1.near) | copy-start | bytes 786436
  110.6 50.8 %copy-start.10 = (f32[8,32,128]{2,1,0:T(8,128)S(1)}, f32[8,32,128]{2,1,0:T(8,128)}, u32[]{:S(2)}) copy-start(f32[8,32,128]{2,1,0:T(8,128)} %get-tuple-element.38.middle_rows) | copy-start | bytes 393220
  110.6 50.8 %copy-start.11 = (f32[1,32,128]{2,1,0:T(8,128)S(1)}, f32[1,32,128]{2,1,0:T(8,128)}, u32[]{:S(2)}) copy-start(f32[1,32,128]{2,1,0:T(8,128)} %get-tuple-element.39.root_rows) | copy-start | bytes 49156
  161.4 0.7 copy-start.4
  162.2 1.2 copy-start.5
  163.4 2.2 %copy-start.6 = (bf16[256,64,128]{2,1,0:T(8,128)(2,1)S(1)}, bf16[256,64,128]{2,1,0:T(8,128)(2,1)}, u32[]{:S(2)}) copy-start(bf16[256,64,128]{2,1,0:T(8,128)(2,1)} %get-tuple-element.32.middle_table_far) | copy-start | bytes 12582916
  165.6 1.2 copy-start.7
  166.8 0.9 copy-start.9

commit v7 on v5

--- a/solution.py
+++ b/solution.py
@@ -776,8 +776,7 @@
         ],
         flops=22 * 10**9,
     )(leaf_near.T, before, tree, after, coords, order_rows)
-    upper, near, skeletons = lax.optimization_barrier((upper, near, skeletons))
-    upper_received = exchange(upper)
+    near, skeletons = lax.optimization_barrier((near, skeletons))
     leaf_table, middle_table = call(
         sources,
         "sources",
@@ -791,6 +790,8 @@
         flops=16 * 10**9,
         outs=(HBM, HBM),
     )(skeletons)
+    upper, leaf_table = lax.optimization_barrier((upper, leaf_table))
+    upper_received = exchange(upper)
     far, inverse = call(
         far_leaves,
         "far_leaves",
@@ -804,7 +805,7 @@
             *kernels,
             pltpu.SemaphoreType.DMA((5,)),
         ],
-        flops=50 * 10**9,
+        flops=10**9,
         outs=(VM, SM),
     )(leaf_far, order, leaf_skeleton, received, leaf_table)
     inverse = inverse.reshape(32, 128)

time: 185 us -> 185 us (level)
  no operation moved by 1% of the time
where the time goes in v7:
time: 185 us
  Pallas kernels  141 us (76%)
  starting transfers between devices  32.9 us (18%)
  waiting for transfers between devices  8.62 us (5%)
  local copies, waits for them, and re-layouts  2.1 us (1%)
    pallas_call x1, Pallas kernels, shards(): call(far_leaves, 'far_leaves', (shape(16, 4096), shape(4096, kind=jnp.int...  50.6 us
    all_to_all x3, starting transfers between devices, exchange(): return lax.all_to_all(x, both, split_axis=0, concat_axis=0, tiled=True)  27.4 us
    pallas_call x1, Pallas kernels, shards(): call(near_field, 'near_field', shape(16, 4096), [SM, VM, VM, VM, VM, VM],...  27.4 us
    pallas_call x1, Pallas kernels, shards(): call(finish, 'finish', shape(16, 4096), [SM, SM, HBM, HBM, VM, VM, VM, VM...  22.6 us
    pallas_call x1, Pallas kernels, shards(): call(sources, 'sources', (shape(1024, 64, 128, kind=bf16), shape(256, 64,...  16.5 us
    pallas_call x1, Pallas kernels, shards(): call(up_pass, 'up_pass', (shape(128, 64, 128), shape(128, 40, 128)), [SM,...  10.5 us
    pallas_call x1, Pallas kernels, shards(): call(tree_order, 'tree_order', (shape(16, 4096), shape(24, 512), shape(24...  9.64 us
    all_to_all x3, waiting for transfers between devices, exchange(): return lax.all_to_all(x, both, split_axis=0, concat_axis=0, tiled=True)  8.61 us
  transfers between devices with their start and end apart: 5, of which 1 were waited for; matrix products, arithmetic and copies ran while one was open for 0% of the time, Pallas kernels for 62%

profile of v7, /device:TPU:1, one launch (start us, length us, event | category | flops | bytes accessed | tf_op | source)
XLA Modules:
  0.0 184.8 jit_solution(7371160580648872917)
XLA Ops:
  0.0 3.7 %pack_skeletons.1 = f32[128,16,128]{2,1,0:T(8,128)} custom-call(s32[1024]{0:T(1024)} %sends.3, s32[256]{0:T(256)} %middle_sends.3, f32[64,192]{1,0:T(8,128)} %skeleton.1, f32[8,192]{1,0:T(8,128)} %middle_skeleton.3), custom_call_target="tpu_custom_call" | custom-call | tf_op jit(solution)/shard_map/pack_skeletons/pallas_call | solution.py:726
  3.7 11.5 %all-to-all-start = ((f32[128,16,128]{2,1,0:T(8,128)}), f32[128,16,128]{2,1,0:T(8,128)S(1)}, u32[]{:S(2)}, u32[]{:S(2)}) async-start(f32[128,16,128]{2,1,0:T(8,128)} %pack_skeletons.1), calls=%async_computation | async-start | bytes 2097152 | tf_op jit(solution)/shard_map/all_to_all | solution.py:690
  15.2 9.6 %tree_order.1 = (f32[16,4096]{1,0:T(8,128)}, f32[24,512]{1,0:T(8,128)}, f32[24,512]{1,0:T(8,128)}, f32[64,32,128]{2,1,0:T(8,128)}, f32[64,32,128]{2,1,0:T(8,128)...) custom-call(f32[16,4096]{1,0:T(8,128)} %values.1, f32[3,4096]{1,0:T(4,128)} %coords.3, s32[32,128]{1,0:T(8,128)} %bitcast.3, ...), custom_call_target="tpu_custom_call" | custom-call | flops 4000000000 | tf_op jit(solution)/shard_map/tree_order/pallas_call | solution.py:713
  24.8 3.5 %collective-permute-start = (f32[24,512]{1,0:T(8,128)}, f32[24,512]{1,0:T(8,128)S(1)}, u32[]{:S(2)}, u32[]{:S(2)}) collective-permute-start(f32[24,512]{1,0:T(8,128)} %get-tuple-element.32), channel_id=1, source_target_pairs={{0,1},{1,2},{2,3},{3,4},{4,5},{5,6},{6,7},{7,8},{8,9},{9,10},{10,1... | collective-permute-start | bytes 147464 | tf_op jit(solution)/shard_map/ppermute | solution.py:686
  28.4 1.9 %collective-permute-start.1 = (f32[24,512]{1,0:T(8,128)}, f32[24,512]{1,0:T(8,128)S(1)}, u32[]{:S(2)}, u32[]{:S(2)}) collective-permute-start(f32[24,512]{1,0:T(8,128)} %get-tuple-element.33), channel_id=1, source_target_pairs={{1,0},{2,1},{3,2},{4,3},{5,4},{6,5},{7,6},{8,7},{9,8},{10,9},{11,1... | collective-permute-start | bytes 147464 | tf_op jit(solution)/shard_map/ppermute | solution.py:686
  30.3 10.5 %up_pass.1 = (f32[128,64,128]{2,1,0:T(8,128)}, f32[128,40,128]{2,1,0:T(8,128)}) custom-call(s32[1024]{0:T(1024)} %sends.3, s32[256]{0:T(256)} %middle_sends.3, f32[16,4096]{1,0:T(8,128)} %get-tuple-element.25.tree, f32[1,192]{1,0:T(1,128)} %root_skeleton.1, f32[64,32,128]{2,1,0:T(8,128)} %get-tuple-element.26.basis_rows.basis_far, ...), custom_call_target="tpu_custom_call" | custom-call | flops 8000000000 | tf_op jit(solution)/shard_map/up_pass/pallas_call | solution.py:742
  40.8 0.0 collective-permute-done.before
  40.8 0.0 copy-start.2
  40.8 0.0 collective-permute-done.1.after
  40.8 0.0 copy-start.3
  40.8 0.0 all-to-all-done.received
  40.8 0.0 copy-start.1
  40.9 0.6 copy-done.2
  41.4 0.0 copy-done.3
  41.5 10.3 %all-to-all-start.2 = ((f32[128,64,128]{2,1,0:T(8,128)}), f32[128,64,128]{2,1,0:T(8,128)}, u32[]{:S(2)}, u32[]{:S(2)}) async-start(f32[128,64,128]{2,1,0:T(8,128)} %get-tuple-element.41), calls=%async_computation.2 | async-start | bytes 8388608 | tf_op jit(solution)/shard_map/all_to_all | solution.py:690
  51.8 0.0 copy-done.1
  51.8 27.4 %near_field.1.near = f32[16,4096]{1,0:T(8,128)} custom-call(s32[26,64]{1,0:T(8,128)} %bitcast.5, f32[24,512]{1,0:T(8,128)} %copy-done.2, f32[16,4096]{1,0:T(8,128)} %get-tuple-element.25.tree, f32[24,512]{1,0:T(8,128)} %copy-done.3, f32[3,4096]{1,0:T(4,128)} %coords.3, s32[32,128]{1,0:T(8,128)} %bitcast.4), custom_call_target="tpu_custom_call" | custom-call | flops 22000001024 | tf_op jit(solution)/shard_map/near_field/pallas_call | solution.py:764
  79.2 16.5 %sources.1 = (bf16[1024,64,128]{2,1,0:T(8,128)(2,1)}, bf16[256,64,128]{2,1,0:T(8,128)(2,1)}) custom-call(f32[128,16,128]{2,1,0:T(8,128)} %copy-done.1), custom_call_target="tpu_custom_call" | custom-call | flops 16000000000 | tf_op jit(solution)/shard_map/sources/pallas_call | solution.py:780
  95.7 8.6 %all-to-all-done.2.received = f32[128,64,128]{2,1,0:T(8,128)} async-done(((f32[128,64,128]{2,1,0:T(8,128)}), f32[128,64,128]{2,1,0:T(8,128)}, u32[]{:S(2)}, u32[]{:S(2)}) %all-to-all-start.2) | async-done | bytes 4194336 | tf_op jit(solution)/shard_map/all_to_all | solution.py:690
  104.3 5.6 %all-to-all-start.1 = ((f32[128,40,128]{2,1,0:T(8,128)}), f32[128,40,128]{2,1,0:T(8,128)S(1)}, u32[]{:S(2)}, u32[]{:S(2)}) async-start(f32[128,40,128]{2,1,0:T(8,128)} %get-tuple-element.38), calls=%async_computation.1 | async-start | bytes 5242880 | tf_op jit(solution)/shard_map/all_to_all | solution.py:690
  109.9 50.6 %far_leaves.1 = (f32[16,4096]{1,0:T(8,128)}, s32[4096]{0:T(1024)}) custom-call(s32[64,64]{1,0:T(8,128)} %index.1, s32[4096]{0:T(1024)} %order_list.1, f32[64,192]{1,0:T(8,128)} %skeleton.1, f32[128,64,128]{2,1,0:T(8,128)} %all-to-all-done.2.received, bf16[1024,64,128]{2,1,0:T(8,128)(2,1)} %get-tuple-element.42.table), custom_call_target="tpu_custom_call" | custom-call | flops 1000000000 | tf_op jit(solution)/shard_map/far_leaves/pallas_call | solution.py:795
  160.6 0.0 all-to-all-done.1.received
  160.6 1.5 copy-done
  162.1 22.6 %finish.1 = f32[16,4096]{1,0:T(8,128)} custom-call(s32[8,64]{1,0:T(8,128)} %middle_index.1, s32[1,64]{1,0:T(1,128)} %root_index.1, f32[128,40,128]{2,1,0:T(8,128)} %copy-done, bf16[256,64,128]{2,1,0:T(8,128)(2,1)} %get-tuple-element.39.middle_table_far, f32[8,192]{1,0:T(8,128)} %middle_skeleton.3, f32[16,192]{1,0:T(8,128)} %top_skeleton.1, ...), custom_call_target="tpu_custom_call" | custom-call | flops 10000000000 | tf_op jit(solution)/shard_map/finish/pallas_call | solution.py:812
  (1 shorter events, 0.0 us)
Async XLA Ops:
  3.7 37.2 %all-to-all-start = ((f32[128,16,128]{2,1,0:T(8,128)}), f32[128,16,128]{2,1,0:T(8,128)S(1)}, u32[]{:S(2)}, u32[]{:S(2)}) async-start(f32[128,16,128]{2,1,0:T(8,128)} %pack_skeletons.1), calls=%async_computation | async-start | bytes 2097152 | tf_op jit(solution)/shard_map/all_to_all | solution.py:690
  24.8 16.0 %collective-permute-start = (f32[24,512]{1,0:T(8,128)}, f32[24,512]{1,0:T(8,128)S(1)}, u32[]{:S(2)}, u32[]{:S(2)}) collective-permute-start(f32[24,512]{1,0:T(8,128)} %get-tuple-element.32), channel_id=1, source_target_pairs={{0,1},{1,2},{2,3},{3,4},{4,5},{5,6},{6,7},{7,8},{8,9},{9,10},{10,1... | collective-permute-start | bytes 147464 | tf_op jit(solution)/shard_map/ppermute | solution.py:686
  28.4 12.4 %collective-permute-start.1 = (f32[24,512]{1,0:T(8,128)}, f32[24,512]{1,0:T(8,128)S(1)}, u32[]{:S(2)}, u32[]{:S(2)}) collective-permute-start(f32[24,512]{1,0:T(8,128)} %get-tuple-element.33), channel_id=1, source_target_pairs={{1,0},{2,1},{3,2},{4,3},{5,4},{6,5},{7,6},{8,7},{9,8},{10,9},{11,1... | collective-permute-start | bytes 147464 | tf_op jit(solution)/shard_map/ppermute | solution.py:686
  40.8 0.6 copy-start.2
  40.8 0.6 copy-start.3
  40.8 10.9 %copy-start.1 = (f32[128,16,128]{2,1,0:T(8,128)}, f32[128,16,128]{2,1,0:T(8,128)S(1)}, u32[]{:S(2)}) copy-start(f32[128,16,128]{2,1,0:T(8,128)S(1)} %all-to-all-done.received) | copy-start | bytes 3145732
  41.5 62.9 %all-to-all-start.2 = ((f32[128,64,128]{2,1,0:T(8,128)}), f32[128,64,128]{2,1,0:T(8,128)}, u32[]{:S(2)}, u32[]{:S(2)}) async-start(f32[128,64,128]{2,1,0:T(8,128)} %get-tuple-element.41), calls=%async_computation.2 | async-start | bytes 8388608 | tf_op jit(solution)/shard_map/all_to_all | solution.py:690
  104.3 56.2 %all-to-all-start.1 = ((f32[128,40,128]{2,1,0:T(8,128)}), f32[128,40,128]{2,1,0:T(8,128)S(1)}, u32[]{:S(2)}, u32[]{:S(2)}) async-start(f32[128,40,128]{2,1,0:T(8,128)} %get-tuple-element.38), calls=%async_computation.1 | async-start | bytes 5242880 | tf_op jit(solution)/shard_map/all_to_all | solution.py:690
  160.6 1.5 copy-start
